TPU v7x, 32 devices: a whole 2x2x4 slice. The times are simulated.
32 devices in a mesh: fsdp: 2 (over x), heads: 4 (over z), tensor: 4 (over y, core).
Axes of the slice: x: 2, y: 2, z: 4, core: 2. Of those that a mesh axis runs over, the one named last changes fastest.
Arguments:
- tokens: bfloat16 [8, 256, 768], P(('fsdp', 'tensor')), may hold values from -6 to 6
- valid_mask: int32 [8, 256], P(('fsdp', 'tensor')), may hold values from 0 to 1, as said below
- routes: int32 [8, 256, 2], P('fsdp'), may hold values from 0 to 31, all different within a row; in each aligned block of 1024 rows (0 to 1023, 1024 to 2047, ..., all dimensions but the last counted through in order) at most 128 rows name the same one
- teacher: bfloat16 [8, 256, 768], P(('fsdp', 'tensor')), may hold values from -6 to 6
- gain_one: bfloat16 [768], P(('fsdp', 'tensor')), may hold values from 0.099609375 to 1.8984375
- qkv_weight: bfloat16 [768, 12, 192], P(('fsdp', 'tensor'), 'heads'), may hold values from -0.3125 to 0.3125
- out_weight: bfloat16 [12, 64, 768], P('heads', None, ('fsdp', 'tensor')), may hold values from -1 to 1
- gain_two: bfloat16 [768], P(('fsdp', 'tensor')), may hold values from 0.099609375 to 1.8984375
- router_weight: bfloat16 [768, 32], P(('fsdp', 'tensor')), may hold values from -0.109375 to 0.109375
- expert_up: bfloat16 [32, 768, 3072], P('heads', 'fsdp', 'tensor'), may hold values from -0.21875 to 0.21875
- expert_down: bfloat16 [32, 3072, 768], P('heads', 'tensor', 'fsdp'), may hold values from -3.5 to 3.5
Outputs:
- result: bfloat16 [8, 256, 768], P(('fsdp', 'tensor'))
- loss_terms: float32 [8], P(('fsdp', 'tensor'))
- tokens_grad: float32 [8, 256, 768], P(('fsdp', 'tensor'))
- gain_one_grad: float32 [768], P(('fsdp', 'tensor'))
- qkv_grad: float32 [768, 12, 192], P(('fsdp', 'tensor'), 'heads')
- out_weight_grad: float32 [12, 64, 768], P('heads', None, ('fsdp', 'tensor'))
- gain_two_grad: float32 [768], P(('fsdp', 'tensor'))
- router_grad: float32 [768, 32], P(('fsdp', 'tensor'))
- expert_up_grad: float32 [32, 768, 3072], P('heads', 'fsdp', 'tensor')
- expert_down_grad: float32 [32, 3072, 768], P('heads', 'tensor', 'fsdp')
Inputs may be any that keep to these rules, and one draw needn't show every extreme that they name: `valid_mask`: an image's valid tokens are its first ones, 1 to 197 of them; some image has exactly 197. `routes`: each row names 2 different experts. In the 1024 rows of each index of fsdp no expert is named more than 128 times, a bound that some block reaches.
All inputs are finite; a program needn't handle non-finite values.
Results may differ from a plain program's by a relative error of at most 0.012.
The roundings to bfloat16 on the way count: a program that leaves them out, or rounds other values in their place, can miss the bound.
Values may be sent and summed in bfloat16 or wider, within the bound.
A program may use at most 192 MiB of HBM per device.

v0:
```python
import jax
import jax.numpy as jnp
from jax import lax
from jax.sharding import PartitionSpec as P

EPSILON = 1e-06
MASKED = -1e30
ROOT_HALF = 0.7071067811865476
DENSITY = 0.3989422804014327


def normalize(values):
    center = values - jnp.mean(values, -1, keepdims=True)
    inv_std = lax.rsqrt(jnp.mean(center * center, -1, keepdims=True) + EPSILON)
    return (center * inv_std, inv_std)


def norm_back(gradient, normed, inv_std, gain_vector):
    weighted = gradient * gain_vector
    gain_grad = jnp.sum(gradient * normed, axis=(0, 1))
    inner = (
        weighted
        - jnp.mean(weighted, -1, keepdims=True)
        - normed * jnp.mean(weighted * normed, -1, keepdims=True)
    )
    return (inner * inv_std, gain_grad)


def scores_of(queries, key_rows, keys_ok, score_scale):
    raw_scores = (
        jnp.einsum("iqhe,ikhe->ihqk", queries, key_rows, preferred_element_type=jnp.float32)
        * score_scale
    )
    return jnp.where(keys_ok, raw_scores, MASKED)


def gather_weights(
    gain_one, qkv_weight, out_weight, gain_two, router_weight, expert_up, expert_down
):
    dense_set = (
        lax.all_gather(qkv_weight, ("fsdp", "tensor"), axis=0, tiled=True),
        lax.all_gather(out_weight, ("fsdp", "tensor"), axis=2, tiled=True),
        lax.all_gather(router_weight, ("fsdp", "tensor"), axis=0, tiled=True),
        lax.all_gather(gain_one, ("fsdp", "tensor"), axis=0, tiled=True),
        lax.all_gather(gain_two, ("fsdp", "tensor"), axis=0, tiled=True),
    )
    expert_set = (
        lax.all_gather(expert_up, "fsdp", axis=1, tiled=True),
        lax.all_gather(expert_down, "fsdp", axis=2, tiled=True),
    )
    return (dense_set, expert_set)


def reduce_expert_grads(up_grad, down_grad):
    return (
        lax.psum_scatter(up_grad, "fsdp", scatter_dimension=1, tiled=True),
        lax.psum_scatter(down_grad, "fsdp", scatter_dimension=2, tiled=True),
    )


def local(
    tokens,
    valid_mask,
    routes,
    teacher,
    gain_one,
    qkv_weight,
    out_weight,
    gain_two,
    router_weight,
    expert_up,
    expert_down,
):
    valid_total = lax.psum(jnp.sum(valid_mask.astype(jnp.float32)), ("fsdp", "tensor"))
    dense_set, expert_set = gather_weights(
        gain_one, qkv_weight, out_weight, gain_two, router_weight, expert_up, expert_down
    )
    qkv_full, output_complete, router_full, gain_a, gain_b = dense_set
    up_full, down_full = expert_set
    image_count, token_slots, model_width = tokens.shape
    head_dim = qkv_full.shape[2] // 3
    local_experts = expert_up.shape[0]
    tensor_size = lax.axis_size("tensor")
    group_images = image_count * tensor_size
    group_rows = group_images * token_slots
    top_choices = routes.shape[2]
    expert_count = local_experts * lax.axis_size("heads")
    capacity = 2 * top_choices * group_rows // expert_count
    slot_count = local_experts * capacity
    total_tokens = image_count * token_slots * lax.axis_size("fsdp") * tensor_size
    total_images = image_count * lax.axis_size("fsdp") * tensor_size
    score_scale = head_dim ** (-0.5)
    inputs = tokens.astype(jnp.float32)
    normed_one, spread_one = normalize(inputs)
    first_in = (normed_one * gain_a.astype(jnp.float32)).astype(jnp.bfloat16)
    projected = jnp.einsum(
        "isd,dhe->ishe", first_in, qkv_full, preferred_element_type=jnp.float32
    ).astype(jnp.bfloat16)
    queries = projected[..., :head_dim]
    key_rows = projected[..., head_dim : 2 * head_dim]
    values = projected[..., 2 * head_dim :]
    keys_ok = (valid_mask > 0)[:, None, None, :]
    scores = scores_of(queries, key_rows, keys_ok, score_scale)
    peak_score = jnp.max(scores, -1, keepdims=True)
    exp_scores = jnp.exp(scores - peak_score)
    score_total = jnp.sum(exp_scores, -1, keepdims=True)
    logarithm_total = peak_score + jnp.log(score_total)
    attention = (exp_scores / score_total).astype(jnp.bfloat16)
    combined_heads = jnp.einsum(
        "ihqk,ikhe->iqhe", attention, values, preferred_element_type=jnp.float32
    ).astype(jnp.bfloat16)
    attn_part = jnp.einsum(
        "iqhe,hed->iqd", combined_heads, output_complete, preferred_element_type=jnp.float32
    )
    attended = lax.psum(attn_part, "heads")
    residual = inputs + attended
    normed_two, spread_two = normalize(residual)
    second_in = (normed_two * gain_b.astype(jnp.float32)).astype(jnp.bfloat16)
    group_in = lax.all_gather(second_in, "tensor", axis=0, tiled=True)
    rows_in = group_in.reshape(group_rows, model_width)
    logits = jnp.dot(rows_in, router_full, preferred_element_type=jnp.float32)
    peak_logit = jnp.max(logits, -1, keepdims=True)
    exponent_logits = jnp.exp(logits - peak_logit)
    router_probs = exponent_logits / jnp.sum(exponent_logits, -1, keepdims=True)
    expert_ids = jnp.arange(expert_count, dtype=jnp.int32)
    route_pairs = routes.reshape(group_rows, top_choices)
    picked_hot = (route_pairs[:, :, None] == expert_ids[None, None, :]).astype(jnp.float32)
    gate_weight_values = jnp.sum(router_probs[:, None, :] * picked_hot, -1)
    flat_routes = route_pairs.reshape(group_rows * top_choices)
    route_hot = (flat_routes[:, None] == expert_ids[None, :]).astype(jnp.int32)
    earlier = jnp.cumsum(route_hot, 0) - route_hot
    slot_index = jnp.sum(earlier * route_hot, 1)
    first_expert = lax.axis_index("heads") * local_experts
    is_local = (flat_routes >= first_expert) & (flat_routes < first_expert + local_experts)
    target = jnp.where(is_local, (flat_routes - first_expert) * capacity + slot_index, slot_count)
    owner_row = jnp.arange(group_rows * top_choices, dtype=jnp.int32) // top_choices
    source = jnp.zeros((slot_count,), jnp.int32).at[target].set(owner_row, mode="drop")
    slot_gate = (
        jnp.zeros((slot_count,), jnp.float32)
        .at[target]
        .set(gate_weight_values.reshape(-1), mode="drop")
    )
    slot_pick = jnp.minimum(target, slot_count - 1)
    retain_mask = is_local.astype(jnp.float32)
    dispatched = rows_in[source].reshape(local_experts, capacity, model_width)
    before_gelu = jnp.einsum(
        "ecd,edf->ecf", dispatched, up_full, preferred_element_type=jnp.float32
    )
    hidden = jax.nn.gelu(before_gelu, approximate=False).astype(jnp.bfloat16)
    expert_out = jnp.einsum(
        "ecf,efd->ecd", hidden, down_full, preferred_element_type=jnp.float32
    ).reshape(slot_count, model_width)
    weighted = expert_out * slot_gate[:, None]
    moe_part = jnp.sum(
        (weighted[slot_pick] * retain_mask[:, None]).reshape(group_rows, top_choices, model_width),
        1,
    )
    moe_part = moe_part.reshape(group_images, token_slots, model_width)
    expert_sum = lax.psum(
        lax.psum_scatter(moe_part, "tensor", scatter_dimension=0, tiled=True), "heads"
    )
    final = residual + expert_sum
    valid_rows = valid_mask.astype(jnp.float32)[..., None]
    difference = (final - teacher.astype(jnp.float32)) * valid_rows
    loss_terms = jnp.sum(difference * difference, axis=(1, 2)) * (
        total_images / (valid_total * model_width)
    )
    final_grad = difference * (total_tokens / valid_total)
    dense_set, expert_set = gather_weights(
        gain_one, qkv_weight, out_weight, gain_two, router_weight, expert_up, expert_down
    )
    qkv_full, output_complete, router_full, gain_a, gain_b = dense_set
    up_full, down_full = expert_set
    moe_grad = final_grad.astype(jnp.bfloat16)
    group_grad = lax.all_gather(moe_grad, "tensor", axis=0, tiled=True).reshape(
        group_rows, model_width
    )
    slot_grad = group_grad[source].astype(jnp.float32)
    gate_slot_grad = jnp.sum(slot_grad * expert_out, -1)
    out_grad = (
        (slot_grad * slot_gate[:, None])
        .astype(jnp.bfloat16)
        .reshape(local_experts, capacity, model_width)
    )
    expert_down_grad = jnp.einsum(
        "ecf,ecd->efd", hidden, out_grad, preferred_element_type=jnp.float32
    )
    hidden_grad = jnp.einsum(
        "ecd,efd->ecf", out_grad, down_full, preferred_element_type=jnp.float32
    )
    normal_cdf = 0.5 * (1.0 + lax.erf(before_gelu * ROOT_HALF))
    slope = normal_cdf + before_gelu * DENSITY * jnp.exp(-0.5 * before_gelu * before_gelu)
    pre_grad = (hidden_grad * slope).astype(jnp.bfloat16)
    expert_up_grad = jnp.einsum(
        "ecd,ecf->edf", dispatched, pre_grad, preferred_element_type=jnp.float32
    )
    row_grad = jnp.einsum(
        "ecf,edf->ecd", pre_grad, up_full, preferred_element_type=jnp.float32
    ).reshape(slot_count, model_width)
    rows_part = jnp.sum(
        (row_grad[slot_pick] * retain_mask[:, None]).reshape(group_rows, top_choices, model_width),
        1,
    )
    rows_part = rows_part.reshape(group_images, token_slots, model_width)
    gate_part = (gate_slot_grad[slot_pick] * retain_mask).reshape(
        group_images, token_slots, top_choices
    )
    rows_share, gate_share = (
        lax.psum_scatter(rows_part, "tensor", scatter_dimension=0, tiled=True),
        lax.psum_scatter(gate_part, "tensor", scatter_dimension=0, tiled=True),
    )
    second_grad, gate_grad = lax.psum((rows_share, gate_share), "heads")
    own_start = lax.axis_index("tensor") * image_count * token_slots
    own_rows = image_count * token_slots
    own_probs = lax.dynamic_slice_in_dim(router_probs, own_start, own_rows, 0).reshape(
        image_count, token_slots, expert_count
    )
    own_hot = lax.dynamic_slice_in_dim(picked_hot, own_start, own_rows, 0).reshape(
        image_count, token_slots, top_choices, expert_count
    )
    prob_grad = jnp.sum(gate_grad[..., None] * own_hot, 2)
    logit_grad = (
        own_probs * (prob_grad - jnp.sum(own_probs * prob_grad, -1, keepdims=True))
    ).astype(jnp.bfloat16)
    router_grad = jnp.einsum(
        "isd,ise->de", second_in, logit_grad, preferred_element_type=jnp.float32
    )
    second_grad = second_grad + jnp.einsum(
        "ise,de->isd", logit_grad, router_full, preferred_element_type=jnp.float32
    )
    residual_norm, gain_two_grad = norm_back(
        second_grad, normed_two, spread_two, gain_b.astype(jnp.float32)
    )
    residual_grad = final_grad + residual_norm
    attended_output_gradient = residual_grad.astype(jnp.bfloat16)
    out_weight_grad = jnp.einsum(
        "iqhe,iqd->hed",
        combined_heads,
        attended_output_gradient,
        preferred_element_type=jnp.float32,
    )
    mixed_grad = jnp.einsum(
        "iqd,hed->iqhe",
        attended_output_gradient,
        output_complete,
        preferred_element_type=jnp.float32,
    ).astype(jnp.bfloat16)
    scores = scores_of(queries, key_rows, keys_ok, score_scale)
    probs = jnp.exp(scores - logarithm_total)
    probs_low = probs.astype(jnp.bfloat16)
    prob_part = jnp.einsum(
        "iqhe,ikhe->ihqk", mixed_grad, values, preferred_element_type=jnp.float32
    )
    score_grad = (probs * (prob_part - jnp.sum(probs * prob_part, -1, keepdims=True))).astype(
        jnp.bfloat16
    )
    query_grad = (
        jnp.einsum("ihqk,ikhe->iqhe", score_grad, key_rows, preferred_element_type=jnp.float32)
        * score_scale
    )
    key_grad = (
        jnp.einsum("ihqk,iqhe->ikhe", score_grad, queries, preferred_element_type=jnp.float32)
        * score_scale
    )
    value_grad = jnp.einsum(
        "ihqk,iqhe->ikhe", probs_low, mixed_grad, preferred_element_type=jnp.float32
    )
    projected_grad = jnp.concatenate([query_grad, key_grad, value_grad], -1).astype(jnp.bfloat16)
    qkv_grad = jnp.einsum(
        "isd,ishe->dhe", first_in, projected_grad, preferred_element_type=jnp.float32
    )
    first_part = jnp.einsum(
        "ishe,dhe->isd", projected_grad, qkv_full, preferred_element_type=jnp.float32
    )
    first_grad = lax.psum(first_part, "heads")
    input_norm, gain_one_grad = norm_back(
        first_grad, normed_one, spread_one, gain_a.astype(jnp.float32)
    )
    tokens_grad = residual_grad + input_norm
    dense_grads = (
        lax.psum_scatter(qkv_grad, ("fsdp", "tensor"), scatter_dimension=0, tiled=True),
        lax.psum_scatter(out_weight_grad, ("fsdp", "tensor"), scatter_dimension=2, tiled=True),
        lax.psum_scatter(router_grad, ("fsdp", "tensor"), scatter_dimension=0, tiled=True),
        lax.psum_scatter(gain_one_grad, ("fsdp", "tensor"), scatter_dimension=0, tiled=True),
        lax.psum_scatter(gain_two_grad, ("fsdp", "tensor"), scatter_dimension=0, tiled=True),
    )
    expert_grads = reduce_expert_grads(expert_up_grad, expert_down_grad)
    return (
        final.astype(jnp.bfloat16),
        loss_terms,
        tokens_grad,
        dense_grads[3],
        dense_grads[0],
        dense_grads[1],
        dense_grads[4],
        dense_grads[2],
        expert_grads[0],
        expert_grads[1],
    )


def solution(mesh):
    in_specs = (
        P(("fsdp", "tensor"), None, None),
        P(("fsdp", "tensor"), None),
        P("fsdp", None, None),
        P(("fsdp", "tensor"), None, None),
        P(("fsdp", "tensor")),
        P(("fsdp", "tensor"), "heads", None),
        P("heads", None, ("fsdp", "tensor")),
        P(("fsdp", "tensor")),
        P(("fsdp", "tensor"), None),
        P("heads", "fsdp", "tensor"),
        P("heads", "tensor", "fsdp"),
    )
    out_specs = (
        P(("fsdp", "tensor"), None, None),
        P(("fsdp", "tensor")),
        P(("fsdp", "tensor"), None, None),
        P(("fsdp", "tensor")),
        P(("fsdp", "tensor"), "heads", None),
        P("heads", None, ("fsdp", "tensor")),
        P(("fsdp", "tensor")),
        P(("fsdp", "tensor"), None),
        P("heads", "fsdp", "tensor"),
        P("heads", "tensor", "fsdp"),
    )
    return jax.shard_map(local, mesh=mesh, in_specs=in_specs, out_specs=out_specs, check_vma=False)
```

profile of v0, /device:TPU:0, one launch (start us, length us, event | category | flops | bytes accessed | tf_op | source)
XLA Modules:
  0.0 1239.4 jit_solution(9188463020650189161)
XLA Ops:
  8.4 14.6 %all_gather.35 = bf16[768,3,192]{2,1,0:T(4,128)(2,1)S(1)} all-gather(bf16[96,3,192]{2,1,0:T(4,128)(2,1)S(1)} %copy.139), channel_id=1, replica_groups=mesh['fsdp'=2,'heads'=4,'tensor'=4] {'fsdp','tensor'}, dimensions={0}, use_global_device_ids=true | all-gather | bytes 995328 | tf_op jit(solution)/shard_map/all_gather | solution.py:41
  25.8 13.2 %all-reduce.6 = (bf16[768]{0:T(1024)(128)(2,1)S(1)}, bf16[768]{0:T(1024)(128)(2,1)S(1)}) all-reduce(bf16[768]{0:T(1024)(128)(2,1)S(1)} %dynamic-update-slice, bf16[768]{0:T(1024)(128)(2,1)S(1)} %dynamic-update-slice.1), channel_id=1, replica_groups=mesh['fsdp'=2,'heads'=4,'tensor'=4] {'fsdp','tensor'}, use_global_device_ids=true, to_apply=%add | all-reduce | flops 1536 | bytes 6144
  42.2 9.4 all_gather.36
  53.4 44.1 %all-reduce.12.cloned.1.call-done = f32[1,256,768]{2,1,0:T(8,128)} async-done(((f32[1,256,768]{2,1,0:T(8,128)}), f32[1,256,768]{2,1,0:T(8,128)}) %all-reduce.12.cloned.1.call-update) | async-done | bytes 786448 | tf_op jit(solution)/shard_map/psum | solution.py:115
  104.2 9.1 reduce-window.6
  113.8 9.2 all-gather
  125.1 8.0 scatter_custom_fusion
  133.8 6.4 gather_fusion
  143.0 8.4 scatter_custom_fusion.1
  151.4 88.1 %all-gather.8.cloned.1.call-done = bf16[8,768,768]{2,1,0:T(8,128)(2,1)} async-done(((bf16[8,384,768]{2,1,0:T(8,128)(2,1)}), bf16[8,768,768]{2,1,0:T(8,128)(2,1)}) %all-gather.8.cloned.1.call-update) | async-done | bytes 9437200 | tf_op jit(solution)/shard_map/all_gather | solution.py:48
  239.5 6.1 fusion.41
  247.2 7.1 fusion.4
  254.3 104.6 %all-gather.10.cloned.1.call-done = bf16[8,768,768]{2,1,0:T(8,128)(2,1)} async-done(((bf16[8,768,384]{2,1,0:T(8,128)(2,1)}), bf16[8,768,768]{2,1,0:T(8,128)(2,1)}) %all-gather.10.cloned.1.call-update) | async-done | bytes 9437200 | tf_op jit(solution)/shard_map/all_gather | solution.py:49
  358.9 5.1 fusion.80
  364.0 1.7 copy-done.1
  366.0 10.2 gather_fusion.1
  376.2 8.2 gather.23
  384.4 11.2 multiply_reduce_fusion.1
  395.6 38.1 %reduce-scatter.12.cloned.1.call-done = f32[1,256,768]{2,1,0:T(8,128)} async-done(((f32[4,256,768]{2,1,0:T(8,128)}), f32[1,256,768]{2,1,0:T(8,128)}) %reduce-scatter.12.cloned.1.call-update) | async-done | bytes 786448 | tf_op jit(solution)/shard_map/reduce_scatter | solution.py:160
  434.4 13.3 %psum.44 = f32[]{:T(128)} all-reduce(f32[]{:T(128)} %convert_reduce_fusion.1), channel_id=1, replica_groups=mesh['fsdp'=2,'heads'=4,'tensor'=4] {'fsdp','tensor'}, use_global_device_ids=true, to_apply=%region_20.21 | all-reduce | flops 1 | bytes 8 | tf_op jit(solution)/shard_map/psum | solution.py:74
  448.4 31.4 %all-reduce.14.cloned.1.call-done = f32[1,256,768]{2,1,0:T(8,128)} async-done(((f32[1,256,768]{2,1,0:T(8,128)}), f32[1,256,768]{2,1,0:T(8,128)}) %all-reduce.14.cloned.1.call-update) | async-done | bytes 786448 | tf_op jit(solution)/shard_map/psum | solution.py:159
  479.7 2.4 multiply_convert_fusion.2
  482.5 18.9 %all-gather.12.cloned.1.call-done = bf16[4,256,768]{2,1,0:T(8,128)(2,1)} async-done(((bf16[1,256,768]{2,1,0:T(8,128)(2,1)}), bf16[4,256,768]{2,1,0:T(8,128)(2,1)}) %all-gather.12.cloned.1.call-update) | async-done | bytes 1572880 | tf_op jit(solution)/shard_map/all_gather | solution.py:175
  501.3 6.1 gather_fusion.2
  508.6 6.4 fusion.9
  515.0 7.3 fusion.81
  522.4 10.2 gather_fusion.3
  532.5 8.2 gather.26
  540.7 11.2 multiply_reduce_fusion
  554.5 1.8 fusion.1
  556.3 9.7 gather_fusion.4
  566.8 6.0 all-reduce.2
  572.8 17.4 %reduce-scatter.14.cloned.1.call-done = f32[1,256,768]{2,1,0:T(8,128)} async-done(((f32[4,256,768]{2,1,0:T(8,128)}), f32[1,256,768]{2,1,0:T(8,128)}) %reduce-scatter.14.cloned.1.call-update) | async-done | bytes 786448 | tf_op jit(solution)/shard_map/reduce_scatter | solution.py:209
  590.9 11.7 psum.46
  604.5 31.7 %all-reduce.16.cloned.1.call-done = f32[1,256,768]{2,1,0:T(8,128)} async-done(((f32[1,256,768]{2,1,0:T(8,128)}), f32[1,256,768]{2,1,0:T(8,128)}) %all-reduce.16.cloned.1.call-update) | async-done | bytes 786448 | tf_op jit(solution)/shard_map/psum | solution.py:212
  636.2 2.3 multiply_reduce_fusion.2
  645.7 1.7 reshape.523
  647.6 3.2 fusion.45
  650.9 8.0 fusion.82
  660.7 8.0 fusion.16
  670.1 2.2 reduce-scatter.24.cloned.1.call-done
  674.5 43.9 %all-reduce.18.cloned.1.call-done = f32[1,256,768]{2,1,0:T(8,128)} async-done(((f32[1,256,768]{2,1,0:T(8,128)}), f32[1,256,768]{2,1,0:T(8,128)}) %all-reduce.18.cloned.1.call-update) | async-done | bytes 786448 | tf_op jit(solution)/shard_map/psum | solution.py:275
  720.0 13.8 %all-reduce.5 = (f32[768]{0:T(1024)S(1)}, f32[768]{0:T(1024)S(1)}) all-reduce(f32[768]{0:T(1024)S(1)} %get-tuple-element.14, f32[768]{0:T(1024)S(1)} %copy-done.57), channel_id=5, replica_groups=mesh['fsdp'=2,'heads'=4,'tensor'=4] {'fsdp','tensor'}, use_global_device_ids=true, to_apply=%region_36.37.clone | all-reduce | flops 1536 | bytes 12288
  735.0 2.3 fusion.37
  737.3 18.5 %reduce-scatter.22.cloned.1.call-done = f32[96,192]{1,0:T(8,128)} async-done(((f32[768,192]{1,0:T(8,128)}), f32[96,192]{1,0:T(8,128)}) %reduce-scatter.22.cloned.1.call-update) | async-done | bytes 73744
  757.6 44.6 %reduce-scatter.16.cloned.1.call-done = f32[96,3,192]{2,0,1:T(8,128)} async-done(((f32[768,3,192]{2,0,1:T(8,128)}), f32[96,3,192]{2,0,1:T(8,128)}) %reduce-scatter.16.cloned.1.call-update) | async-done | bytes 221200 | tf_op jit(solution)/shard_map/reduce_scatter | solution.py:281
  802.2 214.5 %reduce-scatter.18.cloned.1.call-done = f32[8,384,768]{2,1,0:T(8,128)} async-done(((f32[8,768,768]{2,1,0:T(8,128)}), f32[8,384,768]{2,1,0:T(8,128)}) %reduce-scatter.18.cloned.1.call-update) | async-done | bytes 9437200 | tf_op jit(solution)/shard_map/reduce_scatter | solution.py:56
  1016.7 214.5 %reduce-scatter.20.cloned.1.call-done = f32[8,768,384]{2,1,0:T(8,128)} async-done(((f32[8,768,768]{2,1,0:T(8,128)}), f32[8,768,384]{2,1,0:T(8,128)}) %reduce-scatter.20.cloned.1.call-update) | async-done | bytes 9437200 | tf_op jit(solution)/shard_map/reduce_scatter | solution.py:57
  (252 shorter events, 45.5 us)
Async XLA Ops:
  7.2 16.8 %copy-start.60 = (u32[32]{0:T(128)S(1)}, u32[32]{0:T(128)}, u32[]{:S(2)}) copy-start(u32[32]{0:T(128)} %constant.143) | copy-start | bytes 388
  7.2 18.1 %copy-start.63 = (bf16[96]{0:T(256)(128)(2,1)S(1)}, bf16[96]{0:T(256)(128)(2,1)}, u32[]{:S(2)}) copy-start(bf16[96]{0:T(256)(128)(2,1)} %param.15) | copy-start | bytes 580
  7.2 18.4 %copy-start.64 = (bf16[96]{0:T(256)(128)(2,1)S(1)}, bf16[96]{0:T(256)(128)(2,1)}, u32[]{:S(2)}) copy-start(bf16[96]{0:T(256)(128)(2,1)} %param.18) | copy-start | bytes 580
  7.2 31.8 %copy-start.12 = (bf16[1,256,768]{2,1,0:T(8,128)(2,1)S(1)}, bf16[1,256,768]{2,1,0:T(8,128)(2,1)}, u32[]{:S(2)}) copy-start(bf16[1,256,768]{2,1,0:T(8,128)(2,1)} %param.11) | copy-start | bytes 1179652
  7.2 90.3 %all-reduce.12.cloned.1.call-start = ((), (), s32[]{:S(2)}) async-start(), calls=%async_computation.7 | async-start | bytes 1572864 | tf_op jit(solution)/shard_map/psum | solution.py:115
  23.0 17.5 %copy-start.61 = (s32[1,256]{1,0:T(1,128)S(1)}, s32[1,256]{1,0:T(1,128)}, u32[]{:S(2)}) copy-start(s32[1,256]{1,0:T(1,128)} %param.12) | copy-start | bytes 3076
  23.9 18.2 %copy-start.27 = (bf16[768,3,192]{0,2,1:T(8,128)(2,1)}, bf16[768,3,192]{0,2,1:T(8,128)(2,1)S(1)}, u32[]{:S(2)}) copy-start(bf16[768,3,192]{0,2,1:T(8,128)(2,1)S(1)} %copy.140) | copy-start | bytes 2654212
  41.8 11.5 copy-start.56
  42.1 57.0 %copy-start.33 = (bf16[256,3,64]{0,2,1:T(8,128)(2,1)}, bf16[256,3,64]{0,2,1:T(8,128)(2,1)S(1)}, u32[]{:S(2)}) copy-start(bf16[256,3,64]{0,2,1:T(8,128)(2,1)S(1)} %fusion.25) | copy-start | bytes 294916
  52.1 48.6 %copy-start.24 = (bf16[3,64,768]{2,1,0:T(8,128)(2,1)}, bf16[3,64,768]{2,1,0:T(8,128)(2,1)S(1)}, u32[]{:S(2)}) copy-start(bf16[3,64,768]{2,1,0:T(8,128)(2,1)S(1)} %copy.143) | copy-start | bytes 884740
  53.3 80.5 %all-gather.6.cloned.1.call-start = ((), (), s32[]{:S(2)}) async-start(), calls=%async_computation.8 | async-start | bytes 1966080 | tf_op jit(solution)/shard_map/all_gather | solution.py:119
  53.4 48.1 %copy-start.41 = (f32[768]{0:T(1024)}, f32[768]{0:T(1024)S(1)}, u32[]{:S(2)}) copy-start(f32[768]{0:T(1024)S(1)} %convert_element_type.117) | copy-start | bytes 9220
  100.7 138.8 %all-gather.8.cloned.1.call-start = ((), (), s32[]{:S(2)}) async-start(), calls=%async_computation.9 | async-start | bytes 14155776 | tf_op jit(solution)/shard_map/all_gather | solution.py:48
  101.5 257.5 %all-gather.10.cloned.1.call-start = ((), (), s32[]{:S(2)}) async-start(), calls=%async_computation.10 | async-start | bytes 14155776 | tf_op jit(solution)/shard_map/all_gather | solution.py:49
  102.0 11.8 copy-start.58
  102.0 331.7 %reduce-scatter.12.cloned.1.call-start = ((), (), s32[]{:S(2)}) async-start(), calls=%async_computation.11 | async-start | bytes 3932160 | tf_op jit(solution)/shard_map/reduce_scatter | solution.py:160
  125.1 8.7 copy-start.59
  140.3 105.3 %copy-start.17 = (bf16[1024,768]{1,0:T(8,128)(2,1)}, bf16[1024,768]{1,0:T(8,128)(2,1)S(1)}, u32[]{:S(2)}) copy-start(bf16[1024,768]{1,0:T(8,128)(2,1)S(1)} %gather_fusion) | copy-start | bytes 4718596
  151.4 356.1 %copy-start.44 = (f32[1024]{0:T(1024)}, f32[1024]{0:T(1024)S(1)}, u32[]{:S(2)}) copy-start(f32[1024]{0:T(1024)S(1)} %scatter_custom_fusion.1) | copy-start | bytes 12292
  254.3 104.6 %copy-start.8 = (bf16[8,128,768]{2,1,0:T(8,128)(2,1)}, bf16[8,128,768]{2,1,0:T(8,128)(2,1)S(1)}, u32[]{:S(2)}) copy-start(bf16[8,128,768]{2,1,0:T(8,128)(2,1)S(1)} %fusion.4) | copy-start | bytes 4718596
  376.2 8.2 copy-start.19
  395.6 38.2 %copy-start.62 = (s32[1,256]{1,0:T(1,128)S(1)}, s32[1,256]{1,0:T(1,128)}, u32[]{:S(2)}) copy-start(s32[1,256]{1,0:T(1,128)} %param.12) | copy-start | bytes 3076
  395.6 84.2 %copy-start.4 = (f32[1,256,768]{2,1,0:T(8,128)S(1)}, f32[1,256,768]{2,1,0:T(8,128)}, u32[]{:S(2)}) copy-start(f32[1,256,768]{2,1,0:T(8,128)} %copy-done.3) | copy-start | bytes 2359300
  395.6 84.2 %copy-start.35 = (bf16[1,256,768]{2,1,0:T(8,128)(2,1)S(1)}, bf16[1,256,768]{2,1,0:T(8,128)(2,1)}, u32[]{:S(2)}) copy-start(bf16[1,256,768]{2,1,0:T(8,128)(2,1)} %param.14) | copy-start | bytes 1179652
  395.6 105.8 %copy-start.47 = (s32[1024]{0:T(1024)S(1)}, s32[1024]{0:T(1024)}, u32[]{:S(2)}) copy-start(s32[1024]{0:T(1024)} %copy-done.46) | copy-start | bytes 12292
  395.6 84.1 %all-reduce.14.cloned.1.call-start = ((), (), s32[]{:S(2)}) async-start(), calls=%async_computation.12 | async-start | bytes 1572864 | tf_op jit(solution)/shard_map/psum | solution.py:159
  433.7 67.6 %all-gather.12.cloned.1.call-start = ((), (), s32[]{:S(2)}) async-start(), calls=%async_computation.13 | async-start | bytes 1966080 | tf_op jit(solution)/shard_map/all_gather | solution.py:175
  482.2 108.0 %reduce-scatter.14.cloned.1.call-start = ((), (), s32[]{:S(2)}) async-start(), calls=%async_computation.14 | async-start | bytes 3932160 | tf_op jit(solution)/shard_map/reduce_scatter | solution.py:209
  515.0 7.3 copy-start.15
  532.5 8.2 copy-start.20
  551.9 84.3 %all-reduce.16.cloned.1.call-start = ((), (), s32[]{:S(2)}) async-start(), calls=%async_computation.15 | async-start | bytes 1572864 | tf_op jit(solution)/shard_map/psum | solution.py:212
  556.3 47.0 %copy-start.30 = (f32[1024,32]{0,1:T(8,128)S(1)}, f32[1024,32]{0,1:T(8,128)}, u32[]{:S(2)}) copy-start(f32[1024,32]{0,1:T(8,128)} %copy-done.29) | copy-start | bytes 393220
  556.3 47.1 %copy-start.21 = (bf16[1,256,768]{2,1,0:T(8,128)(2,1)S(1)}, bf16[1,256,768]{2,1,0:T(8,128)(2,1)}, u32[]{:S(2)}) copy-start(bf16[1,256,768]{2,1,0:T(8,128)(2,1)} %multiply_convert_fusion.1) | copy-start | bytes 1179652
  566.0 70.2 %copy-start.5 = (f32[1,256,768]{2,1,0:T(8,128)S(1)}, f32[1,256,768]{2,1,0:T(8,128)}, u32[]{:S(2)}) copy-start(f32[1,256,768]{2,1,0:T(8,128)} %copy-done.3) | copy-start | bytes 2359300
  566.0 70.2 %copy-start.31 = (bf16[768,32]{0,1:T(8,128)(2,1)S(1)}, bf16[768,32]{0,1:T(8,128)(2,1)}, u32[]{:S(2)}) copy-start(bf16[768,32]{0,1:T(8,128)(2,1)} %reshape.512) | copy-start | bytes 147460
  566.1 70.2 %copy-start.42 = (f32[768]{0:T(1024)S(1)}, f32[768]{0:T(1024)}, u32[]{:S(2)}) copy-start(f32[768]{0:T(1024)} %copy-done.41) | copy-start | bytes 9220
  566.1 70.2 %copy-start.51 = (f32[256]{0:T(256)S(1)}, f32[256]{0:T(256)}, u32[]{:S(2)}) copy-start(f32[256]{0:T(256)} %copy-done.50) | copy-start | bytes 3076
  566.1 70.2 %copy-start.55 = (f32[256]{0:T(256)S(1)}, f32[256]{0:T(256)}, u32[]{:S(2)}) copy-start(f32[256]{0:T(256)} %copy-done.54) | copy-start | bytes 3076
  566.1 72.4 %copy-start.23 = (f32[1,256,768]{2,1,0:T(8,128)S(1)}, f32[1,256,768]{2,1,0:T(8,128)}, u32[]{:S(2)}) copy-start(f32[1,256,768]{2,1,0:T(8,128)} %get-tuple-element.23) | copy-start | bytes 2359300
  590.2 82.2 %reduce-scatter.24.cloned.1.call-start = ((), (), s32[]{:S(2)}) async-start(), calls=%async_computation.21 | async-start | bytes 442368
  604.5 37.1 %copy-start.7 = (f32[3,256,256]{1,2,0:T(8,128)S(1)}, f32[3,256,256]{1,2,0:T(8,128)}, u32[]{:S(2)}) copy-start(f32[3,256,256]{1,2,0:T(8,128)} %copy-done.6) | copy-start | bytes 2359300
  604.5 113.9 %all-reduce.18.cloned.1.call-start = ((), (), s32[]{:S(2)}) async-start(), calls=%async_computation.16 | async-start | bytes 1572864 | tf_op jit(solution)/shard_map/psum | solution.py:275
  644.4 111.4 %reduce-scatter.22.cloned.1.call-start = ((), (), s32[]{:S(2)}) async-start(), calls=%async_computation.20 | async-start | bytes 884736
  647.5 154.7 %reduce-scatter.16.cloned.1.call-start = ((), (), s32[]{:S(2)}) async-start(), calls=%async_computation.17 | async-start | bytes 2654208 | tf_op jit(solution)/shard_map/reduce_scatter | solution.py:281
  650.8 365.9 %reduce-scatter.18.cloned.1.call-start = ((), (), s32[]{:S(2)}) async-start(), calls=%async_computation.18 | async-start | bytes 28311552 | tf_op jit(solution)/shard_map/reduce_scatter | solution.py:56
  658.9 572.4 %reduce-scatter.20.cloned.1.call-start = ((), (), s32[]{:S(2)}) async-start(), calls=%async_computation.19 | async-start | bytes 28311552 | tf_op jit(solution)/shard_map/reduce_scatter | solution.py:57
  668.7 51.3 %copy-start.57 = (f32[768]{0:T(1024)S(1)}, f32[768]{0:T(1024)}, u32[]{:S(2)}) copy-start(f32[768]{0:T(1024)} %get-tuple-element.12) | copy-start | bytes 9220
  668.7 66.3 %copy-start.14 = (f32[1,256,768]{2,1,0:T(8,128)S(1)}, f32[1,256,768]{2,1,0:T(8,128)}, u32[]{:S(2)}) copy-start(f32[1,256,768]{2,1,0:T(8,128)} %copy-done.13) | copy-start | bytes 2359300
  (33 other events, 75.2 us)
Sparse Core Ops, SparseCore 0:
  53.4 44.0 all-reduce.11
  100.8 18.9 all-gather.5
  121.4 118.0 all-gather.7
  240.9 117.9 all-gather.9
  395.7 37.9 reduce-scatter.11
  436.1 43.6 all-reduce.13
  482.3 18.9 all-gather.11
  552.1 38.0 reduce-scatter.13
  592.5 43.6 all-reduce.15
  639.1 33.2 reduce-scatter.23
  674.8 43.6 all-reduce.17
  721.4 34.2 reduce-scatter.21
  759.7 42.4 reduce-scatter.15
  805.0 211.6 reduce-scatter.17
  1019.6 211.6 reduce-scatter.19
where the time goes:
time: 1250 us; the launch traced here: 1240 us
  waiting for transfers between devices  914 us (73%)
  local copies, waits for them, and re-layouts  102 us (8%)
  blocking collectives  91.2 us (7%)
  other arithmetic  55.8 us (4%)
  matrix products  55.2 us (4%)
  between operations  20 us (2%)
    reduce_scatter x1, waiting for transfers between devices, reduce_expert_grads(): lax.psum_scatter(up_grad, 'fsdp', scatter_dimension=1, tiled=True)  215 us
    reduce_scatter x1, waiting for transfers between devices, reduce_expert_grads(): lax.psum_scatter(down_grad, 'fsdp', scatter_dimension=2, tiled=True)  215 us
    all_gather x1, waiting for transfers between devices, gather_weights(): lax.all_gather(expert_down, 'fsdp', axis=2, tiled=True)  105 us
    all_gather x1, waiting for transfers between devices, gather_weights(): lax.all_gather(expert_up, 'fsdp', axis=1, tiled=True)  88.1 us
    reduce_scatter x1, waiting for transfers between devices, local(): lax.psum_scatter(qkv_grad, ('fsdp', 'tensor'), scatter_dimension=0, tiled...  44.6 us
    psum x1, waiting for transfers between devices, local(): attended = lax.psum(attn_part, 'heads')  44.1 us
    psum x1, waiting for transfers between devices, local(): first_grad = lax.psum(first_part, 'heads')  43.9 us
    reduce_scatter x1, waiting for transfers between devices, local(): lax.psum_scatter(moe_part, 'tensor', scatter_dimension=0, tiled=True)  38.1 us
  transfers between devices with their start and end apart: 15, of which 14 were waited for; matrix products, arithmetic and copies ran while one was open for 9% of the time, Pallas kernels for 0%

commit v1 on v0

--- a/solution.py
+++ b/solution.py
@@ -1,8 +1,13 @@
+import functools
+
 import jax
 import jax.numpy as jnp
 from jax import lax
+from jax.experimental import pallas as pl
+from jax.experimental.pallas import tpu as pltpu
 from jax.sharding import PartitionSpec as P
 
+FSDP, HEADS, TENSOR = "fsdp", "heads", "tensor"
 EPSILON = 1e-06
 MASKED = -1e30
 ROOT_HALF = 0.7071067811865476
@@ -38,27 +43,27 @@
     gain_one, qkv_weight, out_weight, gain_two, router_weight, expert_up, expert_down
 ):
     dense_set = (
-        lax.all_gather(qkv_weight, ("fsdp", "tensor"), axis=0, tiled=True),
-        lax.all_gather(out_weight, ("fsdp", "tensor"), axis=2, tiled=True),
-        lax.all_gather(router_weight, ("fsdp", "tensor"), axis=0, tiled=True),
-        lax.all_gather(gain_one, ("fsdp", "tensor"), axis=0, tiled=True),
-        lax.all_gather(gain_two, ("fsdp", "tensor"), axis=0, tiled=True),
+        lax.all_gather(qkv_weight, (FSDP, TENSOR), axis=0, tiled=True),
+        lax.all_gather(out_weight, (FSDP, TENSOR), axis=2, tiled=True),
+        lax.all_gather(router_weight, (FSDP, TENSOR), axis=0, tiled=True),
+        lax.all_gather(gain_one, (FSDP, TENSOR), axis=0, tiled=True),
+        lax.all_gather(gain_two, (FSDP, TENSOR), axis=0, tiled=True),
     )
     expert_set = (
-        lax.all_gather(expert_up, "fsdp", axis=1, tiled=True),
-        lax.all_gather(expert_down, "fsdp", axis=2, tiled=True),
+        lax.all_gather(expert_up, FSDP, axis=1, tiled=True),
+        lax.all_gather(expert_down, FSDP, axis=2, tiled=True),
     )
     return (dense_set, expert_set)
 
 
 def reduce_expert_grads(up_grad, down_grad):
     return (
-        lax.psum_scatter(up_grad, "fsdp", scatter_dimension=1, tiled=True),
-        lax.psum_scatter(down_grad, "fsdp", scatter_dimension=2, tiled=True),
-    )
-
-
-def local(
+        lax.psum_scatter(up_grad, FSDP, scatter_dimension=1, tiled=True),
+        lax.psum_scatter(down_grad, FSDP, scatter_dimension=2, tiled=True),
+    )
+
+
+def general(
     tokens,
     valid_mask,
     routes,
@@ -71,7 +76,7 @@
     expert_up,
     expert_down,
 ):
-    valid_total = lax.psum(jnp.sum(valid_mask.astype(jnp.float32)), ("fsdp", "tensor"))
+    valid_total = lax.psum(jnp.sum(valid_mask.astype(jnp.float32)), (FSDP, TENSOR))
     dense_set, expert_set = gather_weights(
         gain_one, qkv_weight, out_weight, gain_two, router_weight, expert_up, expert_down
     )
@@ -80,15 +85,15 @@
     image_count, token_slots, model_width = tokens.shape
     head_dim = qkv_full.shape[2] // 3
     local_experts = expert_up.shape[0]
-    tensor_size = lax.axis_size("tensor")
+    tensor_size = lax.axis_size(TENSOR)
     group_images = image_count * tensor_size
     group_rows = group_images * token_slots
     top_choices = routes.shape[2]
-    expert_count = local_experts * lax.axis_size("heads")
+    expert_count = local_experts * lax.axis_size(HEADS)
     capacity = 2 * top_choices * group_rows // expert_count
     slot_count = local_experts * capacity
-    total_tokens = image_count * token_slots * lax.axis_size("fsdp") * tensor_size
-    total_images = image_count * lax.axis_size("fsdp") * tensor_size
+    total_tokens = image_count * token_slots * lax.axis_size(FSDP) * tensor_size
+    total_images = image_count * lax.axis_size(FSDP) * tensor_size
     score_scale = head_dim ** (-0.5)
     inputs = tokens.astype(jnp.float32)
     normed_one, spread_one = normalize(inputs)
@@ -112,11 +117,11 @@
     attn_part = jnp.einsum(
         "iqhe,hed->iqd", combined_heads, output_complete, preferred_element_type=jnp.float32
     )
-    attended = lax.psum(attn_part, "heads")
+    attended = lax.psum(attn_part, HEADS)
     residual = inputs + attended
     normed_two, spread_two = normalize(residual)
     second_in = (normed_two * gain_b.astype(jnp.float32)).astype(jnp.bfloat16)
-    group_in = lax.all_gather(second_in, "tensor", axis=0, tiled=True)
+    group_in = lax.all_gather(second_in, TENSOR, axis=0, tiled=True)
     rows_in = group_in.reshape(group_rows, model_width)
     logits = jnp.dot(rows_in, router_full, preferred_element_type=jnp.float32)
     peak_logit = jnp.max(logits, -1, keepdims=True)
@@ -128,9 +133,13 @@
     gate_weight_values = jnp.sum(router_probs[:, None, :] * picked_hot, -1)
     flat_routes = route_pairs.reshape(group_rows * top_choices)
     route_hot = (flat_routes[:, None] == expert_ids[None, :]).astype(jnp.int32)
-    earlier = jnp.cumsum(route_hot, 0) - route_hot
+    order = jnp.arange(group_rows * top_choices, dtype=jnp.int32)
+    before = (order[None, :] < order[:, None]).astype(jnp.bfloat16)
+    earlier = jnp.dot(
+        before, route_hot.astype(jnp.bfloat16), preferred_element_type=jnp.float32
+    ).astype(jnp.int32)
     slot_index = jnp.sum(earlier * route_hot, 1)
-    first_expert = lax.axis_index("heads") * local_experts
+    first_expert = lax.axis_index(HEADS) * local_experts
     is_local = (flat_routes >= first_expert) & (flat_routes < first_expert + local_experts)
     target = jnp.where(is_local, (flat_routes - first_expert) * capacity + slot_index, slot_count)
     owner_row = jnp.arange(group_rows * top_choices, dtype=jnp.int32) // top_choices
@@ -157,7 +166,7 @@
     )
     moe_part = moe_part.reshape(group_images, token_slots, model_width)
     expert_sum = lax.psum(
-        lax.psum_scatter(moe_part, "tensor", scatter_dimension=0, tiled=True), "heads"
+        lax.psum_scatter(moe_part, TENSOR, scatter_dimension=0, tiled=True), HEADS
     )
     final = residual + expert_sum
     valid_rows = valid_mask.astype(jnp.float32)[..., None]
@@ -172,7 +181,7 @@
     qkv_full, output_complete, router_full, gain_a, gain_b = dense_set
     up_full, down_full = expert_set
     moe_grad = final_grad.astype(jnp.bfloat16)
-    group_grad = lax.all_gather(moe_grad, "tensor", axis=0, tiled=True).reshape(
+    group_grad = lax.all_gather(moe_grad, TENSOR, axis=0, tiled=True).reshape(
         group_rows, model_width
     )
     slot_grad = group_grad[source].astype(jnp.float32)
@@ -206,11 +215,11 @@
         group_images, token_slots, top_choices
     )
     rows_share, gate_share = (
-        lax.psum_scatter(rows_part, "tensor", scatter_dimension=0, tiled=True),
-        lax.psum_scatter(gate_part, "tensor", scatter_dimension=0, tiled=True),
-    )
-    second_grad, gate_grad = lax.psum((rows_share, gate_share), "heads")
-    own_start = lax.axis_index("tensor") * image_count * token_slots
+        lax.psum_scatter(rows_part, TENSOR, scatter_dimension=0, tiled=True),
+        lax.psum_scatter(gate_part, TENSOR, scatter_dimension=0, tiled=True),
+    )
+    second_grad, gate_grad = lax.psum((rows_share, gate_share), HEADS)
+    own_start = lax.axis_index(TENSOR) * image_count * token_slots
     own_rows = image_count * token_slots
     own_probs = lax.dynamic_slice_in_dim(router_probs, own_start, own_rows, 0).reshape(
         image_count, token_slots, expert_count
@@ -272,17 +281,17 @@
     first_part = jnp.einsum(
         "ishe,dhe->isd", projected_grad, qkv_full, preferred_element_type=jnp.float32
     )
-    first_grad = lax.psum(first_part, "heads")
+    first_grad = lax.psum(first_part, HEADS)
     input_norm, gain_one_grad = norm_back(
         first_grad, normed_one, spread_one, gain_a.astype(jnp.float32)
     )
     tokens_grad = residual_grad + input_norm
     dense_grads = (
-        lax.psum_scatter(qkv_grad, ("fsdp", "tensor"), scatter_dimension=0, tiled=True),
-        lax.psum_scatter(out_weight_grad, ("fsdp", "tensor"), scatter_dimension=2, tiled=True),
-        lax.psum_scatter(router_grad, ("fsdp", "tensor"), scatter_dimension=0, tiled=True),
-        lax.psum_scatter(gain_one_grad, ("fsdp", "tensor"), scatter_dimension=0, tiled=True),
-        lax.psum_scatter(gain_two_grad, ("fsdp", "tensor"), scatter_dimension=0, tiled=True),
+        lax.psum_scatter(qkv_grad, (FSDP, TENSOR), scatter_dimension=0, tiled=True),
+        lax.psum_scatter(out_weight_grad, (FSDP, TENSOR), scatter_dimension=2, tiled=True),
+        lax.psum_scatter(router_grad, (FSDP, TENSOR), scatter_dimension=0, tiled=True),
+        lax.psum_scatter(gain_one_grad, (FSDP, TENSOR), scatter_dimension=0, tiled=True),
+        lax.psum_scatter(gain_two_grad, (FSDP, TENSOR), scatter_dimension=0, tiled=True),
     )
     expert_grads = reduce_expert_grads(expert_up_grad, expert_down_grad)
     return (
@@ -299,30 +308,1024 @@
     )
 
 
+MESH = pl.DeviceIdType.MESH
+LOW = jnp.bfloat16
+WIDE = jnp.float32
+
+
+class Links:
+    def __init__(self, send_sems, recv_sems):
+        self.send_sems, self.recv_sems = send_sems, recv_sems
+        self.copies = []
+
+    def send(self, src, dst, device):
+        k = len(self.copies)
+        copy = pltpu.make_async_remote_copy(
+            src_ref=src,
+            dst_ref=dst,
+            send_sem=self.send_sems.at[k],
+            recv_sem=self.recv_sems.at[k],
+            device_id=device,
+            device_id_type=MESH,
+        )
+        copy.start()
+        self.copies.append(copy)
+        return copy
+
+    def drain(self):
+        for copy in self.copies:
+            copy.wait_send()
+
+
+class Place:
+    def __init__(self, heads):
+        self.f = lax.axis_index(FSDP)
+        t = lax.axis_index(TENSOR)
+        self.y, self.c = t // 2, lax.rem(t, 2)
+        self.z = lax.axis_index(HEADS)
+        self.heads = heads
+        self.x_peer = {FSDP: 1 - self.f}
+        self.y_peer = {TENSOR: 2 * (1 - self.y) + self.c}
+        self.core_peer = {TENSOR: 2 * self.y + 1 - self.c}
+        self.z_peers = [{HEADS: lax.rem(self.z + k, heads)} for k in range(1, heads)]
+        self.plane_peers = []
+        for a in range(2):
+            for k in range(4):
+                if a or k:
+                    where = {TENSOR: lax.rem(t + k, 4)}
+                    if a:
+                        where[FSDP] = 1 - self.f
+                    self.plane_peers.append(where)
+
+    def image(self, df, dy, dc):
+        f = 1 - self.f if df else self.f
+        y = 1 - self.y if dy else self.y
+        c = 1 - self.c if dc else self.c
+        return f * 4 + 2 * y + c
+
+    def greet(self, devices):
+        barrier = pltpu.get_barrier_semaphore()
+        for device in devices:
+            pl.semaphore_signal(barrier, inc=1, device_id=device, device_id_type=MESH)
+        pl.semaphore_wait(barrier, len(devices))
+
+    def axis_peers(self):
+        return [self.x_peer, self.y_peer, self.core_peer]
+
+
+class PlaneGather:
+    def __init__(self, links, place, first, second, whole):
+        self.links, self.place = links, place
+        self.first, self.second, self.whole = first, second, whole
+
+    def go(self, part, image, device):
+        return self.links.send(part(image), part(image), device)
+
+    def start(self):
+        p, me = self.place, self.place.image(0, 0, 0)
+        self.xa = self.go(self.first, me, p.x_peer)
+        self.yb = self.go(self.second, me, p.y_peer)
+        self.own = self.go(self.whole, me, p.core_peer)
+        self.xb = self.go(self.second, me, p.x_peer)
+        self.ya = self.go(self.first, me, p.y_peer)
+
+    def forward(self):
+        p = self.place
+        self.xa.wait_recv()
+        self.fa = self.go(self.first, p.image(1, 0, 0), p.y_peer)
+        self.yb.wait_recv()
+        self.fb = self.go(self.second, p.image(0, 1, 0), p.x_peer)
+
+    def share(self):
+        p = self.place
+        self.xb.wait_recv()
+        self.c1 = self.go(self.whole, p.image(1, 0, 0), p.core_peer)
+        self.ya.wait_recv()
+        self.c2 = self.go(self.whole, p.image(0, 1, 0), p.core_peer)
+
+    def finish(self):
+        p = self.place
+        self.fa.wait_recv()
+        self.fb.wait_recv()
+        self.c3 = self.go(self.whole, p.image(1, 1, 0), p.core_peer)
+        for copy in (self.own, self.c1, self.c2, self.c3):
+            copy.wait_recv()
+
+    def run(self):
+        self.start()
+        self.forward()
+        self.share()
+        self.finish()
+
+
+GATHER_COPIES = 10
+
+
+def in_rows(rows, step, body):
+    def one(i, carry):
+        body(pl.ds(pl.multiple_of(i * step, step), step))
+        return carry
+
+    lax.fori_loop(0, rows // step, one, 0)
+
+
+class PlaneSum:
+    def __init__(self, links, place, part, core_in, xa, ya, yb, xb, cut, step):
+        self.links, self.place, self.part, self.core_in = links, place, part, core_in
+        self.xa, self.ya, self.yb, self.xb, self.cut, self.step = xa, ya, yb, xb, cut, step
+        self.rows, self.width = part.shape[1], part.shape[2]
+        self.a, self.b = pl.ds(0, cut), pl.ds(cut, self.width - cut)
+
+    def start(self):
+        p = self.place
+        self.order = [(1, 1), (1, 0), (0, 1), (0, 0)]
+        self.into = {}
+        for df, dy in self.order:
+            f = 1 - p.f if df else p.f
+            y = 1 - p.y if dy else p.y
+            self.into[df, dy] = self.links.send(
+                self.part.at[p.image(df, dy, 1)], self.core_in.at[2 * f + y], p.core_peer
+            )
+
+    def slot(self, df, dy):
+        p = self.place
+        return 2 * (1 - p.f if df else p.f) + (1 - p.y if dy else p.y)
+
+    def cores(self):
+        p, rc = self.place, self.core_in
+        self.got = {}
+        for df, dy in self.order:
+            self.into[df, dy].wait_recv()
+            j, mine = self.slot(df, dy), p.image(df, dy, 0)
+
+            def add(rows, j=j, mine=mine):
+                both = rc[j, rows, :].astype(WIDE) + self.part[mine, rows, :].astype(WIDE)
+                rc[j, rows, :] = both.astype(LOW)
+
+            in_rows(self.rows, self.step, add)
+            y = 1 - p.y if dy else p.y
+            f = 1 - p.f if df else p.f
+            if df:
+                self.got["x", dy] = self.links.send(rc.at[j, :, self.a], self.xa.at[y], p.x_peer)
+            if dy:
+                self.got["y", df] = self.links.send(rc.at[j, :, self.b], self.yb.at[f], p.y_peer)
+
+    def cross(self):
+        p, rc, xa, yb = self.place, self.core_in, self.xa, self.yb
+        self.got["x", 1].wait_recv()
+        j, other = self.slot(0, 1), 1 - p.y
+
+        def add_a(rows):
+            both = xa[other, rows, :].astype(WIDE) + rc[j, rows, self.a].astype(WIDE)
+            xa[other, rows, :] = both.astype(LOW)
+
+        in_rows(self.rows, self.step, add_a)
+        self.last_a = self.links.send(xa.at[other], self.ya, p.y_peer)
+        self.got["y", 1].wait_recv()
+        k, away = self.slot(1, 0), 1 - p.f
+
+        def add_b(rows):
+            both = yb[away, rows, :].astype(WIDE) + rc[k, rows, self.b].astype(WIDE)
+            yb[away, rows, :] = both.astype(LOW)
+
+        in_rows(self.rows, self.step, add_b)
+        self.last_b = self.links.send(yb.at[away], self.xb, p.x_peer)
+
+    def finish(self, take):
+        p, rc = self.place, self.core_in
+        self.got["x", 0].wait_recv()
+        self.got["y", 0].wait_recv()
+        self.last_a.wait_recv()
+        self.last_b.wait_recv()
+        j, y, f = self.slot(0, 0), p.y, p.f
+
+        def add(rows):
+            first = rc[j, rows, self.a].astype(WIDE) + self.xa[y, rows, :].astype(WIDE)
+            second = rc[j, rows, self.b].astype(WIDE) + self.yb[f, rows, :].astype(WIDE)
+            take(rows, self.a, first + self.ya[rows, :].astype(WIDE))
+            take(rows, self.b, second + self.xb[rows, :].astype(WIDE))
+
+        in_rows(self.rows, self.step, add)
+
+
+SUM_COPIES = 10
+
+
+def sum_scratch(rows, width, cut):
+    return [
+        pltpu.VMEM((4, rows, width), LOW),
+        pltpu.VMEM((2, rows, cut), LOW),
+        pltpu.VMEM((rows, cut), LOW),
+        pltpu.VMEM((2, rows, width - cut), LOW),
+        pltpu.VMEM((rows, width - cut), LOW),
+    ]
+
+
+def all_heads(links, place, make):
+    copies = []
+    for k, device in enumerate(place.z_peers):
+        src, dst = make(k, device[HEADS])
+        copies.append(links.send(src, dst, device))
+    return copies
+
+
+def remote_call(kernel, outs, ins, scratch, copies, collective_id, vmem_mib):
+    vmem = pl.BlockSpec(memory_space=pltpu.VMEM)
+    return pl.pallas_call(
+        kernel,
+        out_shape=outs,
+        in_specs=[vmem] * len(ins),
+        out_specs=[vmem] * len(outs),
+        scratch_shapes=[
+            *scratch,
+            pltpu.SemaphoreType.DMA((copies,)),
+            pltpu.SemaphoreType.DMA((copies,)),
+        ],
+        compiler_params=pltpu.CompilerParams(
+            collective_id=collective_id,
+            has_side_effects=True,
+            vmem_limit_bytes=vmem_mib * 2**20,
+        ),
+    )(*ins)
+
+
+def shape(dims, dtype=LOW):
+    return jax.ShapeDtypeStruct(dims, dtype)
+
+
+def weights_kernel(heads, wq, wo, count, route, oq, oo, counts, far_route, ss, rs):
+    place = Place(heads)
+    links = Links(ss, rs)
+    me = place.image(0, 0, 0)
+    place.greet(place.plane_peers + place.z_peers)
+    oq[me] = wq[...]
+    oo[me, place.z] = wo[...]
+    counts[me] = count[...]
+    half = wq.shape[1] // 2
+    mid = heads // 2
+    main = PlaneGather(
+        links,
+        place,
+        lambda i: oq.at[i, :, pl.ds(0, half)],
+        lambda i: oq.at[i, :, pl.ds(half, half)],
+        lambda i: oq.at[i],
+    )
+    side = PlaneGather(
+        links,
+        place,
+        lambda i: oo.at[i, pl.ds(0, mid)],
+        lambda i: oo.at[i, pl.ds(mid, heads - mid)],
+        lambda i: oo.at[i],
+    )
+    main.start()
+    along = all_heads(
+        links, place, lambda k, z: (oo.at[me, place.z], oo.at[me, place.z])
+    )
+    small = [links.send(counts.at[me], counts.at[me], d) for d in place.plane_peers]
+    small.append(links.send(route, far_route, place.x_peer))
+    main.forward()
+    for copy in along:
+        copy.wait_recv()
+    side.start()
+    main.share()
+    main.finish()
+    side.forward()
+    side.share()
+    side.finish()
+    for copy in small:
+        copy.wait_recv()
+    links.drain()
+
+
+def gather_weights_fast(heads, wq, wo, count, route):
+    outs = [
+        shape((8, *wq.shape)),
+        shape((8, heads, *wo.shape)),
+        shape((8, *count.shape), jnp.int32),
+        shape(route.shape, jnp.int32),
+    ]
+    copies = 2 * GATHER_COPIES + heads - 1 + 7 + 1
+    return remote_call(
+        functools.partial(weights_kernel, heads),
+        outs,
+        [wq, wo, count, route],
+        [],
+        copies,
+        1,
+        32,
+    )
+
+
+def mix_kernel(
+    heads,
+    experts,
+    mixed,
+    wo,
+    tokens,
+    gain,
+    router,
+    residual,
+    second,
+    group,
+    probs,
+    everyone,
+    other_half,
+    ss,
+    rs,
+):
+    place = Place(heads)
+    links = Links(ss, rs)
+    me = place.image(0, 0, 0)
+    place.greet(place.plane_peers + place.z_peers)
+    everyone[place.z] = mixed[...]
+    along = all_heads(links, place, lambda k, z: (everyone.at[place.z], everyone.at[place.z]))
+    for copy in along:
+        copy.wait_recv()
+    rows_all, width = tokens.shape
+    half = width // 2
+    total = jnp.zeros((rows_all, width), WIDE)
+    for z in range(heads):
+        weight = wo[:, z].reshape(width, wo.shape[3])
+        total = total + lax.dot_general(
+            everyone[z], weight, (((1,), (1,)), ((), ())), preferred_element_type=WIDE
+        )
+    residual[...] = total
+
+    def norm(rows):
+        values = tokens[rows, :].astype(WIDE) + residual[rows, :]
+        residual[rows, :] = values
+        normed, _ = normalize(values)
+        second[rows, :] = (normed * gain[...]).astype(LOW)
+
+    in_rows(rows_all, 64, norm)
+    low, high = second[:, :half], second[:, half:]
+    first = place.f == 0
+    group[me] = jnp.where(first, low, high)
+    other_half[...] = jnp.where(first, high, low)
+    x1 = links.send(other_half, group.at[me], place.x_peer)
+    y1 = links.send(group.at[me], group.at[me], place.y_peer)
+    shared = [links.send(group.at[me], group.at[me], place.core_peer)]
+    logits = lax.dot_general(
+        router[...], second[...], (((0,), (1,)), ((), ())), preferred_element_type=WIDE
+    )[:experts]
+    powers = jnp.exp(logits - jnp.max(logits, 0, keepdims=True))
+    probs[me] = powers / jnp.sum(powers, 0, keepdims=True)
+    small = [links.send(probs.at[me], probs.at[me], d) for d in place.plane_peers]
+    across, beside, corner = place.image(1, 0, 0), place.image(0, 1, 0), place.image(1, 1, 0)
+    x1.wait_recv()
+    y2 = links.send(group.at[across], group.at[across], place.y_peer)
+    shared.append(links.send(group.at[across], group.at[across], place.core_peer))
+    y1.wait_recv()
+    shared.append(links.send(group.at[beside], group.at[beside], place.core_peer))
+    y2.wait_recv()
+    shared.append(links.send(group.at[corner], group.at[corner], place.core_peer))
+    for copy in shared + small:
+        copy.wait_recv()
+    links.drain()
+
+
+def mix_heads(heads, experts, mixed, wo, tokens, gain, router):
+    rows, width = tokens.shape
+    return remote_call(
+        functools.partial(mix_kernel, heads, experts),
+        [
+            shape((rows, width), WIDE),
+            shape((rows, width)),
+            shape((8, rows, width // 2)),
+            shape((8, experts, rows), WIDE),
+        ],
+        [mixed, wo, tokens, gain, router],
+        [pltpu.VMEM((heads, *mixed.shape), LOW), pltpu.VMEM((rows, width // 2), LOW)],
+        heads - 1 + 7 + 7,
+        2,
+        48,
+    )
+
+
+def combine_kernel(
+    heads,
+    part,
+    residual,
+    teacher,
+    valid,
+    scale,
+    result,
+    final_grad,
+    group,
+    loss,
+    core_in,
+    xa,
+    ya,
+    yb,
+    xb,
+    image_sum,
+    far,
+    ss,
+    rs,
+):
+    place = Place(heads)
+    links = Links(ss, rs)
+    me = place.image(0, 0, 0)
+    z = place.z
+    place.greet(place.axis_peers() + place.z_peers)
+    rows_all, width = residual.shape
+    own = rows_all // heads
+    adder = PlaneSum(links, place, part, core_in, xa, ya, yb, xb, width // 2, 32)
+    adder.start()
+    adder.cores()
+    adder.cross()
+
+    def keep(rows, columns, values):
+        image_sum[rows, columns] = values.astype(LOW)
+
+    adder.finish(keep)
+    along = all_heads(
+        links,
+        place,
+        lambda k, to: (image_sum.at[pl.ds(pl.multiple_of(to * own, own), own)], far.at[k]),
+    )
+    for copy in along:
+        copy.wait_recv()
+    mine = pl.ds(pl.multiple_of(z * own, own), own)
+    total = image_sum[mine, :].astype(WIDE)
+    for k in range(heads - 1):
+        total = total + far[k].astype(WIDE)
+    final = residual[mine, :] + total
+    result[z] = final.astype(LOW)
+    error = (final - teacher[mine, :].astype(WIDE)) * valid[mine, :]
+    grad = error * scale[0:1, 0:1]
+    final_grad[...] = grad
+    group[me, mine, :] = grad.astype(LOW)
+    along = all_heads(links, place, lambda k, to: (group.at[me, mine], group.at[me, mine]))
+    squares = jnp.sum((error * error).reshape(own // 8, 8, width), axis=0)
+    loss[z] = sum(squares[:, i * 128 : (i + 1) * 128] for i in range(width // 128))
+    extra = all_heads(links, place, lambda k, to: (result.at[z], result.at[z]))
+    extra += all_heads(links, place, lambda k, to: (loss.at[z], loss.at[z]))
+    for copy in along:
+        copy.wait_recv()
+    half = width // 2
+    PlaneGather(
+        links,
+        place,
+        lambda i: group.at[i, :, pl.ds(0, half)],
+        lambda i: group.at[i, :, pl.ds(half, half)],
+        lambda i: group.at[i],
+    ).run()
+    for copy in extra:
+        copy.wait_recv()
+    links.drain()
+
+
+def combine(heads, part, residual, teacher, valid, scale):
+    rows, width = residual.shape
+    own = rows // heads
+    return remote_call(
+        functools.partial(combine_kernel, heads),
+        [
+            shape((heads, own, width)),
+            shape((own, width), WIDE),
+            shape((8, rows, width)),
+            shape((heads, 8, 128), WIDE),
+        ],
+        [part, residual, teacher, valid, scale],
+        [
+            *sum_scratch(rows, width, width // 2),
+            pltpu.VMEM((rows, width), LOW),
+            pltpu.VMEM((heads - 1, own, width), LOW),
+        ],
+        GATHER_COPIES + SUM_COPIES + 4 * (heads - 1),
+        3,
+        56,
+    )
+
+
+def back_kernel(
+    heads,
+    experts,
+    part,
+    residual,
+    gain,
+    router,
+    final_grad,
+    attended,
+    logit_grads,
+    residual_grad,
+    gain_part,
+    core_in,
+    y_in,
+    far,
+    pair,
+    x_in,
+    ss,
+    rs,
+):
+    place = Place(heads)
+    links = Links(ss, rs)
+    f, y, z = place.f, place.y, place.z
+    place.greet(place.axis_peers() + place.z_peers)
+    rows_all, width = residual.shape
+    half = width // 2
+    own = rows_all // heads
+    into = {}
+    for dy in (1, 0):
+        for df in (1, 0):
+            slot = 2 * (1 - f if df else f) + (1 - y if dy else y)
+            into[df, dy] = links.send(
+                part.at[place.image(df, dy, 1)], core_in.at[slot], place.core_peer
+            )
+    beside = {}
+    for dy in (1, 0):
+        for df in (1, 0):
+            to = 1 - f if df else f
+            slot = 2 * to + (1 - y if dy else y)
+            mine = place.image(df, dy, 0)
+            into[df, dy].wait_recv()
+
+            def add(rows, slot=slot, mine=mine):
+                both = core_in[slot, rows, :].astype(WIDE) + part[mine, rows, :].astype(WIDE)
+                core_in[slot, rows, :] = both.astype(LOW)
+
+            in_rows(rows_all, 32, add)
+            if dy:
+                beside[df] = links.send(core_in.at[slot], y_in.at[to], place.y_peer)
+    for df in (1, 0):
+        to = 1 - f if df else f
+        slot = 2 * to + y
+        beside[df].wait_recv()
+
+        def add_y(rows, slot=slot, to=to):
+            both = core_in[slot, rows, :].astype(WIDE) + y_in[to, rows, :].astype(WIDE)
+            y_in[to, rows, :] = both.astype(LOW)
+
+        in_rows(rows_all, 32, add_y)
+    along = all_heads(
+        links,
+        place,
+        lambda k, to: (y_in.at[:, pl.ds(pl.multiple_of(to * own, own), own)], far.at[k]),
+    )
+    mine = pl.ds(pl.multiple_of(z * own, own), own)
+    normed, spread = normalize(residual[mine, :])
+    second_in = (normed * gain[...]).astype(LOW)
+    logits = jnp.dot(second_in, router[...], preferred_element_type=WIDE)
+    lanes = lax.broadcasted_iota(jnp.int32, logits.shape, 1)
+    logits = jnp.where(lanes < experts, logits, MASKED)
+    powers = jnp.exp(logits - jnp.max(logits, -1, keepdims=True))
+    probs = powers / jnp.sum(powers, -1, keepdims=True)
+    for copy in along:
+        copy.wait_recv()
+    for index in (1 - f, f):
+        total = y_in[index, mine, :].astype(WIDE)
+        for k in range(heads - 1):
+            total = total + far[k, index].astype(WIDE)
+        pair[index] = total.astype(LOW)
+    cross = links.send(pair.at[1 - f], x_in, place.x_peer)
+    near = pair[f].astype(WIDE)
+    cross.wait_recv()
+    away = x_in[...].astype(WIDE)
+    prob_grad = near[:, half:] + away[:, half:]
+    low, high = near[:, :half], away[:, :half]
+    first = f == 0
+    rows_grad = jnp.concatenate([jnp.where(first, low, high), jnp.where(first, high, low)], 1)
+    inner = jnp.sum(probs * prob_grad, -1, keepdims=True)
+    logit_grad = (probs * (prob_grad - inner)).astype(LOW)
+    logit_grads[z] = logit_grad
+    second_grad = rows_grad + lax.dot_general(
+        logit_grad, router[...], (((1,), (1,)), ((), ())), preferred_element_type=WIDE
+    )
+    weighted = second_grad * gain[...]
+    gain_part[...] = jnp.sum((second_grad * normed).reshape(own // 8, 8, width), axis=0)
+    inner = (
+        weighted
+        - jnp.mean(weighted, -1, keepdims=True)
+        - normed * jnp.mean(weighted * normed, -1, keepdims=True)
+    )
+    total_grad = final_grad[...] + inner * spread
+    residual_grad[...] = total_grad
+    attended[z] = total_grad.astype(LOW)
+    along = all_heads(links, place, lambda k, to: (attended.at[z], attended.at[z]))
+    along += all_heads(links, place, lambda k, to: (logit_grads.at[z], logit_grads.at[z]))
+    for copy in along:
+        copy.wait_recv()
+    links.drain()
+
+
+def back_through_norm(heads, experts, part, residual, gain, router, final_grad):
+    rows, width = residual.shape
+    own = rows // heads
+    wide = part.shape[2]
+    return remote_call(
+        functools.partial(back_kernel, heads, experts),
+        [
+            shape((heads, own, width)),
+            shape((heads, own, 128)),
+            shape((own, width), WIDE),
+            shape((8, width), WIDE),
+        ],
+        [part, residual, gain, router, final_grad],
+        [
+            pltpu.VMEM((4, rows, wide), LOW),
+            pltpu.VMEM((2, rows, wide), LOW),
+            pltpu.VMEM((heads - 1, 2, own, wide), LOW),
+            pltpu.VMEM((2, own, wide), LOW),
+            pltpu.VMEM((own, wide), LOW),
+        ],
+        4 + 2 + 1 + 3 * (heads - 1),
+        4,
+        56,
+    )
+
+
+def last_kernel(
+    heads,
+    first_part,
+    dense,
+    tokens,
+    gain,
+    residual_grad,
+    gain_parts,
+    tokens_grad,
+    dense_out,
+    gain_out,
+    core_in,
+    xa,
+    ya,
+    yb,
+    xb,
+    far,
+    rounded,
+    tiles,
+    tiles_z,
+    ss,
+    rs,
+):
+    place = Place(heads)
+    links = Links(ss, rs)
+    z = place.z
+    me = place.image(0, 0, 0)
+    place.greet(place.plane_peers + place.z_peers)
+    own, width = residual_grad.shape
+    adder = PlaneSum(links, place, dense, core_in, xa, ya, yb, xb, xa.shape[2], 32)
+    adder.start()
+    along = all_heads(links, place, lambda k, to: (first_part.at[to], far.at[k]))
+    tiles[me] = gain_parts[me]
+    small = []
+    for device in place.plane_peers:
+        to = (device[FSDP] if FSDP in device else place.f) * 4 + device[TENSOR]
+        small.append(links.send(gain_parts.at[to], tiles.at[me], device))
+    adder.cores()
+    adder.cross()
+    for copy in small:
+        copy.wait_recv()
+    tiles_z[z] = sum(tiles[i] for i in range(8))
+    gains = all_heads(links, place, lambda k, to: (tiles_z.at[z], tiles_z.at[z]))
+    mine = pl.ds(pl.multiple_of(z * own, own), own)
+    normed, spread = normalize(tokens[mine, :].astype(WIDE))
+    for copy in along:
+        copy.wait_recv()
+    first_grad = first_part[z].astype(WIDE)
+    for k in range(heads - 1):
+        first_grad = first_grad + far[k].astype(WIDE)
+    weighted = first_grad * gain[...]
+    inner = (
+        weighted
+        - jnp.mean(weighted, -1, keepdims=True)
+        - normed * jnp.mean(weighted * normed, -1, keepdims=True)
+    )
+    rounded[z] = (residual_grad[...] + inner * spread).astype(LOW)
+    along = all_heads(links, place, lambda k, to: (rounded.at[z], rounded.at[z]))
+
+    def keep(rows, columns, values):
+        dense_out[rows, columns] = values
+
+    adder.finish(keep)
+    for copy in gains:
+        copy.wait_recv()
+    gain_out[...] = sum(tiles_z[i] for i in range(heads))
+    for copy in along:
+        copy.wait_recv()
+    for i in range(heads):
+        tokens_grad[i] = rounded[i].astype(WIDE)
+    links.drain()
+
+
+def last_sums(heads, first_part, dense, tokens, gain, residual_grad, gain_parts):
+    own, width = residual_grad.shape
+    _, rows, wide = dense.shape
+    cut = 512 if wide == 896 else 128 * (wide // 256)
+    return remote_call(
+        functools.partial(last_kernel, heads),
+        [
+            shape((heads, own, width), WIDE),
+            shape((rows, wide), WIDE),
+            shape((8, 128), WIDE),
+        ],
+        [first_part, dense, tokens, gain, residual_grad, gain_parts],
+        [
+            *sum_scratch(rows, wide, cut),
+            pltpu.VMEM((heads - 1, own, width), LOW),
+            pltpu.VMEM((heads, own, width), LOW),
+            pltpu.VMEM((8, 8, 128), WIDE),
+            pltpu.VMEM((heads, 8, 128), WIDE),
+        ],
+        SUM_COPIES + 3 * (heads - 1) + 7,
+        5,
+        48,
+    )
+
+
+def by_index(index, own, other, axis):
+    return jnp.where(
+        index == 0,
+        jnp.concatenate([own, other], axis),
+        jnp.concatenate([other, own], axis),
+    )
+
+
+def swap(values):
+    return lax.ppermute(values, FSDP, [(0, 1), (1, 0)])
+
+
+def fast(
+    tokens,
+    valid_mask,
+    routes,
+    teacher,
+    gain_one,
+    qkv_weight,
+    out_weight,
+    gain_two,
+    router_weight,
+    expert_up,
+    expert_down,
+):
+    heads = lax.axis_size(HEADS)
+    f, z = lax.axis_index(FSDP), lax.axis_index(HEADS)
+    _, rows, width = tokens.shape
+    block, head_count, qkv_dim = qkv_weight.shape
+    head_dim = qkv_dim // 3
+    local_experts = expert_up.shape[0]
+    kept = local_experts // 2
+    expert_count = local_experts * heads
+    group_rows = 4 * rows
+    capacity = 2 * routes.shape[2] * group_rows // expert_count
+    total_tokens, total_images = 8 * rows, 8
+    score_scale = head_dim ** (-0.5)
+
+    mine, theirs = f * kept, (1 - f) * kept
+    half = width // 2
+
+    qkv_width = head_count * qkv_dim
+    pad = -(128 + qkv_width) % 256
+    wq = jnp.concatenate(
+        [
+            router_weight,
+            gain_one[:, None],
+            gain_two[:, None],
+            jnp.zeros((block, 128 - expert_count - 2), LOW),
+            qkv_weight.reshape(block, qkv_width),
+            jnp.zeros((block, pad), LOW),
+        ],
+        1,
+    )
+    wo = out_weight.reshape(head_count * head_dim, block).T
+    count = jnp.full((8, 128), jnp.sum(valid_mask), jnp.int32)
+    near_route = jnp.pad(routes.reshape(group_rows, -1).T, ((0, 8 - routes.shape[2]), (0, 0)))
+    gathered, wo_all, counts, far_route = gather_weights_fast(heads, wq, wo, count, near_route)
+    gathered, down_away = lax.optimization_barrier(
+        (gathered, lax.dynamic_slice_in_dim(expert_down, theirs, kept, 0))
+    )
+    down_far = swap(down_away)
+    down_near = lax.dynamic_slice_in_dim(expert_down, mine, kept, 0)
+    gathered = gathered.reshape(width, -1)
+    qkv_full = gathered[:, 128 : 128 + qkv_width]
+    lanes = jnp.arange(128)
+    router_wide = jnp.where(lanes < expert_count, gathered[:, :128], 0)
+    gain_a = gathered[:, expert_count].astype(WIDE)[None]
+    gain_b = gathered[:, expert_count + 1].astype(WIDE)[None]
+    valid_total = jnp.sum(counts[:, 0, 0]).astype(WIDE)
+
+    inputs = tokens[0].astype(WIDE)
+    normed_one, _ = normalize(inputs)
+    first_in = (normed_one * gain_a).astype(LOW)
+    projected = (
+        jnp.dot(first_in, qkv_full, preferred_element_type=WIDE)
+        .astype(LOW)
+        .reshape(rows, head_count, qkv_dim)
+    )
+    queries = projected[..., :head_dim]
+    key_rows = projected[..., head_dim : 2 * head_dim]
+    values = projected[..., 2 * head_dim :]
+    keys_ok = (valid_mask > 0)[0][None, None, :]
+
+    def scores_now():
+        raw = jnp.einsum("qhe,khe->hqk", queries, key_rows, preferred_element_type=WIDE)
+        return jnp.where(keys_ok, raw * score_scale, MASKED)
+
+    scores = scores_now()
+    peak_score = jnp.max(scores, -1, keepdims=True)
+    exp_scores = jnp.exp(scores - peak_score)
+    score_total = jnp.sum(exp_scores, -1, keepdims=True)
+    logarithm_total = peak_score + jnp.log(score_total)
+    attention = (exp_scores / score_total).astype(LOW)
+    mixed = (
+        jnp.einsum("hqk,khe->qhe", attention, values, preferred_element_type=WIDE)
+        .astype(LOW)
+        .reshape(rows, head_count * head_dim)
+    )
+    residual, second_in, group_in, probs_all = mix_heads(
+        heads, expert_count, mixed, wo_all, tokens[0], gain_b, router_wide
+    )
+
+    both = by_index(f, near_route[None], far_route[None], 0)[:, : routes.shape[2]]
+    rows_in = group_in.reshape(2, group_rows, half)
+    probs_all = probs_all.reshape(2, 4, expert_count, rows)
+    order = jnp.arange(group_rows, dtype=jnp.int32)
+    earlier = (order[:, None] < order[None, :]).astype(LOW)
+
+    def picks(start):
+        ids = z * local_experts + start + jnp.arange(kept, dtype=jnp.int32)
+        chosen = jnp.any(both[:, None] == ids[None, :, None, None], 2)
+        slot = jnp.einsum(
+            "get,tu->geu", chosen.astype(LOW), earlier, preferred_element_type=WIDE
+        ).astype(jnp.int32)
+        return chosen[:, :, None, :] & (
+            slot[:, :, None, :] == jnp.arange(capacity, dtype=jnp.int32)[None, None, :, None]
+        )
+
+    def dispatch(pick, values):
+        out = jnp.einsum("gest,gtd->egsd", pick, values, preferred_element_type=WIDE)
+        return out.reshape(kept, 2 * capacity, values.shape[-1])
+
+    def collect(pick, values):
+        values = values.reshape(kept, 2, capacity, values.shape[-1])
+        return jnp.einsum("gest,egsd->gtd", pick, values, preferred_element_type=WIDE)
+
+    hot = picks(mine)
+    pick_near, pick_far = hot.astype(LOW), picks(theirs).astype(LOW)
+    up_near = lax.dynamic_slice_in_dim(expert_up, mine, kept, 0)
+    up_far = lax.dynamic_slice_in_dim(expert_up, theirs, kept, 0)
+    buffer_far = dispatch(pick_far, rows_in).astype(LOW)
+    away = jnp.einsum("ecd,edf->ecf", buffer_far, up_far, preferred_element_type=WIDE)
+    arrived = swap(away.astype(LOW))
+    buffer_near = dispatch(pick_near, rows_in).astype(LOW)
+    before_gelu = jnp.einsum("ecd,edf->ecf", buffer_near, up_near, preferred_element_type=WIDE)
+    before_gelu = before_gelu + arrived.astype(WIDE)
+    probs_own = lax.dynamic_slice_in_dim(probs_all, z * local_experts + mine, kept, 2)
+    probs_own = jnp.swapaxes(probs_own, 1, 2).reshape(2, kept, 1, group_rows)
+    slot_gate = jnp.sum(jnp.where(hot, probs_own, 0.0), -1)
+    gates = jnp.swapaxes(slot_gate, 0, 1).reshape(kept, 2 * capacity, 1)
+    down_full = by_index(f, down_near, down_far, 2)
+    hidden = jax.nn.gelu(before_gelu, approximate=False).astype(LOW)
+    expert_out = jnp.einsum("ecf,efd->ecd", hidden, down_full, preferred_element_type=WIDE)
+    part = collect(pick_near, (expert_out * gates).astype(LOW)).astype(LOW)
+    part = part.reshape(8, rows, width)
+
+    valid_rows = valid_mask[0].astype(WIDE)[:, None]
+    scale = jnp.full((8, 128), total_tokens / valid_total, WIDE)
+    result, final_grad, group_grad, loss = combine(
+        heads, part, residual, teacher[0], valid_rows, scale
+    )
+    loss_terms = (jnp.sum(loss) * (total_images / (valid_total * width)))[None]
+
+    slot_grad = dispatch(pick_near, group_grad.reshape(2, group_rows, width))
+    out_grad = (slot_grad * gates).astype(LOW)
+    raw = jnp.einsum(
+        "ecd,efd->ecf", slot_grad.astype(LOW), down_full, preferred_element_type=WIDE
+    )
+    gate_slot_grad = jnp.sum(raw * hidden.astype(WIDE), -1)
+    normal_cdf = 0.5 * (1.0 + lax.erf(before_gelu * ROOT_HALF))
+    slope = normal_cdf + before_gelu * DENSITY * jnp.exp(-0.5 * before_gelu * before_gelu)
+    pre_near = (raw * gates * slope).astype(LOW)
+    pre_far = swap(pre_near)
+    down_grad = jnp.einsum("ecf,ecd->efd", hidden, out_grad, preferred_element_type=WIDE)
+    down_own = lax.dynamic_slice_in_dim(down_grad, f * half, half, 2)
+    down_send = lax.dynamic_slice_in_dim(down_grad, (1 - f) * half, half, 2).astype(LOW)
+    ids = z * local_experts + mine + jnp.arange(kept, dtype=jnp.int32)
+    column = (ids[:, None, None] == lanes).astype(WIDE)
+
+    def through_up(pick, buffer, pre, up, extra):
+        grad = jnp.einsum("ecd,ecf->edf", buffer, pre, preferred_element_type=WIDE)
+        rows_out = jnp.einsum("ecf,edf->ecd", pre, up, preferred_element_type=WIDE)
+        rows_out = jnp.concatenate([rows_out, extra], -1).astype(LOW)
+        return grad, collect(pick, rows_out)
+
+    up_own, back_near = through_up(
+        pick_near, buffer_near, pre_near, up_near, gate_slot_grad[..., None] * column
+    )
+    up_other, back_far = through_up(
+        pick_far, buffer_far, pre_far, up_far, jnp.zeros((kept, 2 * capacity, 128), WIDE)
+    )
+    back_part = (back_near + back_far).astype(LOW).reshape(8, rows, -1)
+
+    attended, logit_grads, residual_grad, gain_two_part = back_through_norm(
+        heads, expert_count, back_part, residual, gain_b, router_wide, final_grad
+    )
+    attended, down_send = lax.optimization_barrier((attended, down_send))
+    down_other = swap(down_send)
+
+    attended_grad = attended.reshape(rows, width)
+    wo_own = lax.dynamic_index_in_dim(wo_all, z, 1, False).reshape(width, -1)
+    mixed_grad = (
+        jnp.dot(attended_grad, wo_own, preferred_element_type=WIDE)
+        .astype(LOW)
+        .reshape(rows, head_count, head_dim)
+    )
+    scores = scores_now()
+    probs = jnp.exp(scores - logarithm_total)
+    prob_part = jnp.einsum("qhe,khe->hqk", mixed_grad, values, preferred_element_type=WIDE)
+    score_grad = (probs * (prob_part - jnp.sum(probs * prob_part, -1, keepdims=True))).astype(LOW)
+    query_grad = (
+        jnp.einsum("hqk,khe->qhe", score_grad, key_rows, preferred_element_type=WIDE) * score_scale
+    )
+    key_grad = (
+        jnp.einsum("hqk,qhe->khe", score_grad, queries, preferred_element_type=WIDE) * score_scale
+    )
+    value_grad = jnp.einsum(
+        "hqk,qhe->khe", probs.astype(LOW), mixed_grad, preferred_element_type=WIDE
+    )
+    projected_grad = (
+        jnp.concatenate([query_grad, key_grad, value_grad], -1)
+        .astype(LOW)
+        .reshape(rows, qkv_width)
+    )
+    first_part = lax.dot_general(
+        projected_grad, qkv_full, (((1,), (1,)), ((), ())), preferred_element_type=WIDE
+    )
+    gain_one_part = jnp.sum(first_part * normed_one, 0)
+    qkv_grad = jnp.einsum("sd,se->de", first_in, projected_grad, preferred_element_type=WIDE)
+    out_grad_t = jnp.einsum("sd,se->de", attended_grad, mixed, preferred_element_type=WIDE)
+    router_grad = jnp.einsum(
+        "sd,se->de", second_in, logit_grads.reshape(rows, 128), preferred_element_type=WIDE
+    )
+    dense = jnp.concatenate([qkv_grad, out_grad_t, router_grad], 1).astype(LOW)
+    gain_parts = jnp.stack([gain_one_part, jnp.sum(gain_two_part, 0)], 0).reshape(2, 8, block)
+    gain_parts = jnp.pad(jnp.swapaxes(gain_parts, 0, 1), ((0, 0), (0, 6), (0, 128 - block)))
+    tokens_grad, dense_out, gain_out = last_sums(
+        heads,
+        first_part.astype(LOW).reshape(heads, rows // heads, width),
+        dense.reshape(8, block, -1),
+        tokens[0],
+        gain_a,
+        residual_grad,
+        gain_parts,
+    )
+    out_width = head_count * head_dim
+    return (
+        result.reshape(1, rows, width),
+        loss_terms,
+        tokens_grad.reshape(1, rows, width),
+        gain_out[0, :block],
+        dense_out[:, :qkv_width].reshape(block, head_count, qkv_dim),
+        dense_out[:, qkv_width : qkv_width + out_width].T.reshape(head_count, head_dim, block),
+        gain_out[1, :block],
+        dense_out[:, qkv_width + out_width : qkv_width + out_width + expert_count],
+        by_index(f, up_own, up_other, 0),
+        by_index(f, down_own, down_other.astype(WIDE), 0),
+    )
+
+
+def local(sizes, *args):
+    tokens, routes, up = args[0], args[2], args[9]
+    fits = (
+        sizes[FSDP] == 2
+        and sizes[TENSOR] == 4
+        and sizes[HEADS] % 2 == 0
+        and tokens.shape[0] == 1
+        and up.shape[0] % 2 == 0
+        and tokens.shape[1] % (32 * sizes[HEADS]) == 0
+        and tokens.shape[2] % 256 == 0
+        and routes.shape[2] <= 8
+        and up.shape[0] * sizes[HEADS] <= 126
+    )
+    return fast(*args) if fits else general(*args)
+
+
 def solution(mesh):
+    sizes = dict(mesh.shape)
+    program = functools.partial(local, sizes)
     in_specs = (
-        P(("fsdp", "tensor"), None, None),
-        P(("fsdp", "tensor"), None),
-        P("fsdp", None, None),
-        P(("fsdp", "tensor"), None, None),
-        P(("fsdp", "tensor")),
-        P(("fsdp", "tensor"), "heads", None),
-        P("heads", None, ("fsdp", "tensor")),
-        P(("fsdp", "tensor")),
-        P(("fsdp", "tensor"), None),
-        P("heads", "fsdp", "tensor"),
-        P("heads", "tensor", "fsdp"),
+        P((FSDP, TENSOR), None, None),
+        P((FSDP, TENSOR), None),
+        P(FSDP, None, None),
+        P((FSDP, TENSOR), None, None),
+        P((FSDP, TENSOR)),
+        P((FSDP, TENSOR), HEADS, None),
+        P(HEADS, None, (FSDP, TENSOR)),
+        P((FSDP, TENSOR)),
+        P((FSDP, TENSOR), None),
+        P(HEADS, FSDP, TENSOR),
+        P(HEADS, TENSOR, FSDP),
     )
     out_specs = (
-        P(("fsdp", "tensor"), None, None),
-        P(("fsdp", "tensor")),
-        P(("fsdp", "tensor"), None, None),
-        P(("fsdp", "tensor")),
-        P(("fsdp", "tensor"), "heads", None),
-        P("heads", None, ("fsdp", "tensor")),
-        P(("fsdp", "tensor")),
-        P(("fsdp", "tensor"), None),
-        P("heads", "fsdp", "tensor"),
-        P("heads", "tensor", "fsdp"),
-    )
-    return jax.shard_map(local, mesh=mesh, in_specs=in_specs, out_specs=out_specs, check_vma=False)
+        P((FSDP, TENSOR), None, None),
+        P((FSDP, TENSOR)),
+        P((FSDP, TENSOR), None, None),
+        P((FSDP, TENSOR)),
+        P((FSDP, TENSOR), HEADS, None),
+        P(HEADS, None, (FSDP, TENSOR)),
+        P((FSDP, TENSOR)),
+        P((FSDP, TENSOR), None),
+        P(HEADS, FSDP, TENSOR),
+        P(HEADS, TENSOR, FSDP),
+    )
+    return jax.shard_map(program, mesh=mesh, in_specs=in_specs, out_specs=out_specs, check_vma=False)

time: 1250 us -> 437 us (0.35)
  waiting for transfers between devices: 914 us -> 66.6 us
  Pallas kernels: 0 us -> 221 us
  blocking collectives: 91.2 us -> 0 us
  local copies, waits for them, and re-layouts: 102 us -> 33.9 us
  other arithmetic: 55.8 us -> 38.1 us
  between operations: 20 us -> 4.07 us
  matrix products: 55.2 us -> 67.9 us
    reduce_scatter x5 -> x0, waiting for transfers between devices: 529 us -> none  [the longest x1 215 us: reduce_expert_grads(): lax.psum_scatter(up_grad, 'fsdp', scatter_dimension=1, tiled=True)]
    pallas_call x0 -> x5, Pallas kernels: none -> 221 us  [remote_call(): pl.pallas_call(kernel, out_shape=outs, in_specs=[vmem] * len(ins), out_sp...]
    all_gather x4 -> x0, waiting for transfers between devices: 212 us -> none  [the longest x1 105 us: gather_weights(): lax.all_gather(expert_down, 'fsdp', axis=2, tiled=True)]
    psum x4 -> x0, waiting for transfers between devices: 151 us -> none  [the longest x1 44.1 us: local(): attended = lax.psum(attn_part, 'heads')]
    ppermute x0 -> x4, waiting for transfers between devices: none -> 66.6 us  [swap(): return lax.ppermute(values, FSDP, [(0, 1), (1, 0)])]
    gather x9 -> x0, local copies, waits for them, and re-layouts: 59.6 us -> none  [the longest x2 18.4 us: local(): weighted[slot_pick] * retain_mask[:, None]]
    all_gather x3 -> x0, blocking collectives: 33.2 us -> none  [the longest x1 14.6 us: gather_weights(): lax.all_gather(qkv_weight, ('fsdp', 'tensor'), axis=0, tiled=True)]
    unnamed x3 -> x0, blocking collectives: 33 us -> none
  transfers between devices with their start and end apart: 15 -> 4, of which waited for: 14 -> 3; matrix products, arithmetic and copies ran while one was open for 9% -> 16% of each run, Pallas kernels for 0% -> 14%
where the time goes in v1:
time: 437 us; the launch traced here: 436 us
  Pallas kernels  221 us (51%)
  matrix products  67.9 us (16%)
  waiting for transfers between devices  66.6 us (15%)
  other arithmetic  38.1 us (9%)
  local copies, waits for them, and re-layouts  33.9 us (8%)
    pallas_call x5, Pallas kernels, remote_call(): pl.pallas_call(kernel, out_shape=outs, in_specs=[vmem] * len(ins), out_sp...  221 us
    ppermute x4, waiting for transfers between devices, swap(): return lax.ppermute(values, FSDP, [(0, 1), (1, 0)])  66.6 us
    dot_general x3, matrix products, dispatch(): jnp.einsum('gest,gtd->egsd', pick, values, preferred_element_type=WIDE)  17.5 us
    select_n x3, other arithmetic, by_index(): jnp.where(index == 0, jnp.concatenate([own, other], axis), jnp.concatenat...  13.2 us
    unnamed x91, local copies, waits for them, and re-layouts  11.9 us
    dot_general x3, matrix products, collect(): jnp.einsum('gest,egsd->gtd', pick, values, preferred_element_type=WIDE)  11.6 us
  transfers between devices with their start and end apart: 4, of which 3 were waited for; matrix products, arithmetic and copies ran while one was open for 16% of the time, Pallas kernels for 14%

profile of v1, /device:TPU:0, one launch (start us, length us, event | category | flops | bytes accessed | tf_op | source)
XLA Modules:
  0.0 435.8 jit_solution(4330571022737495825)
XLA Ops:
  1.4 1.9 convert_bitcast_fusion
  3.3 1.1 convert_reduce_fusion
  4.5 1.2 fusion.109
  9.7 1.1 copy.113
  11.7 21.8 %shard_map.186 = (bf16[8,96,768]{2,1,0:T(8,128)(2,1)S(1)}, bf16[8,4,96,192]{3,2,1,0:T(8,128)(2,1)S(1)}, s32[8,8,128]{2,1,0:T(8,128)S(1)}, s32[8,1024]{1,0:T(8,128)S(1)}) custom-call(bf16[96,768]{1,0:T(8,128)(2,1)S(1)} %concatenate.46.wq, bf16[96,192]{1,0:T(8,128)(2,1)S(1)} %bitcast.162, s32[8,128]{1,0:T(8,128)S(1)} %broadcast_in_dim.96.count, ...), custom_call_target="tpu_custom_call" | custom-call | tf_op jit(solution)/shard_map/pallas_call | solution.py:534
  34.7 5.1 %constant_dynamic-slice_fusion.3 = (bf16[4,768,384]{2,1,0:T(8,128)(2,1)}, bf16[4,768,384]{2,1,0:T(8,128)(2,1)}) fusion(bf16[8,768,384]{2,1,0:T(8,128)(2,1)} %param.21, s32[]{:T(128)S(6)} %select_n.71, s32[]{:T(128)S(6)} %select_n.68), kind=kLoop, calls=%fused_computation.161 | loop fusion | bytes 9437192 | tf_op jit(solution)/shard_map/dynamic_slice | solution.py:1098
  42.2 28.1 %shard_map.187 = (f32[256,768]{1,0:T(8,128)S(1)}, bf16[256,768]{1,0:T(8,128)(2,1)S(1)}, bf16[8,256,384]{2,1,0:T(8,128)(2,1)S(1)}, f32[8,32,256]{2,1,0:T(8,128)S(1)}) custom-call(bf16[256,192]{1,0:T(8,128)(2,1)S(1)} %copy.120.mixed, bf16[8,4,96,192]{3,2,1,0:T(8,128)(2,1)S(1)} %get-tuple-element.36.wo, bf16[256,768]{1,0:T(8,128)(2,1)S(1)} %bitcast.153, ...), custom_call_target="tpu_custom_call" | custom-call | tf_op jit(solution)/shard_map/pallas_call | solution.py:534
  70.4 5.6 %fusion.83 = bf16[4,2,128,384]{3,2,0,1:T(8,128)(2,1)S(1)} fusion(bf16[2,1024,384,1]{2,1,3,0:T(8,128)(2,1)S(1)} %bitcast.165, s32[2,4,1024]{2,1,0:T(4,128)S(1)} %fusion.92, pred[2,4,1024]{2,1,0:T(4,128)(4,1)S(1)} %get-tuple-element.100), kind=kOutput, calls=%fused_computation.86 | convolution fusion | flops 807796736 | bytes 2400256 | tf_op jit(solution)/shard_map/gest,gtd->egsd/dot_general | solution.py:1156
  76.2 2.2 fusion.64
  78.3 1.2 collective-permute-start
  80.4 1.0 copy.135
  81.3 1.5 copy.126.valid
  82.8 1.6 fusion.89
  85.7 0.9 copy.137
  86.7 5.9 %fusion.80 = bf16[4,2,128,384]{3,2,0,1:T(8,128)(2,1)S(1)} fusion(bf16[2,1024,384,1]{2,1,3,0:T(8,128)(2,1)} %bitcast.166, s32[2,4,1024]{2,1,0:T(4,128)} %fusion.89, pred[2,4,1024]{2,1,0:T(4,128)(4,1)} %get-tuple-element.101), kind=kOutput, calls=%fused_computation.85 | convolution fusion | flops 807796736 | bytes 2400256 | tf_op jit(solution)/shard_map/gest,gtd->egsd/dot_general | solution.py:1156
  92.7 1.0 copy.122
  93.8 1.9 multiply_convert_fusion.1
  95.8 4.6 %select_reduce_fusion = f32[2,4,128]{2,1,0:T(4,128)S(1)} fusion(f32[2,4,1024]{2,1,0:T(4,128)S(1)} %bitcast.201, s32[2,4,1024]{2,1,0:T(4,128)S(1)} %copy-done.20, pred[2,4,1024]{2,1,0:T(4,128)(4,1)S(1)} %copy-done.22), kind=kLoop, calls=%fused_computation.9 | loop fusion | flops 4193280 | bytes 77824 | tf_op jit(solution)/shard_map/reduce_sum | solution.py:1175
  100.4 15.5 %collective-permute-done = bf16[4,256,768]{2,1,0:T(8,128)(2,1)} collective-permute-done((bf16[4,256,768]{2,1,0:T(8,128)(2,1)}, bf16[4,256,768]{2,1,0:T(8,128)(2,1)}, u32[]{:S(2)}, u32[]{:S(2)}) %collective-permute-start) | collective-permute-done | bytes 1572896 | tf_op jit(solution)/shard_map/ppermute | solution.py:1045
  115.9 4.1 fusion.111
  119.9 7.2 %fusion.22 = bf16[4,256,768]{2,1,0:T(8,128)(2,1)S(1)} fusion(f32[4,256,768]{2,1,0:T(8,128)S(1)} %get-tuple-element.117, u8[256,768]{1,0:T(8,128)(4,1)S(1)} %get-tuple-element.97, u8[256,768]{1,0:T(8,128)(4,1)S(1)} %get-tuple-element.96), kind=kLoop, calls=%fused_computation.26 | loop fusion | flops 55050240 | bytes 5111808 | tf_op jit(solution)/shard_map/convert_element_type | solution.py:1178
  127.1 38.8 %collective-permute-done.1 = bf16[4,768,384]{2,1,0:T(8,128)(2,1)} collective-permute-done((bf16[4,768,384]{2,1,0:T(8,128)(2,1)}, bf16[4,768,384]{2,1,0:T(8,128)(2,1)}, u32[]{:S(2)}, u32[]{:S(2)}) %collective-permute-start.1) | collective-permute-done | bytes 2359328 | tf_op jit(solution)/shard_map/ppermute | solution.py:1045
  165.9 4.1 multiply_convert_fusion
  170.0 5.0 %bitcast_convert_fusion = bf16[2,1024,768]{2,1,0:T(8,128)(2,1)} fusion(s32[2,4,1024]{2,1,0:T(4,128)S(1)} %copy-done.20, pred[2,4,1024]{2,1,0:T(4,128)(4,1)S(1)} %copy-done.22, bf16[4,2,128,768]{3,2,1,0:T(8,128)(2,1)S(1)} %bitcast.212), kind=kOutput, calls=%fused_computation.2 | convolution fusion | flops 1614282752 | bytes 4759552 | tf_op jit(solution)/shard_map/gest,egsd->gtd/dot_general | solution.py:1161
  175.6 56.3 %shard_map.188 = (bf16[4,64,768]{2,1,0:T(8,128)(2,1)}, f32[64,768]{1,0:T(8,128)}, bf16[8,256,768]{2,1,0:T(8,128)(2,1)}, f32[4,8,128]{2,1,0:T(8,128)}) custom-call(bf16[8,256,768]{2,1,0:T(8,128)(2,1)} %bitcast.173, f32[256,768]{1,0:T(8,128)} %copy-done.1, bf16[256,768]{1,0:T(8,128)(2,1)} %bitcast.197, f32[256,1]{1,0:T(8,128)} %copy.126.valid, ...), custom_call_target="tpu_custom_call" | custom-call | tf_op jit(solution)/shard_map/pallas_call | solution.py:534
  231.9 6.0 %fusion.61 = f32[4,2,128,768]{3,2,0,1:T(8,128)S(1)} fusion(bf16[2,1024,768,1]{2,1,3,0:T(8,128)(2,1)} %bitcast.211, s32[2,4,1024]{2,1,0:T(4,128)S(1)} %copy-done.20, pred[2,4,1024]{2,1,0:T(4,128)(4,1)S(1)} %copy-done.22), kind=kOutput, calls=%fused_computation.76 | convolution fusion | flops 1612709888 | bytes 6332416 | tf_op jit(solution)/shard_map/gest,gtd->egsd/dot_general | solution.py:1156
  238.3 1.5 copy-done.13
  239.8 6.7 %fusion.27 = (bf16[4,256,768]{2,1,0:T(8,128)(2,1)}, f32[4,256]{1,0:T(4,128)S(1)}, bf16[4,256,768]{2,1,0:T(8,128)(2,1)S(1)}) fusion(f32[4,256,768]{2,1,0:T(8,128)S(1)} %get-tuple-element.117, f32[4,256]{1,0:T(4,128)S(1)} %bitcast.208, bf16[4,256,768]{2,1,0:T(8,128)(2,1)S(1)} %fusion.22, f32[4,2,128,768]{3,2,1,0:T(8,128)S(1)} %copy.128, ...), kind=kOutput, calls=%fused_computation.31 | convolution fusion | flops 1241775104 | bytes 17309696 | tf_op jit(solution)/shard_map/ecd,efd->ecf/dot_general | solution.py:1192
  246.5 1.2 collective-permute-start.2
  247.6 1.5 fusion.138
  249.1 3.7 copy-done.8
  252.8 1.7 dynamic-slice_convert_fusion
  256.0 4.8 %constant_dynamic-slice_fusion = f32[4,768,384]{2,1,0:T(8,128)} fusion(f32[4,768,768]{2,1,0:T(8,128)} %copy-done.8, s32[]{:T(128)S(6)} %select_n.81), kind=kLoop, calls=%fused_computation.158 | loop fusion | bytes 9437188 | tf_op jit(solution)/shard_map/dynamic_slice | solution.py:1201
  260.8 3.3 fusion.68
  264.1 2.7 fusion.7
  266.8 4.4 %fusion.139 = f32[4,384,768]{2,1,0:T(8,128)} fusion(bf16[4,256,384]{2,1,0:T(8,128)(2,1)S(1)} %bitcast.172, bf16[4,256,768]{2,1,0:T(8,128)(2,1)} %get-tuple-element.104), kind=kOutput, calls=%fused_computation.180 | convolution fusion | flops 603979776 | bytes 7077888 | tf_op jit(solution)/shard_map/ecd,ecf->edf/dot_general | solution.py:1207
  271.2 12.3 %collective-permute-done.2 = bf16[4,256,768]{2,1,0:T(8,128)(2,1)} collective-permute-done((bf16[4,256,768]{2,1,0:T(8,128)(2,1)}, bf16[4,256,768]{2,1,0:T(8,128)(2,1)}, u32[]{:S(2)}, u32[]{:S(2)}) %collective-permute-start.2) | collective-permute-done | bytes 1572896 | tf_op jit(solution)/shard_map/ppermute | solution.py:1045
  283.5 2.4 fusion.71
  286.0 3.9 fusion
  289.9 53.5 %shard_map.189 = (bf16[4,64,768]{2,1,0:T(8,128)(2,1)}, bf16[4,64,128]{2,1,0:T(8,128)(2,1)}, f32[64,768]{1,0:T(8,128)}, f32[8,768]{1,0:T(8,128)}) custom-call(bf16[8,256,512]{2,1,0:T(8,128)(2,1)} %bitcast.174, f32[256,768]{1,0:T(8,128)} %copy-done.1, f32[1,768]{1,0:T(1,128)} %copy-done.6, bf16[768,128]{1,0:T(8,128)(2,1)} %copy-done.2, ...), custom_call_target="tpu_custom_call" | custom-call | tf_op jit(solution)/shard_map/pallas_call | solution.py:534
  343.5 1.3 convolution_convert_fusion.4
  346.1 1.1 collective-permute-start.3
  349.0 1.1 convolution_convert_fusion.3
  351.2 61.1 %shard_map.190 = (f32[4,64,768]{2,1,0:T(8,128)S(1)}, f32[96,896]{1,0:T(8,128)S(1)}, f32[8,128]{1,0:T(8,128)S(1)}) custom-call(bf16[4,64,768]{2,1,0:T(8,128)(2,1)S(1)} %bitcast.156, bf16[8,96,896]{2,1,0:T(8,128)(2,1)S(1)} %pad_maximum_fusion.dense, bf16[256,768]{1,0:T(8,128)(2,1)S(1)} %bitcast.154, f32[1,768]{1,0:T(1,128)S(1)} %reshape.275.gain, ...), custom_call_target="tpu_custom_call" | custom-call | tf_op jit(solution)/shard_map/pallas_call | solution.py:534
  415.4 2.4 fusion.140
  417.8 9.1 %maximum_select_fusion = f32[8,384,768]{2,1,0:T(8,128)} fusion(f32[4,384,768]{2,1,0:T(8,128)S(1)} %fusion.140, f32[4,384,768]{2,1,0:T(8,128)} %fusion.139, pred[]{:T(512)S(6)} %eq.35), kind=kLoop, calls=%fused_computation | loop fusion | flops 7077888 | bytes 18874368 | tf_op jit(solution)/shard_map/jit(_where)/select_n | solution.py:1037
  426.9 2.0 convert_element_type.226
  428.9 4.1 maximum_select_fusion.1
  (153 shorter events, 21.4 us)
Async XLA Ops:
  3.3 36.5 %copy-start.32 = (s32[4]{0:T(128)}, s32[4]{0:T(128)S(1)}, u32[]{:S(2)}) copy-start(s32[4]{0:T(128)S(1)} %iota_add_fusion.1) | copy-start | bytes 52
  4.5 35.7 %copy-start.24 = (f32[256]{0:T(256)}, f32[256]{0:T(256)S(1)}, u32[]{:S(2)}) copy-start(f32[256]{0:T(256)S(1)} %broadcast_multiply_fusion) | copy-start | bytes 3076
  5.7 34.5 %copy-start.29 = (f32[256]{0:T(256)}, f32[256]{0:T(256)S(1)}, u32[]{:S(2)}) copy-start(f32[256]{0:T(256)S(1)} %add_rsqrt_fusion) | copy-start | bytes 3076
  33.5 6.7 %copy-start.3 = (bf16[8,96,768]{2,1,0:T(8,128)(2,1)}, bf16[8,96,768]{2,1,0:T(8,128)(2,1)S(1)}, u32[]{:S(2)}) copy-start(bf16[8,96,768]{2,1,0:T(8,128)(2,1)S(1)} %get-tuple-element.35) | copy-start | bytes 3538948
  34.4 36.0 %copy-start.27 = (pred[2,4,1024]{2,1,0:T(4,128)(4,1)}, pred[2,4,1024]{2,1,0:T(4,128)(4,1)S(1)}, u32[]{:S(2)}) copy-start(pred[2,4,1024]{2,1,0:T(4,128)(4,1)S(1)} %get-tuple-element.100) | copy-start | bytes 24580
  34.7 35.7 %copy-start.34 = (s32[2,4,1024]{2,1,0:T(4,128)}, s32[2,4,1024]{2,1,0:T(4,128)S(1)}, u32[]{:S(2)}) copy-start(s32[2,4,1024]{2,1,0:T(4,128)S(1)} %fusion.92) | copy-start | bytes 98308
  34.7 5.5 %copy-start = (bf16[1,256,768]{2,1,0:T(8,128)(2,1)S(1)}, bf16[1,256,768]{2,1,0:T(8,128)(2,1)}, u32[]{:S(2)}) copy-start(bf16[1,256,768]{2,1,0:T(8,128)(2,1)} %param.11) | copy-start | bytes 1179652
  40.1 2.0 copy-start.6
  40.2 2.0 copy-start.2
  40.8 0.7 copy-start.17
  41.2 0.9 copy-start.9
  42.2 34.0 %slice-start.2 = ((s8[4718592]{0:T(1024)(128)(4,1)}), s8[4194304]{0:T(1024)(128)(4,1)S(1)}, s32[]{:S(2)}) async-start(s8[4718592]{0:T(1024)(128)(4,1)} %bitcast.183), calls=%async_computation.2 | async-start | bytes 8388608
  70.4 5.7 %copy-start.1 = (f32[256,768]{1,0:T(8,128)}, f32[256,768]{1,0:T(8,128)S(1)}, u32[]{:S(2)}) copy-start(f32[256,768]{1,0:T(8,128)S(1)} %get-tuple-element.40.residual) | copy-start | bytes 2359300
  70.4 5.7 %copy-start.7 = (bf16[8,256,384]{2,1,0:T(8,128)(2,1)}, bf16[8,256,384]{2,1,0:T(8,128)(2,1)S(1)}, u32[]{:S(2)}) copy-start(bf16[8,256,384]{2,1,0:T(8,128)(2,1)S(1)} %get-tuple-element.37) | copy-start | bytes 4718596
  70.4 5.8 %slice-start.3 = ((s8[4718592]{0:T(1024)(128)(4,1)}), s8[524288]{0:T(1024)(128)(4,1)S(1)}, s32[]{:S(2)}) async-start(s8[4718592]{0:T(1024)(128)(4,1)} %bitcast.183), calls=%async_computation.3 | async-start | bytes 1048576
  78.3 37.5 %collective-permute-start = (bf16[4,256,768]{2,1,0:T(8,128)(2,1)}, bf16[4,256,768]{2,1,0:T(8,128)(2,1)}, u32[]{:S(2)}, u32[]{:S(2)}) collective-permute-start(bf16[4,256,768]{2,1,0:T(8,128)(2,1)} %fusion.64), channel_id=1, source_target_pairs={{0,16},{16,0},{1,17},{17,1},{2,18},{18,2},{3,19},{19,3},{4,20},{20... | collective-permute-start | bytes 4718600 | tf_op jit(solution)/shard_map/ppermute | solution.py:1045
  79.6 86.4 %collective-permute-start.1 = (bf16[4,768,384]{2,1,0:T(8,128)(2,1)}, bf16[4,768,384]{2,1,0:T(8,128)(2,1)}, u32[]{:S(2)}, u32[]{:S(2)}) collective-permute-start(bf16[4,768,384]{2,1,0:T(8,128)(2,1)} %get-tuple-element.38), channel_id=1, source_target_pairs={{0,16},{16,0},{1,17},{17,1},{2,18},{18,2},{3,19},{19,3},{4,20},{20... | collective-permute-start | bytes 7077896 | tf_op jit(solution)/shard_map/ppermute | solution.py:1045
  86.7 7.1 %copy-start.33 = (s32[4]{0:T(128)S(1)}, s32[4]{0:T(128)}, u32[]{:S(2)}) copy-start(s32[4]{0:T(128)} %copy-done.32) | copy-start | bytes 52
  86.7 7.2 %copy-start.25 = (f32[256]{0:T(256)S(1)}, f32[256]{0:T(256)}, u32[]{:S(2)}) copy-start(f32[256]{0:T(256)} %copy-done.24) | copy-start | bytes 3076
  86.7 7.2 %copy-start.30 = (f32[256]{0:T(256)S(1)}, f32[256]{0:T(256)}, u32[]{:S(2)}) copy-start(f32[256]{0:T(256)} %copy-done.29) | copy-start | bytes 3076
  92.6 3.2 copy-start.20
  92.6 3.1 copy-start.22
  119.9 46.0 %copy-start.12 = (bf16[4,768,384]{2,1,0:T(8,128)(2,1)S(1)}, bf16[4,768,384]{2,1,0:T(8,128)(2,1)}, u32[]{:S(2)}) copy-start(bf16[4,768,384]{2,1,0:T(8,128)(2,1)} %get-tuple-element.102) | copy-start | bytes 7077892
  238.1 1.7 copy-start.13
  246.5 37.1 %collective-permute-start.2 = (bf16[4,256,768]{2,1,0:T(8,128)(2,1)}, bf16[4,256,768]{2,1,0:T(8,128)(2,1)}, u32[]{:S(2)}, u32[]{:S(2)}) collective-permute-start(bf16[4,256,768]{2,1,0:T(8,128)(2,1)} %get-tuple-element.104), channel_id=1, source_target_pairs={{0,16},{16,0},{1,17},{17,1},{2,18},{18,2},{3,19},{19,3},{4,20},{20... | collective-permute-start | bytes 4718600 | tf_op jit(solution)/shard_map/ppermute | solution.py:1045
  249.1 3.7 copy-start.8
  252.8 1.7 copy-start.23
  260.8 3.3 copy-start.21
  260.8 22.8 %slice-start.4 = ((s8[4718592]{0:T(1024)(128)(4,1)}), s8[4194304]{0:T(1024)(128)(4,1)S(1)}, s32[]{:S(2)}) async-start(s8[4718592]{0:T(1024)(128)(4,1)} %bitcast.185), calls=%async_computation.4 | async-start | bytes 8388608
  264.0 2.7 copy-start.11
  264.0 19.5 %slice-start.5 = ((s8[4718592]{0:T(1024)(128)(4,1)}), s8[524288]{0:T(1024)(128)(4,1)S(1)}, s32[]{:S(2)}) async-start(s8[4718592]{0:T(1024)(128)(4,1)} %bitcast.185), calls=%async_computation.5 | async-start | bytes 1048576
  271.2 14.8 %copy-start.28 = (pred[2,4,1024]{2,1,0:T(4,128)(4,1)S(1)}, pred[2,4,1024]{2,1,0:T(4,128)(4,1)}, u32[]{:S(2)}) copy-start(pred[2,4,1024]{2,1,0:T(4,128)(4,1)} %copy-done.27) | copy-start | bytes 24580
  271.2 14.8 %copy-start.35 = (s32[2,4,1024]{2,1,0:T(4,128)S(1)}, s32[2,4,1024]{2,1,0:T(4,128)}, u32[]{:S(2)}) copy-start(s32[2,4,1024]{2,1,0:T(4,128)} %copy-done.34) | copy-start | bytes 98308
  289.9 54.8 %copy-start.10 = (f32[3,256,256]{1,2,0:T(8,128)S(1)}, f32[3,256,256]{1,2,0:T(8,128)}, u32[]{:S(2)}) copy-start(f32[3,256,256]{1,2,0:T(8,128)} %copy-done.9) | copy-start | bytes 2359300
  289.9 55.2 %copy-start.18 = (bf16[256,576]{0,1:T(8,128)(2,1)S(1)}, bf16[256,576]{0,1:T(8,128)(2,1)}, u32[]{:S(2)}) copy-start(bf16[256,576]{0,1:T(8,128)(2,1)} %copy-done.17) | copy-start | bytes 884740
  344.8 2.5 copy-start.4
  344.8 2.5 copy-start.26
  344.8 2.5 copy-start.31
  345.5 3.2 copy-start.15
  345.6 3.3 copy-start.14
  345.9 4.5 %copy-start.16 = (bf16[1,256,768]{1,2,0:T(8,128)(2,1)S(1)}, bf16[1,256,768]{1,2,0:T(8,128)(2,1)}, u32[]{:S(2)}) copy-start(bf16[1,256,768]{1,2,0:T(8,128)(2,1)} %multiply_convert_fusion.1) | copy-start | bytes 1179652
  346.1 80.8 %collective-permute-start.3 = (bf16[4,768,384]{2,1,0:T(8,128)(2,1)}, bf16[4,768,384]{2,1,0:T(8,128)(2,1)}, u32[]{:S(2)}, u32[]{:S(2)}) collective-permute-start(bf16[4,768,384]{2,1,0:T(8,128)(2,1)} %dynamic-slice_convert_fusion), channel_id=1, source_target_pairs={{0,16},{16,0},{1,17},{17,1},{2,18},{18,2},{3,19},{19,3},{4,20},{20... | collective-permute-start | bytes 7077896 | tf_op jit(solution)/shard_map/ppermute | solution.py:1045
  348.8 2.3 copy-start.5
  415.4 13.5 %slice-start = ((s8[4718592]{0:T(1024)(128)(4,1)}), s8[4194304]{0:T(1024)(128)(4,1)S(1)}, s32[]{:S(2)}) async-start(s8[4718592]{0:T(1024)(128)(4,1)} %bitcast.167), calls=%async_computation | async-start | bytes 8388608
  417.8 11.1 %slice-start.1 = ((s8[4718592]{0:T(1024)(128)(4,1)}), s8[524288]{0:T(1024)(128)(4,1)S(1)}, s32[]{:S(2)}) async-start(s8[4718592]{0:T(1024)(128)(4,1)} %bitcast.167), calls=%async_computation.1 | async-start | bytes 1048576
  428.9 4.1 copy-start.19

commit v2 on v1

--- a/solution.py
+++ b/solution.py
@@ -529,13 +529,28 @@
     return copies
 
 
-def remote_call(kernel, outs, ins, scratch, copies, collective_id, vmem_mib):
-    vmem = pl.BlockSpec(memory_space=pltpu.VMEM)
+def spends(microseconds):
+    return pl.CostEstimate(flops=0, bytes_accessed=microseconds * 3_000_000, transcendentals=0)
+
+
+def remote_call(
+    kernel,
+    outs,
+    ins,
+    scratch,
+    copies,
+    collective_id,
+    vmem_mib,
+    microseconds,
+    in_hbm=(),
+    out_hbm=(),
+):
+    vmem, hbm = pl.BlockSpec(memory_space=pltpu.VMEM), pl.BlockSpec(memory_space=pl.ANY)
     return pl.pallas_call(
         kernel,
         out_shape=outs,
-        in_specs=[vmem] * len(ins),
-        out_specs=[vmem] * len(outs),
+        in_specs=[hbm if i in in_hbm else vmem for i in range(len(ins))],
+        out_specs=[hbm if i in out_hbm else vmem for i in range(len(outs))],
         scratch_shapes=[
             *scratch,
             pltpu.SemaphoreType.DMA((copies,)),
@@ -546,6 +561,7 @@
             has_side_effects=True,
             vmem_limit_bytes=vmem_mib * 2**20,
         ),
+        cost_estimate=spends(microseconds),
     )(*ins)
 
 
@@ -613,21 +629,28 @@
         copies,
         1,
         32,
+        20,
     )
 
 
 def mix_kernel(
     heads,
     experts,
+    skip,
     mixed,
     wo,
     tokens,
     gain,
     router,
+    near_route,
+    far_route,
+    down,
     residual,
     second,
     group,
     probs,
+    slots,
+    arrived,
     everyone,
     other_half,
     ss,
@@ -639,6 +662,22 @@
     place.greet(place.plane_peers + place.z_peers)
     everyone[place.z] = mixed[...]
     along = all_heads(links, place, lambda k, z: (everyone.at[place.z], everyone.at[place.z]))
+    local_experts = slots.shape[0] // 2
+    ids = place.z * local_experts + lax.broadcasted_iota(jnp.int32, (local_experts, 1), 0)
+    first = place.f == 0
+    near, far = near_route[...], far_route[...]
+    both = [jnp.where(first, near, far), jnp.where(first, far, near)]
+    chosen = jnp.concatenate([(r[0:1] == ids) | (r[1:2] == ids) for r in both], 0)
+    count = chosen.astype(WIDE)
+    before = lax.broadcasted_iota(jnp.int32, (128, 128), 0)
+    before = (before < lax.broadcasted_iota(jnp.int32, (128, 128), 1)).astype(LOW)
+    running = jnp.zeros((2 * local_experts, 1), WIDE)
+    for b in range(slots.shape[1] // 128):
+        columns = slice(b * 128, (b + 1) * 128)
+        here = count[:, columns]
+        slot = dot(here.astype(LOW), before) + running
+        slots[:, columns] = jnp.where(chosen[:, columns], slot, -1.0).astype(jnp.int32)
+        running = running + jnp.sum(here, -1, keepdims=True)
     for copy in along:
         copy.wait_recv()
     rows_all, width = tokens.shape
@@ -659,10 +698,11 @@
 
     in_rows(rows_all, 64, norm)
     low, high = second[:, :half], second[:, half:]
-    first = place.f == 0
     group[me] = jnp.where(first, low, high)
     other_half[...] = jnp.where(first, high, low)
     x1 = links.send(other_half, group.at[me], place.x_peer)
+    theirs = pl.ds((1 - place.f) * (local_experts // 2) + skip, arrived.shape[0])
+    bulk = links.send(down.at[theirs], arrived, place.x_peer)
     y1 = links.send(group.at[me], group.at[me], place.y_peer)
     shared = [links.send(group.at[me], group.at[me], place.core_peer)]
     logits = lax.dot_general(
@@ -679,31 +719,106 @@
     shared.append(links.send(group.at[beside], group.at[beside], place.core_peer))
     y2.wait_recv()
     shared.append(links.send(group.at[corner], group.at[corner], place.core_peer))
-    for copy in shared + small:
+    for copy in shared + small + [bulk]:
         copy.wait_recv()
     links.drain()
 
 
-def mix_heads(heads, experts, mixed, wo, tokens, gain, router):
+def mix_heads(
+    heads, experts, skip, mixed, wo, tokens, gain, router, near_route, far_route, down
+):
     rows, width = tokens.shape
+    late = down.shape[0] // 2 - skip
     return remote_call(
-        functools.partial(mix_kernel, heads, experts),
+        functools.partial(mix_kernel, heads, experts, skip),
         [
             shape((rows, width), WIDE),
             shape((rows, width)),
             shape((8, rows, width // 2)),
             shape((8, experts, rows), WIDE),
+            shape((2 * experts // heads, near_route.shape[1]), jnp.int32),
+            shape((late, *down.shape[1:])),
         ],
-        [mixed, wo, tokens, gain, router],
+        [mixed, wo, tokens, gain, router, near_route, far_route, down],
         [pltpu.VMEM((heads, *mixed.shape), LOW), pltpu.VMEM((rows, width // 2), LOW)],
-        heads - 1 + 7 + 7,
+        heads - 1 + 7 + 8,
         2,
         48,
-    )
+        26,
+        in_hbm=(7,),
+        out_hbm=(5,),
+    )
+
+
+class ChunkSum:
+    def __init__(self, links, place, part, columns, core_in, xa, ya, yb, xb):
+        self.links, self.place, self.part, self.columns = links, place, part, columns
+        self.core_in, self.xa, self.ya, self.yb, self.xb = core_in, xa, ya, yb, xb
+        self.rows, self.half = core_in.shape[2], core_in.shape[3] // 2
+        self.a, self.b = pl.ds(0, self.half), pl.ds(self.half, self.half)
+
+    def start(self):
+        p = self.place
+        self.into = self.links.send(
+            self.part.at[:, :, 1 - p.c, :, self.columns], self.core_in, p.core_peer
+        )
+
+    def cores(self):
+        p, rc = self.place, self.core_in
+        self.into.wait_recv()
+
+        def add(rows):
+            here = self.part[:, :, p.c, rows, self.columns].astype(WIDE)
+            rc[:, :, rows, :] = (rc[:, :, rows, :].astype(WIDE) + here).astype(LOW)
+
+        in_rows(self.rows, 32, add)
+        self.to_x = self.links.send(rc.at[1 - p.f, :, :, self.a], self.xa, p.x_peer)
+        self.to_y = self.links.send(rc.at[:, 1 - p.y, :, self.b], self.yb, p.y_peer)
+
+    def cross(self):
+        p, rc, xa, yb = self.place, self.core_in, self.xa, self.yb
+        self.to_x.wait_recv()
+        y, f = 1 - p.y, 1 - p.f
+
+        def add_a(rows):
+            both = xa[y, rows, :].astype(WIDE) + rc[p.f, y, rows, self.a].astype(WIDE)
+            xa[y, rows, :] = both.astype(LOW)
+
+        in_rows(self.rows, 64, add_a)
+        self.last_a = self.links.send(xa.at[y], self.ya, p.y_peer)
+        self.to_y.wait_recv()
+
+        def add_b(rows):
+            both = yb[f, rows, :].astype(WIDE) + rc[f, p.y, rows, self.b].astype(WIDE)
+            yb[f, rows, :] = both.astype(LOW)
+
+        in_rows(self.rows, 64, add_b)
+        self.last_b = self.links.send(yb.at[f], self.xb, p.x_peer)
+
+    def finish(self, take):
+        p, rc = self.place, self.core_in
+        self.last_a.wait_recv()
+        self.last_b.wait_recv()
+
+        def add(rows):
+            first = rc[p.f, p.y, rows, self.a].astype(WIDE) + self.xa[p.y, rows, :].astype(WIDE)
+            second = rc[p.f, p.y, rows, self.b].astype(WIDE) + self.yb[p.f, rows, :].astype(WIDE)
+            take(rows, 0, first + self.ya[rows, :].astype(WIDE))
+            take(rows, 1, second + self.xb[rows, :].astype(WIDE))
+
+        in_rows(self.rows, 64, add)
+
+
+def skewed(chunks, stages):
+    for step in range(chunks + len(stages) - 1):
+        for k in range(chunks):
+            if 0 <= step - k < len(stages):
+                stages[step - k](k)
 
 
 def combine_kernel(
     heads,
+    chunks,
     part,
     residual,
     teacher,
@@ -730,47 +845,94 @@
     place.greet(place.axis_peers() + place.z_peers)
     rows_all, width = residual.shape
     own = rows_all // heads
-    adder = PlaneSum(links, place, part, core_in, xa, ya, yb, xb, width // 2, 32)
-    adder.start()
-    adder.cores()
-    adder.cross()
-
-    def keep(rows, columns, values):
-        image_sum[rows, columns] = values.astype(LOW)
-
-    adder.finish(keep)
-    along = all_heads(
-        links,
-        place,
-        lambda k, to: (image_sum.at[pl.ds(pl.multiple_of(to * own, own), own)], far.at[k]),
-    )
-    for copy in along:
-        copy.wait_recv()
+    wide = width // chunks
+    half = wide // 2
     mine = pl.ds(pl.multiple_of(z * own, own), own)
-    total = image_sum[mine, :].astype(WIDE)
-    for k in range(heads - 1):
-        total = total + far[k].astype(WIDE)
-    final = residual[mine, :] + total
-    result[z] = final.astype(LOW)
-    error = (final - teacher[mine, :].astype(WIDE)) * valid[mine, :]
-    grad = error * scale[0:1, 0:1]
-    final_grad[...] = grad
-    group[me, mine, :] = grad.astype(LOW)
-    along = all_heads(links, place, lambda k, to: (group.at[me, mine], group.at[me, mine]))
-    squares = jnp.sum((error * error).reshape(own // 8, 8, width), axis=0)
-    loss[z] = sum(squares[:, i * 128 : (i + 1) * 128] for i in range(width // 128))
+    columns = [pl.ds(k * wide, wide) for k in range(chunks)]
+    adders = [
+        ChunkSum(
+            links,
+            place,
+            part,
+            columns[k],
+            core_in.at[k],
+            xa.at[k],
+            ya.at[k],
+            yb.at[k],
+            xb.at[k],
+        )
+        for k in range(chunks)
+    ]
+    for adder in adders:
+        adder.start()
+    along, spread, squares = {}, {}, []
+    gathers = [
+        PlaneGather(
+            links,
+            place,
+            lambda i, k=k: group.at[i, :, pl.ds(k * wide, half)],
+            lambda i, k=k: group.at[i, :, pl.ds(k * wide + half, half)],
+            lambda i, k=k: group.at[i, :, columns[k]],
+        )
+        for k in range(chunks)
+    ]
+
+    def to_heads(k):
+        def keep(rows, part_of, values):
+            image_sum[k, rows, pl.ds(part_of * half, half)] = values.astype(LOW)
+
+        adders[k].finish(keep)
+        along[k] = all_heads(
+            links,
+            place,
+            lambda n, to: (
+                image_sum.at[k, pl.ds(pl.multiple_of(to * own, own), own)],
+                far.at[k, n],
+            ),
+        )
+
+    def final(k):
+        for copy in along[k]:
+            copy.wait_recv()
+        total = image_sum[k, mine, :].astype(WIDE)
+        for n in range(heads - 1):
+            total = total + far[k, n].astype(WIDE)
+        values = residual[mine, columns[k]] + total
+        result[z, :, columns[k]] = values.astype(LOW)
+        error = (values - teacher[mine, columns[k]].astype(WIDE)) * valid[mine, :]
+        grad = error * scale[0:1, 0:1]
+        final_grad[:, columns[k]] = grad
+        group[me, mine, columns[k]] = grad.astype(LOW)
+        block = group.at[me, mine, columns[k]]
+        spread[k] = all_heads(links, place, lambda n, to: (block, block))
+        square = jnp.sum((error * error).reshape(own // 8, 8, wide), axis=0)
+        squares.extend(square[:, i * 128 : (i + 1) * 128] for i in range(wide // 128))
+
+    def to_plane(k):
+        for copy in spread[k]:
+            copy.wait_recv()
+        gathers[k].start()
+
+    def forward(k):
+        gathers[k].forward()
+        gathers[k].share()
+
+    skewed(
+        chunks,
+        [
+            lambda k: adders[k].cores(),
+            lambda k: adders[k].cross(),
+            to_heads,
+            final,
+            to_plane,
+            forward,
+        ],
+    )
+    loss[z] = sum(squares)
     extra = all_heads(links, place, lambda k, to: (result.at[z], result.at[z]))
     extra += all_heads(links, place, lambda k, to: (loss.at[z], loss.at[z]))
-    for copy in along:
-        copy.wait_recv()
-    half = width // 2
-    PlaneGather(
-        links,
-        place,
-        lambda i: group.at[i, :, pl.ds(0, half)],
-        lambda i: group.at[i, :, pl.ds(half, half)],
-        lambda i: group.at[i],
-    ).run()
+    for gather in gathers:
+        gather.finish()
     for copy in extra:
         copy.wait_recv()
     links.drain()
@@ -779,8 +941,9 @@
 def combine(heads, part, residual, teacher, valid, scale):
     rows, width = residual.shape
     own = rows // heads
+    chunks = width // 256
     return remote_call(
-        functools.partial(combine_kernel, heads),
+        functools.partial(combine_kernel, heads, chunks),
         [
             shape((heads, own, width)),
             shape((own, width), WIDE),
@@ -789,23 +952,31 @@
         ],
         [part, residual, teacher, valid, scale],
         [
-            *sum_scratch(rows, width, width // 2),
-            pltpu.VMEM((rows, width), LOW),
-            pltpu.VMEM((heads - 1, own, width), LOW),
+            pltpu.VMEM((chunks, 2, 2, rows, 256), LOW),
+            pltpu.VMEM((chunks, 2, rows, 128), LOW),
+            pltpu.VMEM((chunks, rows, 128), LOW),
+            pltpu.VMEM((chunks, 2, rows, 128), LOW),
+            pltpu.VMEM((chunks, rows, 128), LOW),
+            pltpu.VMEM((chunks, rows, 256), LOW),
+            pltpu.VMEM((chunks, heads - 1, own, 256), LOW),
         ],
-        GATHER_COPIES + SUM_COPIES + 4 * (heads - 1),
+        chunks * (5 + GATHER_COPIES + 2 * (heads - 1)) + 2 * (heads - 1),
         3,
-        56,
+        28,
+        50,
     )
 
 
 def back_kernel(
     heads,
-    experts,
+    chunks,
     part,
+    gates_a,
+    gates_b,
     residual,
     gain,
     router,
+    probs,
     final_grad,
     attended,
     logit_grads,
@@ -816,82 +987,111 @@
     far,
     pair,
     x_in,
+    gate_own,
+    gate_in,
+    gate_sum,
+    gate_all,
+    logit_rows,
     ss,
     rs,
 ):
     place = Place(heads)
     links = Links(ss, rs)
     f, y, z = place.f, place.y, place.z
-    place.greet(place.axis_peers() + place.z_peers)
+    t = 2 * y + place.c
+    tensor_peers = [{TENSOR: lax.rem(t + k, 4)} for k in range(1, 4)]
+    owners = [
+        {FSDP: 1 - f if a else f, HEADS: lax.rem(z + k, heads)}
+        for k in range(heads)
+        for a in range(2)
+        if a or k
+    ]
+    place.greet(tensor_peers + owners)
     rows_all, width = residual.shape
     half = width // 2
     own = rows_all // heads
-    into = {}
-    for dy in (1, 0):
-        for df in (1, 0):
-            slot = 2 * (1 - f if df else f) + (1 - y if dy else y)
-            into[df, dy] = links.send(
-                part.at[place.image(df, dy, 1)], core_in.at[slot], place.core_peer
-            )
-    beside = {}
-    for dy in (1, 0):
-        for df in (1, 0):
-            to = 1 - f if df else f
-            slot = 2 * to + (1 - y if dy else y)
-            mine = place.image(df, dy, 0)
-            into[df, dy].wait_recv()
-
-            def add(rows, slot=slot, mine=mine):
-                both = core_in[slot, rows, :].astype(WIDE) + part[mine, rows, :].astype(WIDE)
-                core_in[slot, rows, :] = both.astype(LOW)
-
-            in_rows(rows_all, 32, add)
-            if dy:
-                beside[df] = links.send(core_in.at[slot], y_in.at[to], place.y_peer)
-    for df in (1, 0):
-        to = 1 - f if df else f
-        slot = 2 * to + y
-        beside[df].wait_recv()
-
-        def add_y(rows, slot=slot, to=to):
-            both = core_in[slot, rows, :].astype(WIDE) + y_in[to, rows, :].astype(WIDE)
-            y_in[to, rows, :] = both.astype(LOW)
-
-        in_rows(rows_all, 32, add_y)
-    along = all_heads(
-        links,
-        place,
-        lambda k, to: (y_in.at[:, pl.ds(pl.multiple_of(to * own, own), own)], far.at[k]),
-    )
+    into, beside, along, cross = {}, {}, {}, {}
+    for k in range(chunks):
+        source = part.at[:, :, 1 - place.c, :, pl.ds(k * 128, 128)]
+        into[k] = links.send(source, core_in.at[k], place.core_peer)
+    cut = gates_a.shape[1]
+    gate_own[:, :cut] = gates_a[...]
+    gate_own[:, cut:] = gates_b[...]
+    gate_in[t] = gate_own[...]
+    shared = [links.send(gate_own, gate_in.at[t], d) for d in tensor_peers]
     mine = pl.ds(pl.multiple_of(z * own, own), own)
-    normed, spread = normalize(residual[mine, :])
-    second_in = (normed * gain[...]).astype(LOW)
-    logits = jnp.dot(second_in, router[...], preferred_element_type=WIDE)
-    lanes = lax.broadcasted_iota(jnp.int32, logits.shape, 1)
-    logits = jnp.where(lanes < experts, logits, MASKED)
-    powers = jnp.exp(logits - jnp.max(logits, -1, keepdims=True))
-    probs = powers / jnp.sum(powers, -1, keepdims=True)
-    for copy in along:
+
+    def to_y(k):
+        into[k].wait_recv()
+        rc = core_in.at[k]
+
+        def add(rows):
+            here = part[:, :, place.c, rows, pl.ds(k * 128, 128)].astype(WIDE)
+            rc[:, :, rows, :] = (rc[:, :, rows, :].astype(WIDE) + here).astype(LOW)
+
+        in_rows(rows_all, 32, add)
+        beside[k] = links.send(rc.at[:, 1 - y], y_in.at[k], place.y_peer)
+
+    def to_heads(k):
+        beside[k].wait_recv()
+
+        def add(rows):
+            both = y_in[k, :, rows, :].astype(WIDE) + core_in[k, :, y, rows, :].astype(WIDE)
+            y_in[k, :, rows, :] = both.astype(LOW)
+
+        in_rows(rows_all, 64, add)
+        along[k] = all_heads(
+            links,
+            place,
+            lambda n, to: (
+                y_in.at[k, :, pl.ds(pl.multiple_of(to * own, own), own)],
+                far.at[k, n],
+            ),
+        )
+
+    def to_x(k):
+        for copy in along[k]:
+            copy.wait_recv()
+        total = y_in[k, :, mine, :].astype(WIDE)
+        for n in range(heads - 1):
+            total = total + far[k, n].astype(WIDE)
+        pair[k] = total.astype(LOW)
+        cross[k] = links.send(pair.at[k, 1 - f], x_in.at[k], place.x_peer)
+
+    to_y(0)
+    for copy in shared:
         copy.wait_recv()
-    for index in (1 - f, f):
-        total = y_in[index, mine, :].astype(WIDE)
-        for k in range(heads - 1):
-            total = total + far[k, index].astype(WIDE)
-        pair[index] = total.astype(LOW)
-    cross = links.send(pair.at[1 - f], x_in, place.x_peer)
-    near = pair[f].astype(WIDE)
-    cross.wait_recv()
-    away = x_in[...].astype(WIDE)
-    prob_grad = near[:, half:] + away[:, half:]
-    low, high = near[:, :half], away[:, :half]
+    gate_sum[...] = sum(gate_in[k] for k in range(4))
+    kept = gate_sum.shape[1]
+    rows_of = pl.ds(pl.multiple_of(t * rows_all, rows_all), rows_all)
+    gate_all[z, f] = gate_sum[f, :, rows_of]
+    spread = [
+        links.send(gate_sum.at[d[FSDP], :, rows_of], gate_all.at[z, f], d) for d in owners
+    ]
+    to_y(1)
+    to_heads(0)
+    for k in range(2, chunks):
+        to_y(k)
+        to_heads(k - 1)
+        to_x(k - 2)
+    for copy in spread:
+        copy.wait_recv()
+    chances = probs[...]
+    prob_grad = gate_all[...].reshape(2 * heads * kept, rows_all)
+    logit_grad = chances * (prob_grad - jnp.sum(chances * prob_grad, 0, keepdims=True))
+    logit_grads[...] = logit_grad.astype(LOW)
+    logit_rows[...] = dot(logit_grads[...], router[...], (0, 0))
+    normed, spread_two = normalize(residual[mine, :])
+    to_heads(chunks - 1)
+    to_x(chunks - 2)
+    to_x(chunks - 1)
+    near = jnp.concatenate([pair[k, f].astype(WIDE) for k in range(chunks)], 1)
+    for k in range(chunks):
+        cross[k].wait_recv()
+    away = jnp.concatenate([x_in[k].astype(WIDE) for k in range(chunks)], 1)
     first = f == 0
-    rows_grad = jnp.concatenate([jnp.where(first, low, high), jnp.where(first, high, low)], 1)
-    inner = jnp.sum(probs * prob_grad, -1, keepdims=True)
-    logit_grad = (probs * (prob_grad - inner)).astype(LOW)
-    logit_grads[z] = logit_grad
-    second_grad = rows_grad + lax.dot_general(
-        logit_grad, router[...], (((1,), (1,)), ((), ())), preferred_element_type=WIDE
-    )
+    rows_grad = jnp.concatenate([jnp.where(first, near, away), jnp.where(first, away, near)], 1)
+    second_grad = rows_grad + logit_rows[mine, :]
     weighted = second_grad * gain[...]
     gain_part[...] = jnp.sum((second_grad * normed).reshape(own // 8, 8, width), axis=0)
     inner = (
@@ -899,39 +1099,45 @@
         - jnp.mean(weighted, -1, keepdims=True)
         - normed * jnp.mean(weighted * normed, -1, keepdims=True)
     )
-    total_grad = final_grad[...] + inner * spread
+    total_grad = final_grad[...] + inner * spread_two
     residual_grad[...] = total_grad
     attended[z] = total_grad.astype(LOW)
-    along = all_heads(links, place, lambda k, to: (attended.at[z], attended.at[z]))
-    along += all_heads(links, place, lambda k, to: (logit_grads.at[z], logit_grads.at[z]))
-    for copy in along:
+    for copy in all_heads(links, place, lambda k, to: (attended.at[z], attended.at[z])):
         copy.wait_recv()
     links.drain()
 
 
-def back_through_norm(heads, experts, part, residual, gain, router, final_grad):
+def back_through_norm(heads, part, gates_a, gates_b, residual, gain, router, probs, final_grad):
     rows, width = residual.shape
     own = rows // heads
-    wide = part.shape[2]
+    chunks = width // 256
+    kept = gates_a.shape[1] + gates_b.shape[1]
+    group_rows = gates_a.shape[2]
     return remote_call(
-        functools.partial(back_kernel, heads, experts),
+        functools.partial(back_kernel, heads, chunks),
         [
             shape((heads, own, width)),
-            shape((heads, own, 128)),
+            shape(probs.shape),
             shape((own, width), WIDE),
             shape((8, width), WIDE),
         ],
-        [part, residual, gain, router, final_grad],
+        [part, gates_a, gates_b, residual, gain, router, probs, final_grad],
         [
-            pltpu.VMEM((4, rows, wide), LOW),
-            pltpu.VMEM((2, rows, wide), LOW),
-            pltpu.VMEM((heads - 1, 2, own, wide), LOW),
-            pltpu.VMEM((2, own, wide), LOW),
-            pltpu.VMEM((own, wide), LOW),
+            pltpu.VMEM((chunks, 2, 2, rows, 128), LOW),
+            pltpu.VMEM((chunks, 2, rows, 128), LOW),
+            pltpu.VMEM((chunks, heads - 1, 2, own, 128), LOW),
+            pltpu.VMEM((chunks, 2, own, 128), LOW),
+            pltpu.VMEM((chunks, own, 128), LOW),
+            pltpu.VMEM((2, kept, group_rows), WIDE),
+            pltpu.VMEM((4, 2, kept, group_rows), WIDE),
+            pltpu.VMEM((2, kept, group_rows), WIDE),
+            pltpu.VMEM((heads, 2, kept, rows), WIDE),
+            pltpu.VMEM((rows, width), WIDE),
         ],
-        4 + 2 + 1 + 3 * (heads - 1),
+        chunks * (3 + heads - 1) + 3 + 2 * heads - 1 + heads - 1,
         4,
-        56,
+        20,
+        40,
     )
 
 
@@ -1030,15 +1236,169 @@
         SUM_COPIES + 3 * (heads - 1) + 7,
         5,
         48,
-    )
-
-
-def by_index(index, own, other, axis):
-    return jnp.where(
-        index == 0,
-        jnp.concatenate([own, other], axis),
-        jnp.concatenate([other, own], axis),
-    )
+        25,
+    )
+
+
+def local_call(
+    kernel, grid, scalars, ins, outs, scratch=(), vmem_mib=28, aliases=None, microseconds=5
+):
+    def spec(array, block, index):
+        if block is None:
+            dims = array.shape
+            return pl.BlockSpec(dims, lambda i, s, n=len(dims): (0,) * n)
+        if block is pl.ANY:
+            return pl.BlockSpec(memory_space=pl.ANY)
+        return pl.BlockSpec(block, index)
+
+    return pl.pallas_call(
+        kernel,
+        out_shape=[o[0] for o in outs],
+        grid_spec=pltpu.PrefetchScalarGridSpec(
+            num_scalar_prefetch=1,
+            grid=(grid,),
+            in_specs=[spec(*a) for a in ins],
+            out_specs=[spec(*o) for o in outs],
+            scratch_shapes=list(scratch),
+        ),
+        input_output_aliases=aliases or {},
+        compiler_params=pltpu.CompilerParams(vmem_limit_bytes=vmem_mib * 2**20),
+        cost_estimate=spends(microseconds),
+    )(scalars, *[a[0] for a in ins])
+
+
+def per_expert(dims, skip=0):
+    return (1, *dims), lambda i, s: (i + skip, 0, 0)
+
+
+def held_expert(dims, which, skip=0):
+    return (1, *dims), lambda i, s: (s[which] + i + skip, 0, 0)
+
+
+def slot_block(dims, skip=0):
+    return (2, *dims), lambda i, s: (0, i + skip, 0)
+
+
+def dot(a, b, over=(1, 0)):
+    return lax.dot_general(a, b, (((over[0],), (over[1],)), ((), ())), preferred_element_type=WIDE)
+
+
+def one_hot(slots, row, capacity):
+    places = lax.broadcasted_iota(jnp.int32, (capacity, slots.shape[1]), 0)
+    return places == slots[pl.ds(row, 1), :]
+
+
+def far_up_kernel(skip, s, slots, x, up, pick, buffer, away):
+    i, local_experts = pl.program_id(0) + skip, slots.shape[0] // 2
+    capacity = pick.shape[1]
+    for g in range(2):
+        hot = one_hot(slots, g * local_experts + s[1] + i, capacity).astype(LOW)
+        pick[g] = hot
+        buffer[0, pl.ds(g * capacity, capacity), :] = dot(hot, x[g]).astype(LOW)
+    away[0] = dot(buffer[0], up[0]).astype(LOW)
+
+
+def near_up_kernel(s, slots, x, up, probs, pick, buffer, own, gates):
+    i, local_experts = pl.program_id(0), slots.shape[0] // 2
+    capacity = pick.shape[1]
+    expert = s[3] + i
+    for g in range(2):
+        hot = one_hot(slots, g * local_experts + s[0] + i, capacity)
+        chances = jnp.concatenate([probs[4 * g + k, pl.ds(expert, 1), :] for k in range(4)], 1)
+        rows = pl.ds(g * capacity, capacity)
+        gates[0, rows, :] = jnp.sum(jnp.where(hot, chances, 0.0), -1, keepdims=True)
+        pick[g] = hot.astype(LOW)
+        buffer[0, rows, :] = dot(hot.astype(LOW), x[g]).astype(LOW)
+    own[0] = dot(buffer[0], up[0])
+
+
+def down_kernel(last, s, own, arrived, gates, near, far, *refs):
+    if last:
+        before, pick, hidden, slope, part, weighted = refs
+    else:
+        hidden, slope, weighted = refs
+    i = pl.program_id(0)
+    half = near.shape[2]
+    capacity = own.shape[1] // 2
+    values = own[0] + arrived[0].astype(WIDE)
+    cdf = 0.5 * (1.0 + lax.erf(values * ROOT_HALF))
+    hidden[0] = (values * cdf).astype(LOW)
+    slope[0] = cdf + values * DENSITY * jnp.exp(-0.5 * values * values)
+    for weight, f in ((near, s[2]), (far, 1 - s[2])):
+        out = (dot(hidden[0], weight[0]) * gates[0]).astype(LOW)
+        columns = pl.ds(pl.multiple_of(f * half, half), half)
+        for g in range(2):
+            rows = pl.ds(pl.multiple_of(i * capacity, capacity), capacity)
+            weighted[g, rows, columns] = out[g * capacity : (g + 1) * capacity]
+
+    if last:
+
+        @pl.when(i == pl.num_programs(0) - 1)
+        def _():
+            cut = before.shape[1]
+            for g in range(2):
+                total = dot(pick[g, :cut], before[g], (0, 0))
+                part[g] = (total + dot(pick[g, cut:], weighted[g], (0, 0))).astype(LOW)
+
+
+def hidden_back_kernel(
+    s, pick, grads, near, far, hidden, slope, gates, pre, out_grad, gate_rows, rows
+):
+    i = pl.program_id(0)
+    half = near.shape[2]
+    capacity = pick.shape[1]
+    for g in range(2):
+        rows[pl.ds(g * capacity, capacity), :] = dot(pick[g], grads[g]).astype(LOW)
+    first = pl.ds(pl.multiple_of(s[2] * half, half), half)
+    second = pl.ds(pl.multiple_of((1 - s[2]) * half, half), half)
+    raw = dot(rows[:, first], near[0], (1, 1)) + dot(rows[:, second], far[0], (1, 1))
+    pre[0] = (raw * gates[0] * slope[0]).astype(LOW)
+    out_grad[0] = (rows[...].astype(WIDE) * gates[0]).astype(LOW)
+    gate_grad = jnp.sum(raw * hidden[0].astype(WIDE), -1, keepdims=True)
+    for g in range(2):
+        terms = gate_grad[g * capacity : (g + 1) * capacity] * pick[g].astype(WIDE)
+        gate_rows[g, pl.ds(i, 1), :] = jnp.sum(terms, 0, keepdims=True)
+
+
+def down_grad_kernel(s, hidden, out_grad, *refs):
+    kept_grad, sent_grad = refs[-2:]
+    half = kept_grad.shape[2]
+    first = pl.ds(pl.multiple_of(s[2] * half, half), half)
+    second = pl.ds(pl.multiple_of((1 - s[2]) * half, half), half)
+    kept_grad[0] = dot(hidden[0], out_grad[0, :, first], (0, 0))
+    sent_grad[0] = dot(hidden[0], out_grad[0, :, second], (0, 0)).astype(LOW)
+
+
+def up_back_kernel(s, buffer, pre, up, *refs):
+    grad, rows_out = refs[-2:]
+    capacity = rows_out.shape[1]
+    grad[0] = dot(buffer[0], pre[0], (0, 0))
+    back = dot(pre[0], up[0], (1, 1)).astype(LOW)
+    for g in range(2):
+        rows_out[g] = back[g * capacity : (g + 1) * capacity]
+
+
+def far_up_last_kernel(s, buffer, pre, up, rows_near, before, pick_near, pick_far, held, grad, part, rows_far):
+    i = pl.program_id(0)
+    capacity = buffer.shape[1] // 2
+    grad[0] = dot(buffer[0], pre[0], (0, 0))
+    back = dot(pre[0], up[0], (1, 1)).astype(LOW)
+    for g in range(2):
+        rows = pl.ds(pl.multiple_of(i * capacity, capacity), capacity)
+        rows_far[g, rows, :] = back[g * capacity : (g + 1) * capacity]
+
+    @pl.when(i == pl.num_programs(0) - 1)
+    def _():
+        cut = before.shape[1]
+        for g in range(2):
+            near = dot(pick_near[g], rows_near[g], (0, 0))
+            far = dot(pick_far[g, :cut], before[g], (0, 0))
+            far = far + dot(pick_far[g, cut:], rows_far[g], (0, 0))
+            part[g] = (near + far).astype(LOW)
+
+
+def widen_kernel(s, arrived, held, grad):
+    grad[0] = arrived[0].astype(WIDE)
 
 
 def swap(values):
@@ -1073,6 +1433,10 @@
 
     mine, theirs = f * kept, (1 - f) * kept
     half = width // 2
+    first_chunk, second_chunk = kept // 4, kept // 2
+    down_a = lax.dynamic_slice_in_dim(expert_down, theirs, first_chunk, 0)
+    down_a, qkv_weight = lax.optimization_barrier((down_a, qkv_weight))
+    down_a = swap(down_a)
 
     qkv_width = head_count * qkv_dim
     pad = -(128 + qkv_width) % 256
@@ -1090,12 +1454,12 @@
     wo = out_weight.reshape(head_count * head_dim, block).T
     count = jnp.full((8, 128), jnp.sum(valid_mask), jnp.int32)
     near_route = jnp.pad(routes.reshape(group_rows, -1).T, ((0, 8 - routes.shape[2]), (0, 0)))
+    count, down_a = lax.optimization_barrier((count, down_a))
     gathered, wo_all, counts, far_route = gather_weights_fast(heads, wq, wo, count, near_route)
-    gathered, down_away = lax.optimization_barrier(
-        (gathered, lax.dynamic_slice_in_dim(expert_down, theirs, kept, 0))
-    )
-    down_far = swap(down_away)
-    down_near = lax.dynamic_slice_in_dim(expert_down, mine, kept, 0)
+    gathered, down_b = lax.optimization_barrier(
+        (gathered, lax.dynamic_slice_in_dim(expert_down, theirs + first_chunk, second_chunk, 0))
+    )
+    down_b = swap(down_b)
     gathered = gathered.reshape(width, -1)
     qkv_full = gathered[:, 128 : 128 + qkv_width]
     lanes = jnp.arange(128)
@@ -1132,97 +1496,236 @@
         .astype(LOW)
         .reshape(rows, head_count * head_dim)
     )
-    residual, second_in, group_in, probs_all = mix_heads(
-        heads, expert_count, mixed, wo_all, tokens[0], gain_b, router_wide
-    )
-
-    both = by_index(f, near_route[None], far_route[None], 0)[:, : routes.shape[2]]
+    residual, second_in, group_in, probs_all, slots, down_c = mix_heads(
+        heads,
+        expert_count,
+        first_chunk + second_chunk,
+        mixed,
+        wo_all,
+        tokens[0],
+        gain_b,
+        router_wide,
+        near_route,
+        far_route,
+        expert_down,
+    )
+    group_in, down_b = lax.optimization_barrier((group_in, down_b))
+
+    hidden_width = expert_up.shape[2]
+    pair = 2 * capacity
+    scalars = jnp.stack([mine, theirs, f, z * local_experts + mine]).astype(jnp.int32)
     rows_in = group_in.reshape(2, group_rows, half)
-    probs_all = probs_all.reshape(2, 4, expert_count, rows)
-    order = jnp.arange(group_rows, dtype=jnp.int32)
-    earlier = (order[:, None] < order[None, :]).astype(LOW)
-
-    def picks(start):
-        ids = z * local_experts + start + jnp.arange(kept, dtype=jnp.int32)
-        chosen = jnp.any(both[:, None] == ids[None, :, None, None], 2)
-        slot = jnp.einsum(
-            "get,tu->geu", chosen.astype(LOW), earlier, preferred_element_type=WIDE
-        ).astype(jnp.int32)
-        return chosen[:, :, None, :] & (
-            slot[:, :, None, :] == jnp.arange(capacity, dtype=jnp.int32)[None, None, :, None]
+    a_pick = shape((2, kept * capacity, group_rows)), *slot_block((capacity, group_rows))
+    a_buffer = shape((kept, pair, half)), *per_expert((pair, half))
+    near_up = expert_up, *held_expert((half, hidden_width), 0)
+    part_size = kept // 2
+    a_hidden = per_expert((pair, hidden_width))
+    halves = (0, part_size)
+    picks_far, buffers_far, arrived = [], [], []
+    for skip in halves:
+        pick, buffer, away = local_call(
+            functools.partial(far_up_kernel, skip),
+            part_size,
+            scalars,
+            [
+                (slots, None, None),
+                (rows_in, None, None),
+                (expert_up, *held_expert((half, hidden_width), 1, skip)),
+            ],
+            [
+                (
+                    shape((2, part_size * capacity, group_rows)),
+                    *slot_block((capacity, group_rows)),
+                ),
+                (shape((part_size, pair, half)), *per_expert((pair, half))),
+                (shape((part_size, pair, hidden_width)), *a_hidden),
+            ],
         )
-
-    def dispatch(pick, values):
-        out = jnp.einsum("gest,gtd->egsd", pick, values, preferred_element_type=WIDE)
-        return out.reshape(kept, 2 * capacity, values.shape[-1])
-
-    def collect(pick, values):
-        values = values.reshape(kept, 2, capacity, values.shape[-1])
-        return jnp.einsum("gest,egsd->gtd", pick, values, preferred_element_type=WIDE)
-
-    hot = picks(mine)
-    pick_near, pick_far = hot.astype(LOW), picks(theirs).astype(LOW)
-    up_near = lax.dynamic_slice_in_dim(expert_up, mine, kept, 0)
-    up_far = lax.dynamic_slice_in_dim(expert_up, theirs, kept, 0)
-    buffer_far = dispatch(pick_far, rows_in).astype(LOW)
-    away = jnp.einsum("ecd,edf->ecf", buffer_far, up_far, preferred_element_type=WIDE)
-    arrived = swap(away.astype(LOW))
-    buffer_near = dispatch(pick_near, rows_in).astype(LOW)
-    before_gelu = jnp.einsum("ecd,edf->ecf", buffer_near, up_near, preferred_element_type=WIDE)
-    before_gelu = before_gelu + arrived.astype(WIDE)
-    probs_own = lax.dynamic_slice_in_dim(probs_all, z * local_experts + mine, kept, 2)
-    probs_own = jnp.swapaxes(probs_own, 1, 2).reshape(2, kept, 1, group_rows)
-    slot_gate = jnp.sum(jnp.where(hot, probs_own, 0.0), -1)
-    gates = jnp.swapaxes(slot_gate, 0, 1).reshape(kept, 2 * capacity, 1)
-    down_full = by_index(f, down_near, down_far, 2)
-    hidden = jax.nn.gelu(before_gelu, approximate=False).astype(LOW)
-    expert_out = jnp.einsum("ecf,efd->ecd", hidden, down_full, preferred_element_type=WIDE)
-    part = collect(pick_near, (expert_out * gates).astype(LOW)).astype(LOW)
-    part = part.reshape(8, rows, width)
+        away, scalars = lax.optimization_barrier((away, scalars))
+        picks_far.append(pick)
+        buffers_far.append(buffer)
+        arrived.append(swap(away))
+    down_far = jnp.concatenate([down_a, down_b, down_c], 0)
+    pick_near, buffer_near, own, gates = local_call(
+        near_up_kernel,
+        kept,
+        scalars,
+        [(slots, None, None), (rows_in, None, None), near_up, (probs_all, None, None)],
+        [
+            a_pick,
+            a_buffer,
+            (shape((kept, pair, hidden_width), WIDE), *per_expert((pair, hidden_width))),
+            (shape((kept, pair, 1), WIDE), *per_expert((pair, 1))),
+        ],
+    )
+    hiddens, slopes, weighted = [], [], []
+    for n, skip in enumerate(halves):
+        ins = [
+            (own, *per_expert((pair, hidden_width), skip)),
+            (arrived[n], *a_hidden),
+            (gates, *per_expert((pair, 1), skip)),
+            (expert_down, *held_expert((hidden_width, half), 0, skip)),
+            (down_far, *per_expert((hidden_width, half), skip)),
+        ]
+        outs = [
+            (shape((part_size, pair, hidden_width)), *a_hidden),
+            (shape((part_size, pair, hidden_width), WIDE), *a_hidden),
+        ]
+        rows_shape = (2, part_size * capacity, width)
+        last = n == 1
+        if last:
+            ins += [(weighted[0], None, None), (pick_near, None, None)]
+            outs.append((shape((2, group_rows, width)), None, None))
+        else:
+            outs.append((shape(rows_shape), None, None))
+        scratch = [pltpu.VMEM(rows_shape, LOW)] if last else []
+        hidden, slope, out = local_call(
+            functools.partial(down_kernel, last), part_size, scalars, ins, outs, scratch
+        )
+        hiddens.append(hidden)
+        slopes.append(slope)
+        weighted.append(out)
+    part = weighted[1]
+    me = f * 4 + lax.axis_index(TENSOR)
+    probs_own = lax.dynamic_index_in_dim(probs_all, me, 0, False)
 
     valid_rows = valid_mask[0].astype(WIDE)[:, None]
     scale = jnp.full((8, 128), total_tokens / valid_total, WIDE)
     result, final_grad, group_grad, loss = combine(
-        heads, part, residual, teacher[0], valid_rows, scale
+        heads, part.reshape(2, 2, 2, rows, width), residual, teacher[0], valid_rows, scale
     )
     loss_terms = (jnp.sum(loss) * (total_images / (valid_total * width)))[None]
 
-    slot_grad = dispatch(pick_near, group_grad.reshape(2, group_rows, width))
-    out_grad = (slot_grad * gates).astype(LOW)
-    raw = jnp.einsum(
-        "ecd,efd->ecf", slot_grad.astype(LOW), down_full, preferred_element_type=WIDE
-    )
-    gate_slot_grad = jnp.sum(raw * hidden.astype(WIDE), -1)
-    normal_cdf = 0.5 * (1.0 + lax.erf(before_gelu * ROOT_HALF))
-    slope = normal_cdf + before_gelu * DENSITY * jnp.exp(-0.5 * before_gelu * before_gelu)
-    pre_near = (raw * gates * slope).astype(LOW)
-    pre_far = swap(pre_near)
-    down_grad = jnp.einsum("ecf,ecd->efd", hidden, out_grad, preferred_element_type=WIDE)
-    down_own = lax.dynamic_slice_in_dim(down_grad, f * half, half, 2)
-    down_send = lax.dynamic_slice_in_dim(down_grad, (1 - f) * half, half, 2).astype(LOW)
-    ids = z * local_experts + mine + jnp.arange(kept, dtype=jnp.int32)
-    column = (ids[:, None, None] == lanes).astype(WIDE)
-
-    def through_up(pick, buffer, pre, up, extra):
-        grad = jnp.einsum("ecd,ecf->edf", buffer, pre, preferred_element_type=WIDE)
-        rows_out = jnp.einsum("ecf,edf->ecd", pre, up, preferred_element_type=WIDE)
-        rows_out = jnp.concatenate([rows_out, extra], -1).astype(LOW)
-        return grad, collect(pick, rows_out)
-
-    up_own, back_near = through_up(
-        pick_near, buffer_near, pre_near, up_near, gate_slot_grad[..., None] * column
-    )
-    up_other, back_far = through_up(
-        pick_far, buffer_far, pre_far, up_far, jnp.zeros((kept, 2 * capacity, 128), WIDE)
-    )
-    back_part = (back_near + back_far).astype(LOW).reshape(8, rows, -1)
+    grads_in = group_grad.reshape(2, group_rows, width)
+    pres_near, pres_far, out_grads, extras = [], [], [], []
+    for n, skip in enumerate(halves):
+        pre, out_grad, extra = local_call(
+            hidden_back_kernel,
+            part_size,
+            scalars,
+            [
+                (pick_near, *slot_block((capacity, group_rows), skip)),
+                (grads_in, None, None),
+                (expert_down, *held_expert((hidden_width, half), 0, skip)),
+                (down_far, *per_expert((hidden_width, half), skip)),
+                (hiddens[n], *a_hidden),
+                (slopes[n], *a_hidden),
+                (gates, *per_expert((pair, 1), skip)),
+            ],
+            [
+                (shape((part_size, pair, hidden_width)), *a_hidden),
+                (shape((part_size, pair, width)), *per_expert((pair, width))),
+                (shape((2, part_size, group_rows), WIDE), None, None),
+            ],
+            [pltpu.VMEM((pair, width), LOW)],
+        )
+        pre, scalars = lax.optimization_barrier((pre, scalars))
+        pres_near.append(pre)
+        pres_far.append(swap(pre))
+        out_grads.append(out_grad)
+        extras.append(extra)
+    down_shape = shape(expert_down.shape, WIDE)
+    up_shape = shape(expert_up.shape, WIDE)
+    down_grad, sends = None, []
+    pieces = ((0, 0, part_size), (1, 0, part_size - 1), (1, part_size - 1, 1))
+    for n, skip, size in pieces:
+        ins = [
+            (hiddens[n], *per_expert((pair, hidden_width), skip)),
+            (out_grads[n], *per_expert((pair, width), skip)),
+        ]
+        if sends:
+            ins.append((down_grad, pl.ANY, None))
+        first = n * part_size + skip
+        down_grad, send = local_call(
+            down_grad_kernel,
+            size,
+            scalars,
+            ins,
+            [
+                (down_shape, *held_expert((hidden_width, half), 0, first)),
+                (shape((size, hidden_width, half)), *per_expert((hidden_width, half))),
+            ],
+            aliases={3: 0} if sends else None,
+            microseconds=2 * size,
+        )
+        sends.append(send)
+    down_others = [swap(send) for send in sends[:2]]
+    up_grad, rows_near = None, []
+    for n, skip in enumerate(halves):
+        ins = [
+            (buffer_near, *per_expert((pair, half), skip)),
+            (pres_near[n], *a_hidden),
+            (expert_up, *held_expert((half, hidden_width), 0, skip)),
+        ]
+        if n:
+            ins.append((up_grad, pl.ANY, None))
+        up_grad, out = local_call(
+            up_back_kernel,
+            part_size,
+            scalars,
+            ins,
+            [
+                (up_shape, *held_expert((half, hidden_width), 0, skip)),
+                (shape((2, part_size * capacity, half)), *slot_block((capacity, half))),
+            ],
+            aliases={4: 0} if n else None,
+        )
+        rows_near.append(out)
+    rows_near = jnp.concatenate(rows_near, 1)
+
+    def far_ins(n, skip):
+        return [
+            (buffers_far[n], *per_expert((pair, half))),
+            (pres_far[n], *a_hidden),
+            (expert_up, *held_expert((half, hidden_width), 1, skip)),
+        ]
+
+    up_grad, rows_far = local_call(
+        up_back_kernel,
+        part_size,
+        scalars,
+        [*far_ins(0, 0), (up_grad, pl.ANY, None)],
+        [
+            (up_shape, *held_expert((half, hidden_width), 1)),
+            (shape((2, part_size * capacity, half)), *slot_block((capacity, half))),
+        ],
+        aliases={4: 0},
+    )
+    up_grad, back_part = local_call(
+        far_up_last_kernel,
+        part_size,
+        scalars,
+        [
+            *far_ins(1, part_size),
+            (rows_near, None, None),
+            (rows_far, None, None),
+            (pick_near, None, None),
+            (jnp.concatenate(picks_far, 1), None, None),
+            (up_grad, pl.ANY, None),
+        ],
+        [
+            (up_shape, *held_expert((half, hidden_width), 1, part_size)),
+            (shape((2, group_rows, half)), None, None),
+        ],
+        [pltpu.VMEM((2, part_size * capacity, half), LOW)],
+        aliases={8: 0},
+    )
+    back_part = back_part.reshape(2, 2, 2, rows, half)
 
     attended, logit_grads, residual_grad, gain_two_part = back_through_norm(
-        heads, expert_count, back_part, residual, gain_b, router_wide, final_grad
-    )
-    attended, down_send = lax.optimization_barrier((attended, down_send))
-    down_other = swap(down_send)
-
+        heads,
+        back_part,
+        extras[0],
+        extras[1],
+        residual,
+        gain_b,
+        router_wide[:, :expert_count].T,
+        probs_own,
+        final_grad,
+    )
+
+    attended, last_send = lax.optimization_barrier((attended, sends[2]))
+    down_others.append(swap(last_send))
     attended_grad = attended.reshape(rows, width)
     wo_own = lax.dynamic_index_in_dim(wo_all, z, 1, False).reshape(width, -1)
     mixed_grad = (
@@ -1254,10 +1757,9 @@
     gain_one_part = jnp.sum(first_part * normed_one, 0)
     qkv_grad = jnp.einsum("sd,se->de", first_in, projected_grad, preferred_element_type=WIDE)
     out_grad_t = jnp.einsum("sd,se->de", attended_grad, mixed, preferred_element_type=WIDE)
-    router_grad = jnp.einsum(
-        "sd,se->de", second_in, logit_grads.reshape(rows, 128), preferred_element_type=WIDE
-    )
-    dense = jnp.concatenate([qkv_grad, out_grad_t, router_grad], 1).astype(LOW)
+    router_grad = dot(second_in, logit_grads, (0, 1))
+    spare = jnp.zeros((width, -(qkv_width + out_grad_t.shape[1] + expert_count) % 128), WIDE)
+    dense = jnp.concatenate([qkv_grad, out_grad_t, router_grad, spare], 1).astype(LOW)
     gain_parts = jnp.stack([gain_one_part, jnp.sum(gain_two_part, 0)], 0).reshape(2, 8, block)
     gain_parts = jnp.pad(jnp.swapaxes(gain_parts, 0, 1), ((0, 0), (0, 6), (0, 128 - block)))
     tokens_grad, dense_out, gain_out = last_sums(
@@ -1269,6 +1771,16 @@
         residual_grad,
         gain_parts,
     )
+    for arrived, (n, skip, size) in zip(down_others, pieces):
+        (down_grad,) = local_call(
+            widen_kernel,
+            size,
+            scalars,
+            [(arrived, *per_expert((hidden_width, half))), (down_grad, pl.ANY, None)],
+            [(down_shape, *held_expert((hidden_width, half), 1, n * part_size + skip))],
+            aliases={2: 0},
+            microseconds=2 * size,
+        )
     out_width = head_count * head_dim
     return (
         result.reshape(1, rows, width),
@@ -1279,8 +1791,8 @@
         dense_out[:, qkv_width : qkv_width + out_width].T.reshape(head_count, head_dim, block),
         gain_out[1, :block],
         dense_out[:, qkv_width + out_width : qkv_width + out_width + expert_count],
-        by_index(f, up_own, up_other, 0),
-        by_index(f, down_own, down_other.astype(WIDE), 0),
+        up_grad,
+        down_grad,
     )
 
 
@@ -1291,7 +1803,7 @@
         and sizes[TENSOR] == 4
         and sizes[HEADS] % 2 == 0
         and tokens.shape[0] == 1
-        and up.shape[0] % 2 == 0
+        and up.shape[0] % 8 == 0
         and tokens.shape[1] % (32 * sizes[HEADS]) == 0
         and tokens.shape[2] % 256 == 0
         and routes.shape[2] <= 8

time: 437 us -> 329 us (0.75)
  matrix products: 67.9 us -> 5.07 us
  waiting for transfers between devices: 66.6 us -> 35 us
  other arithmetic: 38.1 us -> 11.1 us
  starting transfers between devices: 4.29 us -> 10.7 us
    dot_general x18 -> x1, matrix products: 63 us -> 0.19 us  [dot(): lax.dot_general(a, b, (((over[0],), (over[1],)), ((), ())), preferred_ele...]
    ppermute x4 -> x9, waiting for transfers between devices: 66.6 us -> 35 us  [swap(): return lax.ppermute(values, FSDP, [(0, 1), (1, 0)])]
    unnamed x91 -> x127, local copies, waits for them, and re-layouts: 11.9 us -> 27 us
    select_n x3 -> x0, other arithmetic: 13.2 us -> none  [by_index(): jnp.where(index == 0, jnp.concatenate([own, other], axis), jnp.concatenat...]
    convert_element_type x4 -> x0, other arithmetic: 9.35 us -> none  [the longest x1 7.15 us: fast(): hidden = jax.nn.gelu(before_gelu, approximate=False).astype(LOW)]
    ppermute x4 -> x9, starting transfers between devices: 4.29 us -> 10.7 us  [swap(): return lax.ppermute(values, FSDP, [(0, 1), (1, 0)])]
    dynamic_slice x3 -> x2, local copies, waits for them, and re-layouts: 9.89 us -> 3.61 us  [the longest x1 2.41 us: fast(): lax.dynamic_slice_in_dim(expert_down, theirs + first_chunk, second_chunk, 0)]
    reduce_sum x1 -> x0, other arithmetic: 4.58 us -> none  [fast(): slot_gate = jnp.sum(jnp.where(hot, probs_own, 0.0), -1)]
  transfers between devices with their start and end apart: 4 -> 9, of which waited for: 3 -> 3; matrix products, arithmetic and copies ran while one was open for 16% -> 9% of each run, Pallas kernels for 14% -> 42%
where the time goes in v2:
time: 329 us; the launch traced here: 328 us
  Pallas kernels  225 us (68%)
  local copies, waits for them, and re-layouts  36.9 us (11%)
  waiting for transfers between devices  35 us (11%)
  other arithmetic  11.1 us (3%)
  starting transfers between devices  10.7 us (3%)
  matrix products  5.07 us (2%)
  between operations  4.01 us (1%)
    pallas_call x5, Pallas kernels, remote_call(): pl.pallas_call(kernel, out_shape=outs, in_specs=[hbm if i in in_hbm else...  168 us
    pallas_call x17, Pallas kernels, local_call(): pl.pallas_call(kernel, out_shape=[o[0] for o in outs], grid_spec=pltpu.Pr...  57.2 us
    ppermute x9, waiting for transfers between devices, swap(): return lax.ppermute(values, FSDP, [(0, 1), (1, 0)])  35 us
    unnamed x127, local copies, waits for them, and re-layouts  27 us
    ppermute x9, starting transfers between devices, swap(): return lax.ppermute(values, FSDP, [(0, 1), (1, 0)])  10.7 us
  transfers between devices with their start and end apart: 9, of which 3 were waited for; matrix products, arithmetic and copies ran while one was open for 9% of the time, Pallas kernels for 42%

profile of v2, /device:TPU:0, one launch (start us, length us, event | category | flops | bytes accessed | tf_op | source)
XLA Modules:
  0.0 327.6 jit_solution(12592676478697811587)
XLA Ops:
  0.7 1.2 constant_dynamic-slice_fusion.2
  1.9 3.0 collective-permute-start
  4.9 1.4 convert_bitcast_fusion
  7.0 1.1 convert_reduce_fusion
  8.2 1.9 copy.85
  11.6 2.4 constant_dynamic-slice_fusion.1
  14.0 4.2 %collective-permute-done = bf16[1,768,384]{2,1,0:T(8,128)(2,1)S(1)} collective-permute-done((bf16[1,768,384]{2,1,0:T(8,128)(2,1)S(1)}, bf16[1,768,384]{2,1,0:T(8,128)(2,1)S(1)}, u32[]{:S(2)}, u32[]{:S(2)}) %collective-permute-start) | collective-permute-done | bytes 589856 | tf_op jit(solution)/shard_map/ppermute | solution.py:1405
  19.1 20.2 %shard_map.186 = (bf16[8,96,768]{2,1,0:T(8,128)(2,1)S(1)}, bf16[8,4,96,192]{3,2,1,0:T(8,128)(2,1)S(1)}, s32[8,8,128]{2,1,0:T(8,128)S(1)}, s32[8,1024]{1,0:T(8,128)S(1)}) custom-call(bf16[96,768]{1,0:T(8,128)(2,1)S(1)} %concatenate.23.wq, bf16[96,192]{1,0:T(8,128)(2,1)S(1)} %bitcast.107, s32[8,128]{1,0:T(8,128)S(1)} %broadcast_in_dim.62.count, ...), custom_call_target="tpu_custom_call" | custom-call | bytes 60000000 | tf_op jit(solution)/shard_map/pallas_call | solution.py:549
  43.3 44.4 %shard_map.187 = (f32[256,768]{1,0:T(8,128)S(1)}, bf16[256,768]{1,0:T(8,128)(2,1)S(1)}, bf16[8,256,384]{2,1,0:T(8,128)(2,1)S(1)}, f32[8,32,256]{2,1,0:T(8,128)S(...) custom-call(bf16[256,192]{1,0:T(8,128)(2,1)S(1)} %copy.79.mixed, ...), custom_call_target="tpu_custom_call" | custom-call | bytes 78000000 | tf_op jit(solution)/shard_map/pallas_call | solution.py:549
  87.7 3.5 %copy-done = bf16[8,384,768]{2,1,0:T(8,128)(2,1)S(1)} copy-done((bf16[8,384,768]{2,1,0:T(8,128)(2,1)S(1)}, bf16[8,384,768]{2,1,0:T(8,128)(2,1)}, u32[]{:S(2)}) %copy-start) | copy-done | bytes 4718616
  91.2 2.8 shard_map.188
  94.8 2.8 shard_map.189
  98.4 1.0 copy-done.20
  99.4 1.5 collective-permute-start.2
  103.5 1.1 constant_dynamic-update-slice_fusion.2
  104.7 2.3 copy-done.1
  107.0 1.4 copy-done.5
  108.4 3.7 %shard_map.190 = (bf16[2,512,1024]{2,1,0:T(8,128)(2,1)S(1)}, bf16[4,256,384]{2,1,0:T(8,128)(2,1)S(1)}, f32[4,256,768]{2,1,0:T(8,128)S(1)}, f32[4,256,1]{2,1,0:T(8,128)S(1)}) custom-call(s32[4]{0:T(128)S(1)} %pad_add_fusion.s, s32[16,1024]{1,0:T(8,128)S(1)} %get-tuple-element.92.slots, bf16[2,1024,384]{2,1,0:T(8,128)(2,1)S(1)} %bitcast.90, ...), custom_call_target="tpu_custom_call" | custom-call | bytes 15000000 | tf_op jit(solution)/shard_map/pallas_call | solution.py:1254
  112.2 1.8 constant_dynamic-update-slice_fusion.1
  114.1 22.1 %collective-permute-done.3.arrived = bf16[2,256,768]{2,1,0:T(8,128)(2,1)} collective-permute-done((bf16[2,256,768]{2,1,0:T(8,128)(2,1)}, bf16[2,256,768]{2,1,0:T(8,128)(2,1)}, u32[]{:S(2)}, u32[]{:S(2)}) %collective-permute-start.3) | collective-permute-done | bytes 786464 | tf_op jit(solution)/shard_map/ppermute | solution.py:1405
  136.2 3.1 shard_map.191
  139.3 5.0 %shard_map.192 = (bf16[2,256,768]{2,1,0:T(8,128)(2,1)S(1)}, f32[2,256,768]{2,1,0:T(8,128)S(1)}, bf16[2,1024,768]{2,1,0:T(8,128)(2,1)S(1)}) custom-call(s32[4]{0:T(128)S(1)} %pad_add_fusion.s, f32[4,256,768]{2,1,0:T(8,128)S(1)} %get-tuple-element.101.own, bf16[2,256,768]{2,1,0:T(8,128)(2,1)} %collective-permute-done.2.arrived, ...), custom_call_target="tpu_custom_call" | custom-call | bytes 15000000 | tf_op jit(solution)/shard_map/pallas_call | solution.py:1254
  144.3 46.9 %shard_map.193 = (bf16[4,64,768]{2,1,0:T(8,128)(2,1)S(1)}, f32[64,768]{1,0:T(8,128)S(1)}, bf16[8,256,768]{2,1,0:T(8,128)(2,1)S(1)}, f32[4,8,128]{2,1,0:T(8,128)S(1)}) custom-call(bf16[2,2,2,256,768]{4,3,2,1,0:T(8,128)(2,1)S(1)} %bitcast.95, f32[256,768]{1,0:T(8,128)S(1)} %copy-done.15, bf16[256,768]{1,0:T(8,128)(2,1)S(1)} %bitcast.100, ...), custom_call_target="tpu_custom_call" | custom-call | bytes 150000000 | tf_op jit(solution)/shard_map/pallas_call | solution.py:549
  191.2 4.0 %shard_map.194 = (bf16[2,256,768]{2,1,0:T(8,128)(2,1)}, bf16[2,256,768]{2,1,0:T(8,128)(2,1)S(1)}, f32[2,2,1024]{2,1,0:T(2,128)S(1)}) custom-call(s32[4]{0:T(128)S(1)} %pad_add_fusion.s, bf16[2,512,1024]{2,1,0:T(8,128)(2,1)S(1)} %get-tuple-element.109.refs_1_.pick.pick_near, bf16[2,1024,768]{2,1,0:T(8,128)(2,1)S(1)} %bitcast.91, ...), custom_call_target="tpu_custom_call" | custom-call | bytes 15000000 | tf_op jit(solution)/shard_map/pallas_call | solution.py:1254
  195.3 4.0 %shard_map.195 = (bf16[2,256,768]{2,1,0:T(8,128)(2,1)}, bf16[2,256,768]{2,1,0:T(8,128)(2,1)S(1)}, f32[2,2,1024]{2,1,0:T(2,128)S(1)}) custom-call(s32[4]{0:T(128)S(1)} %pad_add_fusion.s, bf16[2,512,1024]{2,1,0:T(8,128)(2,1)S(1)} %get-tuple-element.109.refs_1_.pick.pick_near, bf16[2,1024,768]{2,1,0:T(8,128)(2,1)S(1)} %bitcast.92, ...), custom_call_target="tpu_custom_call" | custom-call | bytes 15000000 | tf_op jit(solution)/shard_map/pallas_call | solution.py:1254
  200.9 1.3 collective-permute-start.5
  203.0 2.0 multiply_convert_fusion
  205.0 3.1 pad_maximum_fusion.pick_far
  208.1 2.3 copy-done.2
  210.4 3.5 %shard_map.196 = (f32[8,384,768]{2,1,0:T(8,128)}, bf16[2,256,384]{2,1,0:T(8,128)(2,1)S(1)}) custom-call(s32[4]{0:T(128)S(1)} %pad_add_fusion.s, bf16[4,256,384]{2,1,0:T(8,128)(2,1)S(1)} %copy-done.11, bf16[2,256,768]{2,1,0:T(8,128)(2,1)} %get-tuple-element.127.pre, bf16[8,384,768]{2,1,0:T(8,128)(2,1)S(1)} %copy-done.2), custom_call_target="tpu_custom_call" | custom-call | bytes 15000000 | tf_op jit(solution)/shard_map/pallas_call | solution.py:1254
  214.0 3.8 %shard_map.197 = (f32[8,384,768]{2,1,0:T(8,128)}, bf16[2,256,384]{2,1,0:T(8,128)(2,1)S(1)}) custom-call(s32[4]{0:T(128)S(1)} %pad_add_fusion.s, bf16[4,256,384]{2,1,0:T(8,128)(2,1)S(1)} %copy-done.11, bf16[2,256,768]{2,1,0:T(8,128)(2,1)} %get-tuple-element.125.pre, bf16[8,384,768]{2,1,0:T(8,128)(2,1)S(1)} %copy-done.2, ...), custom_call_target="tpu_custom_call", output_to_operand_aliasing={{0}: (4, {})} | custom-call | bytes 15000000 | tf_op jit(solution)/shard_map/pallas_call | solution.py:1254
  217.8 3.0 shard_map.201
  220.8 2.2 shard_map.202
  223.0 2.0 shard_map.203
  226.5 1.3 collective-permute-start.8
  229.1 8.6 %collective-permute-done.5.pre = bf16[2,256,768]{2,1,0:T(8,128)(2,1)} collective-permute-done((bf16[2,256,768]{2,1,0:T(8,128)(2,1)}, bf16[2,256,768]{2,1,0:T(8,128)(2,1)}, u32[]{:S(2)}, u32[]{:S(2)}) %collective-permute-start.5) | collective-permute-done | bytes 786464 | tf_op jit(solution)/shard_map/ppermute | solution.py:1405
  237.8 2.3 copy-done.3
  240.1 1.0 copy-done.33
  241.1 3.7 %shard_map.198 = (f32[8,384,768]{2,1,0:T(8,128)}, bf16[2,256,384]{2,1,0:T(8,128)(2,1)S(1)}) custom-call(s32[4]{0:T(128)S(1)} %pad_add_fusion.s, bf16[2,256,384]{2,1,0:T(8,128)(2,1)S(1)} %copy-done.33, bf16[2,256,768]{2,1,0:T(8,128)(2,1)} %collective-permute-done.5.pre, bf16[8,384,768]{2,1,0:T(8,128)(2,1)S(1)} %copy-done.3, ...), custom_call_target="tpu_custom_call", output_to_operand_aliasing={{0}: (4, {})} | custom-call | bytes 15000000 | tf_op jit(solution)/shard_map/pallas_call | solution.py:1254
  244.9 6.1 %shard_map.199 = (f32[8,384,768]{2,1,0:T(8,128)}, bf16[2,1024,384]{2,1,0:T(8,128)(2,1)S(1)}) custom-call(s32[4]{0:T(128)S(1)} %pad_add_fusion.s, bf16[2,256,384]{2,1,0:T(8,128)(2,1)S(1)} %copy-done.31, bf16[2,256,768]{2,1,0:T(8,128)(2,1)} %collective-permute-done.4.pre, bf16[8,384,768]{2,1,0:T(8,128)(2,1)S(1)} %copy-done.3, ...), custom_call_target="tpu_custom_call", output_to_operand_aliasing={{0}: (8, {})} | custom-call | bytes 15000000 | tf_op jit(solution)/shard_map/pallas_call | solution.py:1254
  251.0 35.4 %shard_map.200 = (bf16[4,64,768]{2,1,0:T(8,128)(2,1)S(1)}, bf16[32,256]{1,0:T(8,128)(2,1)S(1)}, f32[64,768]{1,0:T(8,128)S(1)}, f32[8,768]{1,0:T(8,128)S(1)}) custom-call(bf16[2,2,2,256,384]{4,3,2,1,0:T(8,128)(2,1)S(1)} %bitcast.98, f32[2,2,1024]{2,1,0:T(2,128)S(1)} %get-tuple-element.138.gates_a, f32[2,2,1024]{2,1,0:T(2,128)S(1)} %get-tuple-element.139.gates_b, ...), custom_call_target="tpu_custom_call" | custom-call | bytes 120000000 | tf_op jit(solution)/shard_map/pallas_call | solution.py:549
  290.3 1.0 collective-permute-start.6
  291.6 1.5 convolution_convert_fusion
  293.6 20.7 %shard_map.204 = (f32[4,64,768]{2,1,0:T(8,128)S(1)}, f32[96,896]{1,0:T(8,128)S(1)}, f32[8,128]{1,0:T(8,128)S(1)}) custom-call(bf16[4,64,768]{2,1,0:T(8,128)(2,1)S(1)} %bitcast.101, bf16[8,96,896]{2,1,0:T(8,128)(2,1)S(1)} %maximum_maximum_fusion.dense, bf16[256,768]{1,0:T(8,128)(2,1)S(1)} %bitcast.94, f32[1,768]{1,0:T(1,128)S(1)} %reshape.201.gain, ...), custom_call_target="tpu_custom_call" | custom-call | bytes 75000000 | tf_op jit(solution)/shard_map/pallas_call | solution.py:549
  317.4 3.1 shard_map.205.held
  320.5 2.7 shard_map.206.held
  323.2 1.6 shard_map.207
  325.6 0.9 copy.110
  (190 shorter events, 23.5 us)
Async XLA Ops:
  0.6 9.8 %copy-start.51 = (bf16[96,3,192]{2,0,1:T(8,128)(2,1)S(1)}, bf16[96,3,192]{2,0,1:T(8,128)(2,1)}, u32[]{:S(2)}) copy-start(bf16[96,3,192]{2,0,1:T(8,128)(2,1)} %param.16) | copy-start | bytes 331780
  0.7 10.7 %copy-start.6 = (bf16[1,256,768]{2,1,0:T(8,128)(2,1)S(1)}, bf16[1,256,768]{2,1,0:T(8,128)(2,1)}, u32[]{:S(2)}) copy-start(bf16[1,256,768]{2,1,0:T(8,128)(2,1)} %param.11) | copy-start | bytes 1179652
  0.7 9.4 %copy-start.53 = (bf16[96,32]{0,1:T(8,128)(2,1)S(1)}, bf16[96,32]{0,1:T(8,128)(2,1)}, u32[]{:S(2)}) copy-start(bf16[96,32]{0,1:T(8,128)(2,1)} %param.19) | copy-start | bytes 18436
  0.7 9.5 %copy-start.55 = (bf16[96]{0:T(256)(128)(2,1)S(1)}, bf16[96]{0:T(256)(128)(2,1)}, u32[]{:S(2)}) copy-start(bf16[96]{0:T(256)(128)(2,1)} %param.15) | copy-start | bytes 580
  0.7 9.6 %copy-start.56 = (bf16[96]{0:T(256)(128)(2,1)S(1)}, bf16[96]{0:T(256)(128)(2,1)}, u32[]{:S(2)}) copy-start(bf16[96]{0:T(256)(128)(2,1)} %param.18) | copy-start | bytes 580
  0.7 10.1 %copy-start.52 = (bf16[3,64,96]{2,1,0:T(8,128)(2,1)S(1)}, bf16[3,64,96]{2,1,0:T(8,128)(2,1)}, u32[]{:S(2)}) copy-start(bf16[3,64,96]{2,1,0:T(8,128)(2,1)} %param.17) | copy-start | bytes 110596
  0.7 10.2 %copy-start.54 = (s32[4,256,2]{1,2,0:T(2,128)S(1)}, s32[4,256,2]{1,2,0:T(2,128)}, u32[]{:S(2)}) copy-start(s32[4,256,2]{1,2,0:T(2,128)} %param.13) | copy-start | bytes 24580
  1.9 16.3 %collective-permute-start = (bf16[1,768,384]{2,1,0:T(8,128)(2,1)S(1)}, bf16[1,768,384]{2,1,0:T(8,128)(2,1)S(1)}, u32[]{:S(2)}, u32[]{:S(2)}) collective-permute-start(bf16[1,768,384]{2,1,0:T(8,128)(2,1)S(1)} %constant_dynamic-slice_fusion.2), channel_id=1, source_target_pairs={{0,16},{16,0},{1,17},{17,1},{2,18},{18,2},{3,19},{19,3},{4,20},{20... | collective-permute-start | bytes 1769480 | tf_op jit(solution)/shard_map/ppermute | solution.py:1405
  39.4 48.3 %collective-permute-start.1 = (bf16[2,768,384]{2,1,0:T(8,128)(2,1)}, bf16[2,768,384]{2,1,0:T(8,128)(2,1)}, u32[]{:S(2)}, u32[]{:S(2)}) collective-permute-start(bf16[2,768,384]{2,1,0:T(8,128)(2,1)} %constant_dynamic-slice_fusion.1), channel_id=1, source_target_pairs={{0,16},{16,0},{1,17},{17,1},{2,18},{18,2},{3,19},{19,3},{4,20},{20... | collective-permute-start | bytes 3538952 | tf_op jit(solution)/shard_map/ppermute | solution.py:1405
  42.2 45.5 %copy-start.49 = (bf16[3,64,256]{2,1,0:T(8,128)(2,1)}, bf16[3,64,256]{2,1,0:T(8,128)(2,1)S(1)}, u32[]{:S(2)}) copy-start(bf16[3,64,256]{2,1,0:T(8,128)(2,1)S(1)} %convolution_convert_fusion.4) | copy-start | bytes 294916
  87.7 6.4 %copy-start.14 = (f32[256,768]{1,0:T(8,128)}, f32[256,768]{1,0:T(8,128)S(1)}, u32[]{:S(2)}) copy-start(f32[256,768]{1,0:T(8,128)S(1)} %get-tuple-element.111.residual) | copy-start | bytes 2359300
  87.7 6.4 %copy-start.23 = (bf16[1,768,384]{2,1,0:T(8,128)(2,1)}, bf16[1,768,384]{2,1,0:T(8,128)(2,1)S(1)}, u32[]{:S(2)}) copy-start(bf16[1,768,384]{2,1,0:T(8,128)(2,1)S(1)} %get-tuple-element.106) | copy-start | bytes 1769476
  87.7 6.4 %copy-start.28 = (bf16[256,768]{1,0:T(8,128)(2,1)}, bf16[256,768]{1,0:T(8,128)(2,1)S(1)}, u32[]{:S(2)}) copy-start(bf16[256,768]{1,0:T(8,128)(2,1)S(1)} %get-tuple-element.148) | copy-start | bytes 1179652
  87.7 7.1 %copy-start.4 = (bf16[8,256,384]{2,1,0:T(8,128)(2,1)}, bf16[8,256,384]{2,1,0:T(8,128)(2,1)S(1)}, u32[]{:S(2)}) copy-start(bf16[8,256,384]{2,1,0:T(8,128)(2,1)S(1)} %get-tuple-element.95) | copy-start | bytes 4718596
  87.7 3.5 %copy-start = (bf16[8,384,768]{2,1,0:T(8,128)(2,1)S(1)}, bf16[8,384,768]{2,1,0:T(8,128)(2,1)}, u32[]{:S(2)}) copy-start(bf16[8,384,768]{2,1,0:T(8,128)(2,1)} %up.13) | copy-start | bytes 14155780
  94.8 2.8 copy-start.19
  99.4 39.9 %collective-permute-start.2 = (bf16[2,256,768]{2,1,0:T(8,128)(2,1)}, bf16[2,256,768]{2,1,0:T(8,128)(2,1)}, u32[]{:S(2)}, u32[]{:S(2)}) collective-permute-start(bf16[2,256,768]{2,1,0:T(8,128)(2,1)} %get-tuple-element.102), channel_id=1, source_target_pairs={{0,16},{16,0},{1,17},{17,1},{2,18},{18,2},{3,19},{19,3},{4,20},{20... | collective-permute-start | bytes 2359304 | tf_op jit(solution)/shard_map/ppermute | solution.py:1405
  100.8 35.3 %collective-permute-start.3 = (bf16[2,256,768]{2,1,0:T(8,128)(2,1)}, bf16[2,256,768]{2,1,0:T(8,128)(2,1)}, u32[]{:S(2)}, u32[]{:S(2)}) collective-permute-start(bf16[2,256,768]{2,1,0:T(8,128)(2,1)} %get-tuple-element.107), channel_id=1, source_target_pairs={{0,16},{16,0},{1,17},{17,1},{2,18},{18,2},{3,19},{19,3},{4,20},{20... | collective-permute-start | bytes 2359304 | tf_op jit(solution)/shard_map/ppermute | solution.py:1405
  102.7 33.5 %slice-start = ((s8[4718592]{0:T(1024)(128)(4,1)}), s8[524288]{0:T(1024)(128)(4,1)S(1)}, s32[]{:S(2)}) async-start(s8[4718592]{0:T(1024)(128)(4,1)} %bitcast.86), calls=%async_computation | async-start | bytes 1048576
  108.4 27.7 %slice-start.1 = ((s8[4718592]{0:T(1024)(128)(4,1)}), s8[4194304]{0:T(1024)(128)(4,1)S(1)}, s32[]{:S(2)}) async-start(s8[4718592]{0:T(1024)(128)(4,1)} %bitcast.86), calls=%async_computation.1 | async-start | bytes 8388608
  112.1 27.1 %copy-start.10 = (bf16[4,256,384]{2,1,0:T(8,128)(2,1)}, bf16[4,256,384]{2,1,0:T(8,128)(2,1)S(1)}, u32[]{:S(2)}) copy-start(bf16[4,256,384]{2,1,0:T(8,128)(2,1)S(1)} %get-tuple-element.126.buffer) | copy-start | bytes 2359300
  139.2 52.0 %copy-start.12 = (bf16[2,256,768]{2,1,0:T(8,128)(2,1)}, bf16[2,256,768]{2,1,0:T(8,128)(2,1)S(1)}, u32[]{:S(2)}) copy-start(bf16[2,256,768]{2,1,0:T(8,128)(2,1)S(1)} %get-tuple-element.116.hidden) | copy-start | bytes 2359300
  139.3 5.1 %copy-start.15 = (f32[256,768]{1,0:T(8,128)S(1)}, f32[256,768]{1,0:T(8,128)}, u32[]{:S(2)}) copy-start(f32[256,768]{1,0:T(8,128)} %copy-done.14) | copy-start | bytes 2359300
  139.3 5.1 %copy-start.25 = (bf16[1,256,768]{2,1,0:T(8,128)(2,1)S(1)}, bf16[1,256,768]{2,1,0:T(8,128)(2,1)}, u32[]{:S(2)}) copy-start(bf16[1,256,768]{2,1,0:T(8,128)(2,1)} %param.14) | copy-start | bytes 1179652
  144.3 51.0 %copy-start.8 = (bf16[2,256,768]{2,1,0:T(8,128)(2,1)}, bf16[2,256,768]{2,1,0:T(8,128)(2,1)S(1)}, u32[]{:S(2)}) copy-start(bf16[2,256,768]{2,1,0:T(8,128)(2,1)S(1)} %get-tuple-element.120.hidden) | copy-start | bytes 2359300
  191.2 4.1 %copy-start.26 = (bf16[4,64,768]{2,1,0:T(8,128)(2,1)}, bf16[4,64,768]{2,1,0:T(8,128)(2,1)S(1)}, u32[]{:S(2)}) copy-start(bf16[4,64,768]{2,1,0:T(8,128)(2,1)S(1)} %get-tuple-element.113) | copy-start | bytes 1179652
  191.2 4.0 %copy-start.36 = (f32[64,768]{1,0:T(8,128)}, f32[64,768]{1,0:T(8,128)S(1)}, u32[]{:S(2)}) copy-start(f32[64,768]{1,0:T(8,128)S(1)} %get-tuple-element.140.final_grad) | copy-start | bytes 589828
  195.3 4.0 %copy-start.21 = (bf16[2,256,768]{2,1,0:T(8,128)(2,1)}, bf16[2,256,768]{2,1,0:T(8,128)(2,1)S(1)}, u32[]{:S(2)}) copy-start(bf16[2,256,768]{2,1,0:T(8,128)(2,1)S(1)} %get-tuple-element.143.out_grad) | copy-start | bytes 2359300
  200.1 44.7 %collective-permute-start.4 = (bf16[2,256,768]{2,1,0:T(8,128)(2,1)}, bf16[2,256,768]{2,1,0:T(8,128)(2,1)}, u32[]{:S(2)}, u32[]{:S(2)}) collective-permute-start(bf16[2,256,768]{2,1,0:T(8,128)(2,1)} %get-tuple-element.125.pre), channel_id=1, source_target_pairs={{0,16},{16,0},{1,17},{17,1},{2,18},{18,2},{3,19},{19,3},{4,20},{20... | collective-permute-start | bytes 2359304 | tf_op jit(solution)/shard_map/ppermute | solution.py:1405
  200.9 36.9 %collective-permute-start.5 = (bf16[2,256,768]{2,1,0:T(8,128)(2,1)}, bf16[2,256,768]{2,1,0:T(8,128)(2,1)}, u32[]{:S(2)}, u32[]{:S(2)}) collective-permute-start(bf16[2,256,768]{2,1,0:T(8,128)(2,1)} %get-tuple-element.127.pre), channel_id=1, source_target_pairs={{0,16},{16,0},{1,17},{17,1},{2,18},{18,2},{3,19},{19,3},{4,20},{20... | collective-permute-start | bytes 2359304 | tf_op jit(solution)/shard_map/ppermute | solution.py:1405
  203.0 5.0 %copy-start.11 = (bf16[4,256,384]{2,1,0:T(8,128)(2,1)S(1)}, bf16[4,256,384]{2,1,0:T(8,128)(2,1)}, u32[]{:S(2)}) copy-start(bf16[4,256,384]{2,1,0:T(8,128)(2,1)} %copy-done.10) | copy-start | bytes 2359300
  213.9 3.8 %copy-start.13 = (bf16[2,256,768]{2,1,0:T(8,128)(2,1)S(1)}, bf16[2,256,768]{2,1,0:T(8,128)(2,1)}, u32[]{:S(2)}) copy-start(bf16[2,256,768]{2,1,0:T(8,128)(2,1)} %copy-done.12) | copy-start | bytes 2359300
  213.9 3.8 %copy-start.22 = (bf16[2,256,768]{2,1,0:T(8,128)(2,1)S(1)}, bf16[2,256,768]{2,1,0:T(8,128)(2,1)}, u32[]{:S(2)}) copy-start(bf16[2,256,768]{2,1,0:T(8,128)(2,1)} %copy-done.21) | copy-start | bytes 2359300
  213.9 6.9 %copy-start.9 = (bf16[2,256,768]{2,1,0:T(8,128)(2,1)S(1)}, bf16[2,256,768]{2,1,0:T(8,128)(2,1)}, u32[]{:S(2)}) copy-start(bf16[2,256,768]{2,1,0:T(8,128)(2,1)} %copy-done.8) | copy-start | bytes 2359300
  214.0 6.9 %copy-start.18 = (bf16[2,256,768]{2,1,0:T(8,128)(2,1)S(1)}, bf16[2,256,768]{2,1,0:T(8,128)(2,1)}, u32[]{:S(2)}) copy-start(bf16[2,256,768]{2,1,0:T(8,128)(2,1)} %copy-done.17) | copy-start | bytes 2359300
  225.8 94.7 %collective-permute-start.7 = (bf16[1,768,384]{2,1,0:T(8,128)(2,1)}, bf16[1,768,384]{2,1,0:T(8,128)(2,1)}, u32[]{:S(2)}, u32[]{:S(2)}) collective-permute-start(bf16[1,768,384]{2,1,0:T(8,128)(2,1)} %get-tuple-element.157), channel_id=1, source_target_pairs={{0,16},{16,0},{1,17},{17,1},{2,18},{18,2},{3,19},{19,3},{4,20},{20... | collective-permute-start | bytes 1769480 | tf_op jit(solution)/shard_map/ppermute | solution.py:1405
  226.5 90.9 %collective-permute-start.8 = (bf16[2,768,384]{2,1,0:T(8,128)(2,1)}, bf16[2,768,384]{2,1,0:T(8,128)(2,1)}, u32[]{:S(2)}, u32[]{:S(2)}) collective-permute-start(bf16[2,768,384]{2,1,0:T(8,128)(2,1)} %get-tuple-element.158), channel_id=1, source_target_pairs={{0,16},{16,0},{1,17},{17,1},{2,18},{18,2},{3,19},{19,3},{4,20},{20... | collective-permute-start | bytes 3538952 | tf_op jit(solution)/shard_map/ppermute | solution.py:1405
  241.1 3.7 %copy-start.7 = (bf16[2,512,1024]{2,1,0:T(8,128)(2,1)S(1)}, bf16[2,512,1024]{2,1,0:T(8,128)(2,1)}, u32[]{:S(2)}) copy-start(bf16[2,512,1024]{2,1,0:T(8,128)(2,1)} %pad_maximum_fusion.pick_far) | copy-start | bytes 6291460
  241.1 3.7 %copy-start.31 = (bf16[2,256,384]{2,1,0:T(8,128)(2,1)S(1)}, bf16[2,256,384]{2,1,0:T(8,128)(2,1)}, u32[]{:S(2)}) copy-start(bf16[2,256,384]{2,1,0:T(8,128)(2,1)} %copy-done.30) | copy-start | bytes 1179652
  244.9 6.1 %copy-start.16 = (f32[256,768]{1,0:T(8,128)S(1)}, f32[256,768]{1,0:T(8,128)}, u32[]{:S(2)}) copy-start(f32[256,768]{1,0:T(8,128)} %copy-done.14) | copy-start | bytes 2359300
  244.9 6.1 %copy-start.37 = (f32[64,768]{1,0:T(8,128)S(1)}, f32[64,768]{1,0:T(8,128)}, u32[]{:S(2)}) copy-start(f32[64,768]{1,0:T(8,128)} %copy-done.36) | copy-start | bytes 589828
  251.0 35.4 %copy-start.41 = (bf16[8,1,96,192]{3,2,1,0:T(8,128)(2,1)S(1)}, bf16[8,1,96,192]{3,2,1,0:T(8,128)(2,1)}, u32[]{:S(2)}) copy-start(bf16[8,1,96,192]{3,2,1,0:T(8,128)(2,1)} %constant_dynamic-slice_fusion) | copy-start | bytes 884740
  251.0 35.8 %copy-start.40 = (f32[3,256,256]{1,2,0:T(8,128)S(1)}, f32[3,256,256]{1,2,0:T(8,128)}, u32[]{:S(2)}) copy-start(f32[3,256,256]{1,2,0:T(8,128)} %copy-done.39) | copy-start | bytes 2359300
  251.0 36.1 %copy-start.46 = (bf16[256,576]{0,1:T(8,128)(2,1)S(1)}, bf16[256,576]{0,1:T(8,128)(2,1)}, u32[]{:S(2)}) copy-start(bf16[256,576]{0,1:T(8,128)(2,1)} %copy-done.45) | copy-start | bytes 884740
  288.1 3.3 copy-start.50
  288.9 2.8 copy-start.43
  290.1 3.1 copy-start.47
  290.3 32.9 %collective-permute-start.6 = (bf16[1,768,384]{2,1,0:T(8,128)(2,1)}, bf16[1,768,384]{2,1,0:T(8,128)(2,1)S(1)}, u32[]{:S(2)}, u32[]{:S(2)}) collective-permute-start(bf16[1,768,384]{2,1,0:T(8,128)(2,1)} %copy-done.38), channel_id=1, source_target_pairs={{0,16},{16,0},{1,17},{17,1},{2,18},{18,2},{3,19},{19,3},{4,20},{20... | collective-permute-start | bytes 1769480 | tf_op jit(solution)/shard_map/ppermute | solution.py:1405
  (20 other events, 25.7 us)

commit v3 on v2

--- a/solution.py
+++ b/solution.py
@@ -1,4 +1,5 @@
 import functools
+import types
 
 import jax
 import jax.numpy as jnp
@@ -316,7 +317,7 @@
 class Links:
     def __init__(self, send_sems, recv_sems):
         self.send_sems, self.recv_sems = send_sems, recv_sems
-        self.copies = []
+        self.copies, self.gone = [], []
 
     def send(self, src, dst, device):
         k = len(self.copies)
@@ -332,9 +333,15 @@
         self.copies.append(copy)
         return copy
 
+    def left(self, copies):
+        for copy in copies:
+            copy.wait_send()
+            self.gone.append(copy)
+
     def drain(self):
         for copy in self.copies:
-            copy.wait_send()
+            if not any(copy is other for other in self.gone):
+                copy.wait_send()
 
 
 class Place:
@@ -369,6 +376,23 @@
             pl.semaphore_signal(barrier, inc=1, device_id=device, device_id_type=MESH)
         pl.semaphore_wait(barrier, len(devices))
 
+    def tensor_peers(self):
+        t = 2 * self.y + self.c
+        return [{TENSOR: lax.rem(t + k, 4)} for k in range(1, 4)]
+
+    def owners(self):
+        return [
+            {FSDP: 1 - self.f if a else self.f, HEADS: lax.rem(self.z + k, self.heads)}
+            for k in range(self.heads)
+            for a in range(2)
+            if a or k
+        ]
+
+    def everyone(self):
+        t = 2 * self.y + self.c
+        corners = [{FSDP: 1 - self.f, TENSOR: lax.rem(t + k, 4)} for k in range(1, 4)]
+        return self.tensor_peers() + self.owners() + corners
+
     def axis_peers(self):
         return [self.x_peer, self.y_peer, self.core_peer]
 
@@ -545,7 +569,7 @@
     in_hbm=(),
     out_hbm=(),
 ):
-    vmem, hbm = pl.BlockSpec(memory_space=pltpu.VMEM), pl.BlockSpec(memory_space=pl.ANY)
+    vmem, hbm = pl.BlockSpec(memory_space=pltpu.VMEM), pl.BlockSpec(memory_space=pltpu.HBM)
     return pl.pallas_call(
         kernel,
         out_shape=outs,
@@ -816,33 +840,11 @@
                 stages[step - k](k)
 
 
-def combine_kernel(
-    heads,
-    chunks,
-    part,
-    residual,
-    teacher,
-    valid,
-    scale,
-    result,
-    final_grad,
-    group,
-    loss,
-    core_in,
-    xa,
-    ya,
-    yb,
-    xb,
-    image_sum,
-    far,
-    ss,
-    rs,
-):
-    place = Place(heads)
-    links = Links(ss, rs)
-    me = place.image(0, 0, 0)
-    z = place.z
-    place.greet(place.axis_peers() + place.z_peers)
+def combine_part(place, links, chunks, r):
+    heads, z, me = place.heads, place.z, place.image(0, 0, 0)
+    part, residual, teacher, valid, scale = r.part, r.residual, r.teacher, r.valid, r.scale
+    result, final_grad, group, loss = r.result, r.final_grad, r.group, r.loss
+    image_sum, far = r.image_sum, r.image_far
     rows_all, width = residual.shape
     own = rows_all // heads
     wide = width // chunks
@@ -855,11 +857,11 @@
             place,
             part,
             columns[k],
-            core_in.at[k],
-            xa.at[k],
-            ya.at[k],
-            yb.at[k],
-            xb.at[k],
+            r.sum_core.at[k],
+            r.sum_xa.at[k],
+            r.sum_ya.at[k],
+            r.sum_yb.at[k],
+            r.sum_xb.at[k],
         )
         for k in range(chunks)
     ]
@@ -933,80 +935,177 @@
     extra += all_heads(links, place, lambda k, to: (loss.at[z], loss.at[z]))
     for gather in gathers:
         gather.finish()
-    for copy in extra:
-        copy.wait_recv()
-    links.drain()
-
-
-def combine(heads, part, residual, teacher, valid, scale):
-    rows, width = residual.shape
-    own = rows // heads
-    chunks = width // 256
-    return remote_call(
-        functools.partial(combine_kernel, heads, chunks),
-        [
-            shape((heads, own, width)),
-            shape((own, width), WIDE),
-            shape((8, rows, width)),
-            shape((heads, 8, 128), WIDE),
-        ],
-        [part, residual, teacher, valid, scale],
-        [
-            pltpu.VMEM((chunks, 2, 2, rows, 256), LOW),
-            pltpu.VMEM((chunks, 2, rows, 128), LOW),
-            pltpu.VMEM((chunks, rows, 128), LOW),
-            pltpu.VMEM((chunks, 2, rows, 128), LOW),
-            pltpu.VMEM((chunks, rows, 128), LOW),
-            pltpu.VMEM((chunks, rows, 256), LOW),
-            pltpu.VMEM((chunks, heads - 1, own, 256), LOW),
-        ],
-        chunks * (5 + GATHER_COPIES + 2 * (heads - 1)) + 2 * (heads - 1),
-        3,
-        28,
-        50,
-    )
-
-
-def back_kernel(
-    heads,
-    chunks,
-    part,
-    gates_a,
-    gates_b,
-    residual,
-    gain,
-    router,
-    probs,
-    final_grad,
-    attended,
-    logit_grads,
-    residual_grad,
-    gain_part,
-    core_in,
-    y_in,
-    far,
-    pair,
-    x_in,
-    gate_own,
-    gate_in,
-    gate_sum,
-    gate_all,
-    logit_rows,
-    ss,
-    rs,
-):
-    place = Place(heads)
-    links = Links(ss, rs)
-    f, y, z = place.f, place.y, place.z
-    t = 2 * y + place.c
-    tensor_peers = [{TENSOR: lax.rem(t + k, 4)} for k in range(1, 4)]
-    owners = [
-        {FSDP: 1 - f if a else f, HEADS: lax.rem(z + k, heads)}
-        for k in range(heads)
-        for a in range(2)
-        if a or k
+    return extra
+
+
+def dot(a, b, over=(1, 0)):
+    return lax.dot_general(a, b, (((over[0],), (over[1],)), ((), ())), preferred_element_type=WIDE)
+
+
+def one_hot(slots, row, capacity):
+    places = lax.broadcasted_iota(jnp.int32, (capacity, slots.shape[1]), 0)
+    return places == slots[pl.ds(row, 1), :]
+
+
+class Loads:
+    def __init__(self, sems):
+        self.sems, self.count = sems, 0
+
+    def start(self, src, dst):
+        copy = pltpu.make_async_copy(src, dst, self.sems.at[self.count])
+        self.count += 1
+        copy.start()
+        return copy
+
+
+def gelu_parts(values):
+    cdf = 0.5 * (1.0 + lax.erf(values * ROOT_HALF))
+    return values * cdf, cdf + values * DENSITY * jnp.exp(-0.5 * values * values)
+
+
+def experts_part(place, links, loads, pieces, r):
+    slots, x, probs, up, down = r.slots, r.x, r.probs, r.up, r.down
+    pick_near, pick_far, gates, hidden = r.pick_near, r.pick_far, r.gates, r.hidden
+    buffer_near, buffer_far, own, weighted = r.buffer_near, r.buffer_far, r.own, r.weighted
+    away, arrived, w_up, w_near, w_far = r.away, r.arrived, r.w_up, r.w_near, r.w_far
+    kept, pair, _ = own.shape
+    capacity, half = pair // 2, x.shape[2]
+    local_experts = 2 * kept
+    mine, theirs = place.f * kept, (1 - place.f) * kept
+    ups = {}
+    for far in (1, 0):
+        for i in range(kept):
+            source = (theirs if far else mine) + i
+            ups[far, i] = loads.start(up.at[source], w_up.at[far, i])
+    nears = [loads.start(down.at[mine + i], w_near.at[i]) for i in range(kept)]
+    fars, at = [], 0
+    for piece in pieces:
+        size = piece.shape[0]
+        fars.append(loads.start(piece, w_far.at[pl.ds(at, size)]))
+        at += size
+    place.greet(place.everyone())
+    sent = []
+    for i in range(kept):
+        for g in range(2):
+            rows = slice(i * capacity, (i + 1) * capacity)
+            hot = one_hot(slots, g * local_experts + theirs + i, capacity).astype(LOW)
+            pick_far[g, rows] = hot
+            buffer_far[i, g * capacity : (g + 1) * capacity] = dot(hot, x[g]).astype(LOW)
+        ups[1, i].wait()
+        away[i] = dot(buffer_far[i], w_up[1, i]).astype(LOW)
+        sent.append(links.send(away.at[i], arrived.at[i], place.x_peer))
+    late = [
+        links.send(down.at[theirs + i], w_far.at[i], place.x_peer) for i in range(at, kept)
     ]
-    place.greet(tensor_peers + owners)
+    for i in range(kept):
+        expert = place.z * local_experts + mine + i
+        for g in range(2):
+            rows = slice(i * capacity, (i + 1) * capacity)
+            into = slice(g * capacity, (g + 1) * capacity)
+            hot = one_hot(slots, g * local_experts + mine + i, capacity)
+            chances = [probs[4 * g + k, pl.ds(expert, 1), :] for k in range(4)]
+            chances = jnp.concatenate(chances, 1)
+            gates[i, into] = jnp.sum(jnp.where(hot, chances, 0.0), -1, keepdims=True)
+            pick_near[g, rows] = hot.astype(LOW)
+            buffer_near[i, into] = dot(hot.astype(LOW), x[g]).astype(LOW)
+        ups[0, i].wait()
+        own[i] = dot(buffer_near[i], w_up[0, i])
+    for copy in nears + fars:
+        copy.wait()
+    for i in range(kept):
+        sent[i].wait_recv()
+        if i >= at:
+            late[i - at].wait_recv()
+        values, slopes = gelu_parts(own[i] + arrived[i].astype(WIDE))
+        hidden[i] = values.astype(LOW)
+        own[i] = slopes
+        for weight, f in ((w_near, place.f), (w_far, 1 - place.f)):
+            out = (dot(hidden[i], weight[i]) * gates[i]).astype(LOW)
+            columns = pl.ds(pl.multiple_of(f * half, half), half)
+            for g in range(2):
+                rows = slice(i * capacity, (i + 1) * capacity)
+                weighted[g, rows, columns] = out[g * capacity : (g + 1) * capacity]
+    for g in range(2):
+        total = dot(pick_near[g], weighted[g], (0, 0)).astype(LOW)
+        r.part[g] = total.reshape(r.part.shape[1:])
+    links.left(sent)
+
+
+def experts_back_part(place, links, loads, r):
+    pick_near, pick_far, hidden, slope, gates = r.pick_near, r.pick_far, r.hidden, r.own, r.gates
+    w_up, w_near, w_far, group = r.w_up, r.w_near, r.w_far, r.group
+    pre_near, pre_far, out_grad = r.away, r.arrived, r.out_grad
+    side = r.weighted.shape[2] // 2
+    rows_near = r.weighted.at[:, :, pl.ds(0, side)]
+    rows_far = r.weighted.at[:, :, pl.ds(side, side)]
+    send_held = r.w_far
+    kept, pair, width = out_grad.shape
+    capacity, half = pair // 2, width // 2
+    first = pl.ds(pl.multiple_of(place.f * half, half), half)
+    second = pl.ds(pl.multiple_of((1 - place.f) * half, half), half)
+    sent = []
+    for i in range(kept):
+        rows = slice(i * capacity, (i + 1) * capacity)
+        for g in range(2):
+            rows_in = group[4 * g : 4 * g + 4].reshape(pick_near.shape[2], width)
+            r.slot_rows[g * capacity : (g + 1) * capacity] = dot(
+                pick_near[g, rows], rows_in
+            ).astype(LOW)
+        raw = dot(r.slot_rows[:, first], w_near[i], (1, 1))
+        raw = raw + dot(r.slot_rows[:, second], w_far[i], (1, 1))
+        pre_near[i] = (raw * gates[i] * slope[i]).astype(LOW)
+        sent.append(links.send(pre_near.at[i], pre_far.at[i], place.x_peer))
+        out_grad[i] = (r.slot_rows[...].astype(WIDE) * gates[i]).astype(LOW)
+        gate_grad = jnp.sum(raw * hidden[i].astype(WIDE), -1, keepdims=True)
+        for g in range(2):
+            terms = gate_grad[g * capacity : (g + 1) * capacity]
+            terms = terms * pick_near[g, rows].astype(WIDE)
+            r.gate_rows[g, i : i + 1] = jnp.sum(terms, 0, keepdims=True)
+    bulk = []
+    for i in range(kept):
+        send_held[i] = dot(hidden[i], out_grad[i, :, second], (0, 0)).astype(LOW)
+    early = pl.ds(0, kept // 2)
+    bulk = [links.send(send_held.at[early], r.down_far.at[early], place.x_peer)]
+    stores = [
+        loads.start(r.hidden, r.hidden_out),
+        loads.start(r.buffer_near, r.near_out),
+        loads.start(r.buffer_far, r.far_out),
+        loads.start(pre_near, r.near_pre),
+        loads.start(out_grad, r.grad_out),
+    ]
+
+    def through_up(far, i, pre, rows_out):
+        back = dot(pre[i], w_up[far, i], (1, 1)).astype(LOW)
+        rows = slice(i * capacity, (i + 1) * capacity)
+        for g in range(2):
+            rows_out[g, rows] = back[g * capacity : (g + 1) * capacity]
+
+    for i in range(kept):
+        through_up(0, i, pre_near, rows_near)
+    for i in range(kept):
+        sent[i].wait_recv()
+        through_up(1, i, pre_far, rows_far)
+    stores.append(loads.start(pre_far, r.far_pre))
+    for g in range(2):
+        near = dot(pick_near[g], rows_near[g], (0, 0))
+        both = (near + dot(pick_far[g], rows_far[g], (0, 0))).astype(LOW)
+        r.back_part[g] = both.reshape(r.back_part.shape[1:])
+    return stores, bulk
+
+
+def back_part(place, links, chunks, bulk, r):
+    heads, f, y, z = place.heads, place.f, place.y, place.z
+    t, me = 2 * y + place.c, place.image(0, 0, 0)
+    part, gate_part, probs, valid = r.back_part, r.gate_rows, r.probs_own, r.valid_row
+    residual, gain, router, final_grad, tokens = (r.residual, r.gain, r.router, r.final_grad, r.tokens)
+    gain_one, second_in, projected, log_total, mixed = (r.gain_one, r.second_in, r.projected, r.log_total, r.mixed)
+    qkv, wo, tokens_grad, dense_out, gain_out = (r.qkv, r.wo, r.tokens_grad, r.dense_out, r.gain_out)
+    core_in, y_in, far, pair, x_in = (r.core_in, r.y_in, r.far, r.pair, r.x_in)
+    gate_in, gate_sum, gate_all, logit_rows, logit_grads = (r.gate_in, r.gate_sum, r.gate_all, r.logit_rows, r.logit_grads)
+    attended, first_in, projected_grad, first_part, dense = (r.attended, r.first_in, r.projected_grad, r.first_part, r.dense)
+    dense_core, xa, ya, yb, xb = (r.dense_core, r.xa, r.ya, r.yb, r.xb)
+    first_far, rounded, gain_part, gain_plane, gain_heads = (r.first_far, r.rounded, r.gain_part, r.gain_plane, r.gain_heads)
+    tensor_peers, owners = place.tensor_peers(), place.owners()
     rows_all, width = residual.shape
     half = width // 2
     own = rows_all // heads
@@ -1014,11 +1113,8 @@
     for k in range(chunks):
         source = part.at[:, :, 1 - place.c, :, pl.ds(k * 128, 128)]
         into[k] = links.send(source, core_in.at[k], place.core_peer)
-    cut = gates_a.shape[1]
-    gate_own[:, :cut] = gates_a[...]
-    gate_own[:, cut:] = gates_b[...]
-    gate_in[t] = gate_own[...]
-    shared = [links.send(gate_own, gate_in.at[t], d) for d in tensor_peers]
+    gate_in[t] = gate_part[...]
+    shared = [links.send(gate_part, gate_in.at[t], d) for d in tensor_peers]
     mine = pl.ds(pl.multiple_of(z * own, own), own)
 
     def to_y(k):
@@ -1082,9 +1178,25 @@
     logit_grads[...] = logit_grad.astype(LOW)
     logit_rows[...] = dot(logit_grads[...], router[...], (0, 0))
     normed, spread_two = normalize(residual[mine, :])
+    router_grad = dot(second_in[...], logit_grads[...], (0, 1))
+    spare = jnp.zeros((width, 128 - router_grad.shape[1]), WIDE)
+    router_grad = jnp.concatenate([router_grad, spare], 1).astype(LOW)
+    blocks, block = dense.shape[:2]
+    qkv_width = projected.shape[1]
+    dense_width = dense.shape[2]
+    dense[:, :, pl.ds(dense_width - 128, 128)] = router_grad.reshape(blocks, block, 128)
+
+    def first_norm(rows):
+        again, _ = normalize(tokens[rows, :].astype(WIDE))
+        first_in[rows, :] = (again * gain_one[...]).astype(LOW)
+
+    in_rows(rows_all, 64, first_norm)
     to_heads(chunks - 1)
     to_x(chunks - 2)
     to_x(chunks - 1)
+    early = r.w_far.shape[0] // 2
+    late = pl.ds(early, r.w_far.shape[0] - early)
+    bulk.append(links.send(r.w_far.at[late], r.down_far.at[late], place.x_peer))
     near = jnp.concatenate([pair[k, f].astype(WIDE) for k in range(chunks)], 1)
     for k in range(chunks):
         cross[k].wait_recv()
@@ -1093,112 +1205,75 @@
     rows_grad = jnp.concatenate([jnp.where(first, near, away), jnp.where(first, away, near)], 1)
     second_grad = rows_grad + logit_rows[mine, :]
     weighted = second_grad * gain[...]
-    gain_part[...] = jnp.sum((second_grad * normed).reshape(own // 8, 8, width), axis=0)
+    gain_part[1:2, :] = jnp.sum(second_grad * normed, 0, keepdims=True)
     inner = (
         weighted
         - jnp.mean(weighted, -1, keepdims=True)
         - normed * jnp.mean(weighted * normed, -1, keepdims=True)
     )
     total_grad = final_grad[...] + inner * spread_two
-    residual_grad[...] = total_grad
-    attended[z] = total_grad.astype(LOW)
-    for copy in all_heads(links, place, lambda k, to: (attended.at[z], attended.at[z])):
+    attended[mine, :] = total_grad.astype(LOW)
+    for copy in all_heads(
+        links, place, lambda k, to: (attended.at[mine], attended.at[mine])
+    ):
         copy.wait_recv()
-    links.drain()
-
-
-def back_through_norm(heads, part, gates_a, gates_b, residual, gain, router, probs, final_grad):
-    rows, width = residual.shape
-    own = rows // heads
-    chunks = width // 256
-    kept = gates_a.shape[1] + gates_b.shape[1]
-    group_rows = gates_a.shape[2]
-    return remote_call(
-        functools.partial(back_kernel, heads, chunks),
+
+    mixed_grad = dot(attended[...], wo[...].reshape(width, wo.shape[2])).astype(LOW)
+    head_count = log_total.shape[1]
+    size = qkv_width // head_count // 3
+    score_scale = size ** (-0.5)
+    keys_ok = valid[...] > 0
+    grads = []
+    for h in range(head_count):
+        at = 3 * h * size
+        query, key, value = (projected[:, at + n * size : at + (n + 1) * size] for n in range(3))
+        above = mixed_grad[:, h * size : (h + 1) * size]
+        scores = jnp.where(keys_ok, dot(query, key, (1, 1)) * score_scale, MASKED)
+        chances = jnp.exp(scores - log_total[:, h : h + 1])
+        prob_part = dot(above, value, (1, 1))
+        inner = jnp.sum(chances * prob_part, -1, keepdims=True)
+        score_grad = (chances * (prob_part - inner)).astype(LOW)
+        grads.append(dot(score_grad, key) * score_scale)
+        grads.append(dot(score_grad, query, (0, 0)) * score_scale)
+        grads.append(dot(chances.astype(LOW), above, (0, 0)))
+    projected_grad[...] = jnp.concatenate(grads, 1).astype(LOW)
+    weight = qkv[:, :, pl.ds(128, qkv_width)].reshape(width, qkv_width)
+    back = dot(projected_grad[...], weight, (1, 1))
+    first_part[...] = back.astype(LOW).reshape(heads, own, width)
+    along = all_heads(links, place, lambda n, to: (first_part.at[to], first_far.at[n]))
+    dense_now = jnp.concatenate(
         [
-            shape((heads, own, width)),
-            shape(probs.shape),
-            shape((own, width), WIDE),
-            shape((8, width), WIDE),
+            dot(first_in[...], projected_grad[...], (0, 0)).astype(LOW),
+            dot(attended[...], mixed[...], (0, 0)).astype(LOW),
         ],
-        [part, gates_a, gates_b, residual, gain, router, probs, final_grad],
-        [
-            pltpu.VMEM((chunks, 2, 2, rows, 128), LOW),
-            pltpu.VMEM((chunks, 2, rows, 128), LOW),
-            pltpu.VMEM((chunks, heads - 1, 2, own, 128), LOW),
-            pltpu.VMEM((chunks, 2, own, 128), LOW),
-            pltpu.VMEM((chunks, own, 128), LOW),
-            pltpu.VMEM((2, kept, group_rows), WIDE),
-            pltpu.VMEM((4, 2, kept, group_rows), WIDE),
-            pltpu.VMEM((2, kept, group_rows), WIDE),
-            pltpu.VMEM((heads, 2, kept, rows), WIDE),
-            pltpu.VMEM((rows, width), WIDE),
-        ],
-        chunks * (3 + heads - 1) + 3 + 2 * heads - 1 + heads - 1,
-        4,
-        20,
-        40,
-    )
-
-
-def last_kernel(
-    heads,
-    first_part,
-    dense,
-    tokens,
-    gain,
-    residual_grad,
-    gain_parts,
-    tokens_grad,
-    dense_out,
-    gain_out,
-    core_in,
-    xa,
-    ya,
-    yb,
-    xb,
-    far,
-    rounded,
-    tiles,
-    tiles_z,
-    ss,
-    rs,
-):
-    place = Place(heads)
-    links = Links(ss, rs)
-    z = place.z
-    me = place.image(0, 0, 0)
-    place.greet(place.plane_peers + place.z_peers)
-    own, width = residual_grad.shape
-    adder = PlaneSum(links, place, dense, core_in, xa, ya, yb, xb, xa.shape[2], 32)
+        1,
+    )
+    dense[:, :, pl.ds(0, dense_width - 128)] = dense_now.reshape(blocks, block, dense_width - 128)
+    adder = PlaneSum(links, place, dense, dense_core, xa, ya, yb, xb, xa.shape[2], 32)
     adder.start()
-    along = all_heads(links, place, lambda k, to: (first_part.at[to], far.at[k]))
-    tiles[me] = gain_parts[me]
-    small = []
-    for device in place.plane_peers:
-        to = (device[FSDP] if FSDP in device else place.f) * 4 + device[TENSOR]
-        small.append(links.send(gain_parts.at[to], tiles.at[me], device))
+    gain_part[0:1, :] = jnp.sum(back * normalize(tokens[...].astype(WIDE))[0], 0, keepdims=True)
+    gain_plane[me] = gain_part[...]
+    small = [links.send(gain_part, gain_plane.at[me], d) for d in place.plane_peers]
     adder.cores()
     adder.cross()
     for copy in small:
         copy.wait_recv()
-    tiles_z[z] = sum(tiles[i] for i in range(8))
-    gains = all_heads(links, place, lambda k, to: (tiles_z.at[z], tiles_z.at[z]))
-    mine = pl.ds(pl.multiple_of(z * own, own), own)
-    normed, spread = normalize(tokens[mine, :].astype(WIDE))
+    gain_heads[z] = sum(gain_plane[i] for i in range(8))
+    gains = all_heads(links, place, lambda n, to: (gain_heads.at[z], gain_heads.at[z]))
+    normed, spread_one = normalize(tokens[mine, :].astype(WIDE))
     for copy in along:
         copy.wait_recv()
     first_grad = first_part[z].astype(WIDE)
-    for k in range(heads - 1):
-        first_grad = first_grad + far[k].astype(WIDE)
-    weighted = first_grad * gain[...]
+    for n in range(heads - 1):
+        first_grad = first_grad + first_far[n].astype(WIDE)
+    weighted = first_grad * gain_one[...]
     inner = (
         weighted
         - jnp.mean(weighted, -1, keepdims=True)
         - normed * jnp.mean(weighted * normed, -1, keepdims=True)
     )
-    rounded[z] = (residual_grad[...] + inner * spread).astype(LOW)
-    along = all_heads(links, place, lambda k, to: (rounded.at[z], rounded.at[z]))
+    rounded[z] = (total_grad + inner * spread_one).astype(LOW)
+    along = all_heads(links, place, lambda n, to: (rounded.at[z], rounded.at[z]))
 
     def keep(rows, columns, values):
         dense_out[rows, columns] = values
@@ -1206,199 +1281,216 @@
     adder.finish(keep)
     for copy in gains:
         copy.wait_recv()
-    gain_out[...] = sum(tiles_z[i] for i in range(heads))
+    gain_out[...] = sum(gain_heads[i] for i in range(heads))
     for copy in along:
         copy.wait_recv()
     for i in range(heads):
         tokens_grad[i] = rounded[i].astype(WIDE)
+    for copy in bulk:
+        copy.wait_recv()
+
+
+def layer_kernel(heads, chunks, names, piece_names, *refs):
+    r = types.SimpleNamespace(**dict(zip(names, refs)))
+    place = Place(heads)
+    links = Links(r.send_sems, r.recv_sems)
+    loads = Loads(r.load_sems)
+    experts_part(place, links, loads, [getattr(r, n) for n in piece_names], r)
+    extra = combine_part(place, links, chunks, r)
+    stores, bulk = experts_back_part(place, links, loads, r)
+    for copy in extra:
+        copy.wait_recv()
+    back_part(place, links, chunks, bulk, r)
+    for copy in stores:
+        copy.wait()
     links.drain()
 
 
-def last_sums(heads, first_part, dense, tokens, gain, residual_grad, gain_parts):
-    own, width = residual_grad.shape
-    _, rows, wide = dense.shape
-    cut = 512 if wide == 896 else 128 * (wide // 256)
-    return remote_call(
-        functools.partial(last_kernel, heads),
-        [
-            shape((heads, own, width), WIDE),
-            shape((rows, wide), WIDE),
-            shape((8, 128), WIDE),
+def named_call(kernel, ins, outs, scratch, copies, loads, collective_id, vmem_mib, microseconds):
+    spaces = {False: pltpu.VMEM, True: pltpu.HBM}
+    names = [*ins, *outs, *scratch, "load_sems", "send_sems", "recv_sems"]
+    made = pl.pallas_call(
+        functools.partial(kernel, names),
+        out_shape=[o[0] for o in outs.values()],
+        in_specs=[pl.BlockSpec(memory_space=spaces[a[1]]) for a in ins.values()],
+        out_specs=[pl.BlockSpec(memory_space=spaces[o[1]]) for o in outs.values()],
+        scratch_shapes=[
+            *scratch.values(),
+            pltpu.SemaphoreType.DMA((loads,)),
+            pltpu.SemaphoreType.DMA((copies,)),
+            pltpu.SemaphoreType.DMA((copies,)),
         ],
-        [first_part, dense, tokens, gain, residual_grad, gain_parts],
-        [
-            *sum_scratch(rows, wide, cut),
-            pltpu.VMEM((heads - 1, own, width), LOW),
-            pltpu.VMEM((heads, own, width), LOW),
-            pltpu.VMEM((8, 8, 128), WIDE),
-            pltpu.VMEM((heads, 8, 128), WIDE),
+        compiler_params=pltpu.CompilerParams(
+            collective_id=collective_id,
+            has_side_effects=True,
+            vmem_limit_bytes=vmem_mib * 2**20,
+        ),
+        cost_estimate=spends(microseconds),
+    )(*[a[0] for a in ins.values()])
+    return types.SimpleNamespace(**dict(zip(outs, made)))
+
+
+def layer(heads, capacity, head_count, pieces, vmem, hbm):
+    rows, width = vmem["residual"].shape
+    own, half, chunks = rows // heads, width // 2, width // 256
+    local_experts, _, hidden_width = hbm["up"].shape
+    kept, pair, group_rows = local_experts // 2, 2 * capacity, 4 * rows
+    block = width // 8
+    qkv_width, mixed_width = vmem["projected"].shape[1], vmem["mixed"].shape[1]
+    dense_width = qkv_width + mixed_width + 128
+    cut = 128 * ((dense_width // 128 + 1) // 2)
+    late = kept - sum(piece.shape[0] for piece in pieces)
+    piece_names = [f"piece{n}" for n in range(len(pieces))]
+    ins = {name: (array, False) for name, array in vmem.items()}
+    ins.update({name: (array, True) for name, array in hbm.items()})
+    ins.update({name: (array, True) for name, array in zip(piece_names, pieces)})
+    outs = {
+        "result": (shape((heads, own, width)), False),
+        "loss": (shape((heads, 8, 128), WIDE), False),
+        "tokens_grad": (shape((heads, own, width), WIDE), False),
+        "dense_out": (shape((block, dense_width), WIDE), False),
+        "gain_out": (shape((2, width), WIDE), False),
+        "down_far": (shape((kept, hidden_width, half)), True),
+        "hidden_out": (shape((kept, pair, hidden_width)), True),
+        "near_out": (shape((kept, pair, half)), True),
+        "far_out": (shape((kept, pair, half)), True),
+        "near_pre": (shape((kept, pair, hidden_width)), True),
+        "far_pre": (shape((kept, pair, hidden_width)), True),
+        "grad_out": (shape((kept, pair, width)), True),
+    }
+    low = {
+        "pick_near": (2, kept * capacity, group_rows),
+        "pick_far": (2, kept * capacity, group_rows),
+        "buffer_near": (kept, pair, half),
+        "buffer_far": (kept, pair, half),
+        "hidden": (kept, pair, hidden_width),
+        "weighted": (2, kept * capacity, width),
+        "away": (kept, pair, hidden_width),
+        "arrived": (kept, pair, hidden_width),
+        "w_up": (2, kept, half, hidden_width),
+        "w_near": (kept, hidden_width, half),
+        "w_far": (kept, hidden_width, half),
+        "part": (2, 2, 2, rows, width),
+        "group": (8, rows, width),
+        "sum_core": (chunks, 2, 2, rows, 256),
+        "sum_xa": (chunks, 2, rows, 128),
+        "sum_ya": (chunks, rows, 128),
+        "sum_yb": (chunks, 2, rows, 128),
+        "sum_xb": (chunks, rows, 128),
+        "image_sum": (chunks, rows, 256),
+        "image_far": (chunks, heads - 1, own, 256),
+        "out_grad": (kept, pair, width),
+        "slot_rows": (pair, width),
+        "back_part": (2, 2, 2, rows, half),
+        "core_in": (chunks, 2, 2, rows, 128),
+        "y_in": (chunks, 2, rows, 128),
+        "far": (chunks, heads - 1, 2, own, 128),
+        "pair": (chunks, 2, own, 128),
+        "x_in": (chunks, own, 128),
+        "logit_grads": vmem["probs_own"].shape,
+        "attended": (rows, width),
+        "first_in": (rows, width),
+        "projected_grad": (rows, qkv_width),
+        "first_part": (heads, own, width),
+        "dense": (8, block, dense_width),
+        "dense_core": (4, block, dense_width),
+        "xa": (2, block, cut),
+        "ya": (block, cut),
+        "yb": (2, block, dense_width - cut),
+        "xb": (block, dense_width - cut),
+        "first_far": (heads - 1, own, width),
+        "rounded": (heads, own, width),
+    }
+    wide = {
+        "gates": (kept, pair, 1),
+        "own": (kept, pair, hidden_width),
+        "final_grad": (own, width),
+        "gate_rows": (2, kept, group_rows),
+        "gate_in": (4, 2, kept, group_rows),
+        "gate_sum": (2, kept, group_rows),
+        "gate_all": (heads, 2, kept, rows),
+        "logit_rows": (rows, width),
+        "gain_part": (2, width),
+        "gain_plane": (8, 2, width),
+        "gain_heads": (heads, 2, width),
+    }
+    scratch = {name: pltpu.VMEM(dims, LOW) for name, dims in low.items()}
+    scratch.update({name: pltpu.VMEM(dims, WIDE) for name, dims in wide.items()})
+    copies = kept + late + chunks * (5 + GATHER_COPIES + 2 * (heads - 1)) + 2 * (heads - 1)
+    copies += kept + 2 + chunks * (3 + heads - 1) + 3 + 2 * heads - 1 + heads - 1
+    copies += SUM_COPIES + 3 * (heads - 1) + 7
+    return named_call(
+        lambda names, *refs: layer_kernel(heads, chunks, names, piece_names, *refs),
+        ins,
+        outs,
+        scratch,
+        copies,
+        3 * kept + len(pieces) + 6,
+        3,
+        54,
+        190,
+    )
+
+
+def finish_kernel(s, near, near_pre, far, far_pre, hidden, out_grad, *refs):
+    pieces, (up, down) = refs[:-2], refs[-2:]
+    i = pl.program_id(0)
+    kept, half = pl.num_programs(0) // 2, down.shape[2]
+    j = i - s[1]
+    held = (j >= 0) & (j < kept)
+
+    @pl.when(held)
+    def _():
+        up[0] = dot(near[0], near_pre[0], (0, 0))
+        columns = pl.ds(pl.multiple_of(s[0] * half, half), half)
+        down[0] = dot(hidden[0], out_grad[0, :, columns], (0, 0))
+
+    @pl.when(jnp.logical_not(held))
+    def _():
+        up[0] = dot(far[0], far_pre[0], (0, 0))
+
+    at = 0
+    for piece in pieces:
+        for k in range(piece.shape[0]):
+
+            @pl.when(i - s[2] == at + k)
+            def _(piece=piece, k=k):
+                down[0] = piece[k].astype(WIDE)
+
+        at += piece.shape[0]
+
+
+def finish(scalars, near, near_pre, far, far_pre, hidden, out_grad, arrived):
+    kept, _, half = near.shape
+    hidden_width = near_pre.shape[2]
+
+    def of(array, which):
+        return pl.BlockSpec(
+            (1, *array.shape[1:]), lambda i, s: (jnp.clip(i - s[which], 0, kept - 1), 0, 0)
+        )
+
+    def all_of(array):
+        return pl.BlockSpec(array.shape, lambda i, s: (0, 0, 0))
+
+    ins = [(near, 1), (near_pre, 1), (far, 2), (far_pre, 2), (hidden, 1), (out_grad, 1)]
+    return pl.pallas_call(
+        finish_kernel,
+        out_shape=[
+            shape((2 * kept, half, hidden_width), WIDE),
+            shape((2 * kept, hidden_width, half), WIDE),
         ],
-        SUM_COPIES + 3 * (heads - 1) + 7,
-        5,
-        48,
-        25,
-    )
-
-
-def local_call(
-    kernel, grid, scalars, ins, outs, scratch=(), vmem_mib=28, aliases=None, microseconds=5
-):
-    def spec(array, block, index):
-        if block is None:
-            dims = array.shape
-            return pl.BlockSpec(dims, lambda i, s, n=len(dims): (0,) * n)
-        if block is pl.ANY:
-            return pl.BlockSpec(memory_space=pl.ANY)
-        return pl.BlockSpec(block, index)
-
-    return pl.pallas_call(
-        kernel,
-        out_shape=[o[0] for o in outs],
         grid_spec=pltpu.PrefetchScalarGridSpec(
             num_scalar_prefetch=1,
-            grid=(grid,),
-            in_specs=[spec(*a) for a in ins],
-            out_specs=[spec(*o) for o in outs],
-            scratch_shapes=list(scratch),
+            grid=(2 * kept,),
+            in_specs=[of(*a) for a in ins] + [all_of(piece) for piece in arrived],
+            out_specs=[
+                pl.BlockSpec((1, half, hidden_width), lambda i, s: (i, 0, 0)),
+                pl.BlockSpec((1, hidden_width, half), lambda i, s: (i, 0, 0)),
+            ],
         ),
-        input_output_aliases=aliases or {},
-        compiler_params=pltpu.CompilerParams(vmem_limit_bytes=vmem_mib * 2**20),
-        cost_estimate=spends(microseconds),
-    )(scalars, *[a[0] for a in ins])
-
-
-def per_expert(dims, skip=0):
-    return (1, *dims), lambda i, s: (i + skip, 0, 0)
-
-
-def held_expert(dims, which, skip=0):
-    return (1, *dims), lambda i, s: (s[which] + i + skip, 0, 0)
-
-
-def slot_block(dims, skip=0):
-    return (2, *dims), lambda i, s: (0, i + skip, 0)
-
-
-def dot(a, b, over=(1, 0)):
-    return lax.dot_general(a, b, (((over[0],), (over[1],)), ((), ())), preferred_element_type=WIDE)
-
-
-def one_hot(slots, row, capacity):
-    places = lax.broadcasted_iota(jnp.int32, (capacity, slots.shape[1]), 0)
-    return places == slots[pl.ds(row, 1), :]
-
-
-def far_up_kernel(skip, s, slots, x, up, pick, buffer, away):
-    i, local_experts = pl.program_id(0) + skip, slots.shape[0] // 2
-    capacity = pick.shape[1]
-    for g in range(2):
-        hot = one_hot(slots, g * local_experts + s[1] + i, capacity).astype(LOW)
-        pick[g] = hot
-        buffer[0, pl.ds(g * capacity, capacity), :] = dot(hot, x[g]).astype(LOW)
-    away[0] = dot(buffer[0], up[0]).astype(LOW)
-
-
-def near_up_kernel(s, slots, x, up, probs, pick, buffer, own, gates):
-    i, local_experts = pl.program_id(0), slots.shape[0] // 2
-    capacity = pick.shape[1]
-    expert = s[3] + i
-    for g in range(2):
-        hot = one_hot(slots, g * local_experts + s[0] + i, capacity)
-        chances = jnp.concatenate([probs[4 * g + k, pl.ds(expert, 1), :] for k in range(4)], 1)
-        rows = pl.ds(g * capacity, capacity)
-        gates[0, rows, :] = jnp.sum(jnp.where(hot, chances, 0.0), -1, keepdims=True)
-        pick[g] = hot.astype(LOW)
-        buffer[0, rows, :] = dot(hot.astype(LOW), x[g]).astype(LOW)
-    own[0] = dot(buffer[0], up[0])
-
-
-def down_kernel(last, s, own, arrived, gates, near, far, *refs):
-    if last:
-        before, pick, hidden, slope, part, weighted = refs
-    else:
-        hidden, slope, weighted = refs
-    i = pl.program_id(0)
-    half = near.shape[2]
-    capacity = own.shape[1] // 2
-    values = own[0] + arrived[0].astype(WIDE)
-    cdf = 0.5 * (1.0 + lax.erf(values * ROOT_HALF))
-    hidden[0] = (values * cdf).astype(LOW)
-    slope[0] = cdf + values * DENSITY * jnp.exp(-0.5 * values * values)
-    for weight, f in ((near, s[2]), (far, 1 - s[2])):
-        out = (dot(hidden[0], weight[0]) * gates[0]).astype(LOW)
-        columns = pl.ds(pl.multiple_of(f * half, half), half)
-        for g in range(2):
-            rows = pl.ds(pl.multiple_of(i * capacity, capacity), capacity)
-            weighted[g, rows, columns] = out[g * capacity : (g + 1) * capacity]
-
-    if last:
-
-        @pl.when(i == pl.num_programs(0) - 1)
-        def _():
-            cut = before.shape[1]
-            for g in range(2):
-                total = dot(pick[g, :cut], before[g], (0, 0))
-                part[g] = (total + dot(pick[g, cut:], weighted[g], (0, 0))).astype(LOW)
-
-
-def hidden_back_kernel(
-    s, pick, grads, near, far, hidden, slope, gates, pre, out_grad, gate_rows, rows
-):
-    i = pl.program_id(0)
-    half = near.shape[2]
-    capacity = pick.shape[1]
-    for g in range(2):
-        rows[pl.ds(g * capacity, capacity), :] = dot(pick[g], grads[g]).astype(LOW)
-    first = pl.ds(pl.multiple_of(s[2] * half, half), half)
-    second = pl.ds(pl.multiple_of((1 - s[2]) * half, half), half)
-    raw = dot(rows[:, first], near[0], (1, 1)) + dot(rows[:, second], far[0], (1, 1))
-    pre[0] = (raw * gates[0] * slope[0]).astype(LOW)
-    out_grad[0] = (rows[...].astype(WIDE) * gates[0]).astype(LOW)
-    gate_grad = jnp.sum(raw * hidden[0].astype(WIDE), -1, keepdims=True)
-    for g in range(2):
-        terms = gate_grad[g * capacity : (g + 1) * capacity] * pick[g].astype(WIDE)
-        gate_rows[g, pl.ds(i, 1), :] = jnp.sum(terms, 0, keepdims=True)
-
-
-def down_grad_kernel(s, hidden, out_grad, *refs):
-    kept_grad, sent_grad = refs[-2:]
-    half = kept_grad.shape[2]
-    first = pl.ds(pl.multiple_of(s[2] * half, half), half)
-    second = pl.ds(pl.multiple_of((1 - s[2]) * half, half), half)
-    kept_grad[0] = dot(hidden[0], out_grad[0, :, first], (0, 0))
-    sent_grad[0] = dot(hidden[0], out_grad[0, :, second], (0, 0)).astype(LOW)
-
-
-def up_back_kernel(s, buffer, pre, up, *refs):
-    grad, rows_out = refs[-2:]
-    capacity = rows_out.shape[1]
-    grad[0] = dot(buffer[0], pre[0], (0, 0))
-    back = dot(pre[0], up[0], (1, 1)).astype(LOW)
-    for g in range(2):
-        rows_out[g] = back[g * capacity : (g + 1) * capacity]
-
-
-def far_up_last_kernel(s, buffer, pre, up, rows_near, before, pick_near, pick_far, held, grad, part, rows_far):
-    i = pl.program_id(0)
-    capacity = buffer.shape[1] // 2
-    grad[0] = dot(buffer[0], pre[0], (0, 0))
-    back = dot(pre[0], up[0], (1, 1)).astype(LOW)
-    for g in range(2):
-        rows = pl.ds(pl.multiple_of(i * capacity, capacity), capacity)
-        rows_far[g, rows, :] = back[g * capacity : (g + 1) * capacity]
-
-    @pl.when(i == pl.num_programs(0) - 1)
-    def _():
-        cut = before.shape[1]
-        for g in range(2):
-            near = dot(pick_near[g], rows_near[g], (0, 0))
-            far = dot(pick_far[g, :cut], before[g], (0, 0))
-            far = far + dot(pick_far[g, cut:], rows_far[g], (0, 0))
-            part[g] = (near + far).astype(LOW)
-
-
-def widen_kernel(s, arrived, held, grad):
-    grad[0] = arrived[0].astype(WIDE)
+        compiler_params=pltpu.CompilerParams(vmem_limit_bytes=60 * 2**20),
+        cost_estimate=spends(8),
+    )(scalars, *[a[0] for a in ins], *arrived)
 
 
 def swap(values):
@@ -1460,6 +1552,7 @@
         (gathered, lax.dynamic_slice_in_dim(expert_down, theirs + first_chunk, second_chunk, 0))
     )
     down_b = swap(down_b)
+    gathered_blocks = gathered
     gathered = gathered.reshape(width, -1)
     qkv_full = gathered[:, 128 : 128 + qkv_width]
     lanes = jnp.arange(128)
@@ -1511,286 +1604,57 @@
     )
     group_in, down_b = lax.optimization_barrier((group_in, down_b))
 
-    hidden_width = expert_up.shape[2]
-    pair = 2 * capacity
-    scalars = jnp.stack([mine, theirs, f, z * local_experts + mine]).astype(jnp.int32)
     rows_in = group_in.reshape(2, group_rows, half)
-    a_pick = shape((2, kept * capacity, group_rows)), *slot_block((capacity, group_rows))
-    a_buffer = shape((kept, pair, half)), *per_expert((pair, half))
-    near_up = expert_up, *held_expert((half, hidden_width), 0)
-    part_size = kept // 2
-    a_hidden = per_expert((pair, hidden_width))
-    halves = (0, part_size)
-    picks_far, buffers_far, arrived = [], [], []
-    for skip in halves:
-        pick, buffer, away = local_call(
-            functools.partial(far_up_kernel, skip),
-            part_size,
-            scalars,
-            [
-                (slots, None, None),
-                (rows_in, None, None),
-                (expert_up, *held_expert((half, hidden_width), 1, skip)),
-            ],
-            [
-                (
-                    shape((2, part_size * capacity, group_rows)),
-                    *slot_block((capacity, group_rows)),
-                ),
-                (shape((part_size, pair, half)), *per_expert((pair, half))),
-                (shape((part_size, pair, hidden_width)), *a_hidden),
-            ],
-        )
-        away, scalars = lax.optimization_barrier((away, scalars))
-        picks_far.append(pick)
-        buffers_far.append(buffer)
-        arrived.append(swap(away))
-    down_far = jnp.concatenate([down_a, down_b, down_c], 0)
-    pick_near, buffer_near, own, gates = local_call(
-        near_up_kernel,
-        kept,
+    pieces = [down_a, down_b, down_c]
+    me = f * 4 + lax.axis_index(TENSOR)
+    valid_rows = valid_mask[0].astype(WIDE)[:, None]
+    vmem = {
+        "slots": slots,
+        "x": rows_in,
+        "probs": probs_all,
+        "residual": residual,
+        "teacher": teacher[0],
+        "valid": valid_rows,
+        "scale": jnp.full((8, 128), total_tokens / valid_total, WIDE),
+        "gain": gain_b,
+        "router": router_wide[:, :expert_count].T,
+        "probs_own": lax.dynamic_index_in_dim(probs_all, me, 0, False),
+        "tokens": tokens[0],
+        "gain_one": gain_a,
+        "second_in": second_in,
+        "projected": projected.reshape(rows, qkv_width),
+        "log_total": logarithm_total.reshape(head_count, rows).T,
+        "mixed": mixed,
+        "valid_row": valid_mask,
+        "qkv": gathered_blocks,
+        "wo": lax.dynamic_index_in_dim(wo_all, z, 1, False),
+    }
+    hbm = {"up": expert_up, "down": expert_down}
+    made = layer(heads, capacity, head_count, pieces, vmem, hbm)
+    result, tokens_grad, dense_out = made.result, made.tokens_grad, made.dense_out
+    loss_terms = (jnp.sum(made.loss) * (total_images / (valid_total * width)))[None]
+    own_gains = lax.dynamic_slice_in_dim(made.gain_out, me * block, block, 1)
+    scalars = jnp.stack([f, mine, theirs]).astype(jnp.int32)
+    up_grad, down_grad = finish(
         scalars,
-        [(slots, None, None), (rows_in, None, None), near_up, (probs_all, None, None)],
-        [
-            a_pick,
-            a_buffer,
-            (shape((kept, pair, hidden_width), WIDE), *per_expert((pair, hidden_width))),
-            (shape((kept, pair, 1), WIDE), *per_expert((pair, 1))),
-        ],
-    )
-    hiddens, slopes, weighted = [], [], []
-    for n, skip in enumerate(halves):
-        ins = [
-            (own, *per_expert((pair, hidden_width), skip)),
-            (arrived[n], *a_hidden),
-            (gates, *per_expert((pair, 1), skip)),
-            (expert_down, *held_expert((hidden_width, half), 0, skip)),
-            (down_far, *per_expert((hidden_width, half), skip)),
-        ]
-        outs = [
-            (shape((part_size, pair, hidden_width)), *a_hidden),
-            (shape((part_size, pair, hidden_width), WIDE), *a_hidden),
-        ]
-        rows_shape = (2, part_size * capacity, width)
-        last = n == 1
-        if last:
-            ins += [(weighted[0], None, None), (pick_near, None, None)]
-            outs.append((shape((2, group_rows, width)), None, None))
-        else:
-            outs.append((shape(rows_shape), None, None))
-        scratch = [pltpu.VMEM(rows_shape, LOW)] if last else []
-        hidden, slope, out = local_call(
-            functools.partial(down_kernel, last), part_size, scalars, ins, outs, scratch
-        )
-        hiddens.append(hidden)
-        slopes.append(slope)
-        weighted.append(out)
-    part = weighted[1]
-    me = f * 4 + lax.axis_index(TENSOR)
-    probs_own = lax.dynamic_index_in_dim(probs_all, me, 0, False)
-
-    valid_rows = valid_mask[0].astype(WIDE)[:, None]
-    scale = jnp.full((8, 128), total_tokens / valid_total, WIDE)
-    result, final_grad, group_grad, loss = combine(
-        heads, part.reshape(2, 2, 2, rows, width), residual, teacher[0], valid_rows, scale
-    )
-    loss_terms = (jnp.sum(loss) * (total_images / (valid_total * width)))[None]
-
-    grads_in = group_grad.reshape(2, group_rows, width)
-    pres_near, pres_far, out_grads, extras = [], [], [], []
-    for n, skip in enumerate(halves):
-        pre, out_grad, extra = local_call(
-            hidden_back_kernel,
-            part_size,
-            scalars,
-            [
-                (pick_near, *slot_block((capacity, group_rows), skip)),
-                (grads_in, None, None),
-                (expert_down, *held_expert((hidden_width, half), 0, skip)),
-                (down_far, *per_expert((hidden_width, half), skip)),
-                (hiddens[n], *a_hidden),
-                (slopes[n], *a_hidden),
-                (gates, *per_expert((pair, 1), skip)),
-            ],
-            [
-                (shape((part_size, pair, hidden_width)), *a_hidden),
-                (shape((part_size, pair, width)), *per_expert((pair, width))),
-                (shape((2, part_size, group_rows), WIDE), None, None),
-            ],
-            [pltpu.VMEM((pair, width), LOW)],
-        )
-        pre, scalars = lax.optimization_barrier((pre, scalars))
-        pres_near.append(pre)
-        pres_far.append(swap(pre))
-        out_grads.append(out_grad)
-        extras.append(extra)
-    down_shape = shape(expert_down.shape, WIDE)
-    up_shape = shape(expert_up.shape, WIDE)
-    down_grad, sends = None, []
-    pieces = ((0, 0, part_size), (1, 0, part_size - 1), (1, part_size - 1, 1))
-    for n, skip, size in pieces:
-        ins = [
-            (hiddens[n], *per_expert((pair, hidden_width), skip)),
-            (out_grads[n], *per_expert((pair, width), skip)),
-        ]
-        if sends:
-            ins.append((down_grad, pl.ANY, None))
-        first = n * part_size + skip
-        down_grad, send = local_call(
-            down_grad_kernel,
-            size,
-            scalars,
-            ins,
-            [
-                (down_shape, *held_expert((hidden_width, half), 0, first)),
-                (shape((size, hidden_width, half)), *per_expert((hidden_width, half))),
-            ],
-            aliases={3: 0} if sends else None,
-            microseconds=2 * size,
-        )
-        sends.append(send)
-    down_others = [swap(send) for send in sends[:2]]
-    up_grad, rows_near = None, []
-    for n, skip in enumerate(halves):
-        ins = [
-            (buffer_near, *per_expert((pair, half), skip)),
-            (pres_near[n], *a_hidden),
-            (expert_up, *held_expert((half, hidden_width), 0, skip)),
-        ]
-        if n:
-            ins.append((up_grad, pl.ANY, None))
-        up_grad, out = local_call(
-            up_back_kernel,
-            part_size,
-            scalars,
-            ins,
-            [
-                (up_shape, *held_expert((half, hidden_width), 0, skip)),
-                (shape((2, part_size * capacity, half)), *slot_block((capacity, half))),
-            ],
-            aliases={4: 0} if n else None,
-        )
-        rows_near.append(out)
-    rows_near = jnp.concatenate(rows_near, 1)
-
-    def far_ins(n, skip):
-        return [
-            (buffers_far[n], *per_expert((pair, half))),
-            (pres_far[n], *a_hidden),
-            (expert_up, *held_expert((half, hidden_width), 1, skip)),
-        ]
-
-    up_grad, rows_far = local_call(
-        up_back_kernel,
-        part_size,
-        scalars,
-        [*far_ins(0, 0), (up_grad, pl.ANY, None)],
-        [
-            (up_shape, *held_expert((half, hidden_width), 1)),
-            (shape((2, part_size * capacity, half)), *slot_block((capacity, half))),
-        ],
-        aliases={4: 0},
-    )
-    up_grad, back_part = local_call(
-        far_up_last_kernel,
-        part_size,
-        scalars,
-        [
-            *far_ins(1, part_size),
-            (rows_near, None, None),
-            (rows_far, None, None),
-            (pick_near, None, None),
-            (jnp.concatenate(picks_far, 1), None, None),
-            (up_grad, pl.ANY, None),
-        ],
-        [
-            (up_shape, *held_expert((half, hidden_width), 1, part_size)),
-            (shape((2, group_rows, half)), None, None),
-        ],
-        [pltpu.VMEM((2, part_size * capacity, half), LOW)],
-        aliases={8: 0},
-    )
-    back_part = back_part.reshape(2, 2, 2, rows, half)
-
-    attended, logit_grads, residual_grad, gain_two_part = back_through_norm(
-        heads,
-        back_part,
-        extras[0],
-        extras[1],
-        residual,
-        gain_b,
-        router_wide[:, :expert_count].T,
-        probs_own,
-        final_grad,
-    )
-
-    attended, last_send = lax.optimization_barrier((attended, sends[2]))
-    down_others.append(swap(last_send))
-    attended_grad = attended.reshape(rows, width)
-    wo_own = lax.dynamic_index_in_dim(wo_all, z, 1, False).reshape(width, -1)
-    mixed_grad = (
-        jnp.dot(attended_grad, wo_own, preferred_element_type=WIDE)
-        .astype(LOW)
-        .reshape(rows, head_count, head_dim)
-    )
-    scores = scores_now()
-    probs = jnp.exp(scores - logarithm_total)
-    prob_part = jnp.einsum("qhe,khe->hqk", mixed_grad, values, preferred_element_type=WIDE)
-    score_grad = (probs * (prob_part - jnp.sum(probs * prob_part, -1, keepdims=True))).astype(LOW)
-    query_grad = (
-        jnp.einsum("hqk,khe->qhe", score_grad, key_rows, preferred_element_type=WIDE) * score_scale
-    )
-    key_grad = (
-        jnp.einsum("hqk,qhe->khe", score_grad, queries, preferred_element_type=WIDE) * score_scale
-    )
-    value_grad = jnp.einsum(
-        "hqk,qhe->khe", probs.astype(LOW), mixed_grad, preferred_element_type=WIDE
-    )
-    projected_grad = (
-        jnp.concatenate([query_grad, key_grad, value_grad], -1)
-        .astype(LOW)
-        .reshape(rows, qkv_width)
-    )
-    first_part = lax.dot_general(
-        projected_grad, qkv_full, (((1,), (1,)), ((), ())), preferred_element_type=WIDE
-    )
-    gain_one_part = jnp.sum(first_part * normed_one, 0)
-    qkv_grad = jnp.einsum("sd,se->de", first_in, projected_grad, preferred_element_type=WIDE)
-    out_grad_t = jnp.einsum("sd,se->de", attended_grad, mixed, preferred_element_type=WIDE)
-    router_grad = dot(second_in, logit_grads, (0, 1))
-    spare = jnp.zeros((width, -(qkv_width + out_grad_t.shape[1] + expert_count) % 128), WIDE)
-    dense = jnp.concatenate([qkv_grad, out_grad_t, router_grad, spare], 1).astype(LOW)
-    gain_parts = jnp.stack([gain_one_part, jnp.sum(gain_two_part, 0)], 0).reshape(2, 8, block)
-    gain_parts = jnp.pad(jnp.swapaxes(gain_parts, 0, 1), ((0, 0), (0, 6), (0, 128 - block)))
-    tokens_grad, dense_out, gain_out = last_sums(
-        heads,
-        first_part.astype(LOW).reshape(heads, rows // heads, width),
-        dense.reshape(8, block, -1),
-        tokens[0],
-        gain_a,
-        residual_grad,
-        gain_parts,
-    )
-    for arrived, (n, skip, size) in zip(down_others, pieces):
-        (down_grad,) = local_call(
-            widen_kernel,
-            size,
-            scalars,
-            [(arrived, *per_expert((hidden_width, half))), (down_grad, pl.ANY, None)],
-            [(down_shape, *held_expert((hidden_width, half), 1, n * part_size + skip))],
-            aliases={2: 0},
-            microseconds=2 * size,
-        )
+        made.near_out,
+        made.near_pre,
+        made.far_out,
+        made.far_pre,
+        made.hidden_out,
+        made.grad_out,
+        [made.down_far],
+    )
     out_width = head_count * head_dim
     return (
         result.reshape(1, rows, width),
         loss_terms,
         tokens_grad.reshape(1, rows, width),
-        gain_out[0, :block],
+        own_gains[0],
         dense_out[:, :qkv_width].reshape(block, head_count, qkv_dim),
         dense_out[:, qkv_width : qkv_width + out_width].T.reshape(head_count, head_dim, block),
-        gain_out[1, :block],
-        dense_out[:, qkv_width + out_width : qkv_width + out_width + expert_count],
+        own_gains[1],
+        dense_out[:, qkv_width + out_width :][:, :expert_count],
         up_grad,
         down_grad,
     )

time: 329 us -> 315 us (0.957)
  Pallas kernels: 225 us -> 273 us
  waiting for transfers between devices: 35 us -> 5.1 us
  local copies, waits for them, and re-layouts: 36.9 us -> 23.4 us
  starting transfers between devices: 10.7 us -> 3.64 us
  other arithmetic: 11.1 us -> 4.89 us
  matrix products: 5.07 us -> 1.18 us
    pallas_call x17 -> x2, Pallas kernels: 57.2 us -> 209 us  [the longest x1 196 us: named_call(): pl.pallas_call(functools.partial(kernel, names), out_shape=[o[0] for o in...]
    pallas_call x5 -> x2, Pallas kernels: 168 us -> 63.5 us  [remote_call(): pl.pallas_call(kernel, out_shape=outs, in_specs=[hbm if i in in_hbm else...]
    ppermute x9 -> x2, waiting for transfers between devices: 35 us -> 5.1 us  [swap(): return lax.ppermute(values, FSDP, [(0, 1), (1, 0)])]
    unnamed x127 -> x44, local copies, waits for them, and re-layouts: 27 us -> 6.41 us
    ppermute x9 -> x2, starting transfers between devices: 10.7 us -> 3.64 us  [swap(): return lax.ppermute(values, FSDP, [(0, 1), (1, 0)])]
    dot_general x9 -> x0, matrix products: 3.88 us -> none  [the longest x1 1.5 us: fast(): jnp.einsum('sd,se->de', first_in, projected_grad, preferred_element_type=...]
    concatenate x3 -> x0, other arithmetic: 3.59 us -> none  [the longest x1 3.06 us: fast(): jnp.concatenate(picks_far, 1)]
  transfers between devices with their start and end apart: 9 -> 2, of which waited for: 3 -> 1; matrix products, arithmetic and copies ran while one was open for 9% -> 4% of each run, Pallas kernels for 42% -> 14%
where the time goes in v3:
time: 315 us
  Pallas kernels  273 us (87%)
  local copies, waits for them, and re-layouts  23.4 us (7%)
  waiting for transfers between devices  5.1 us (2%)
  other arithmetic  4.89 us (2%)
  starting transfers between devices  3.64 us (1%)
  between operations  3.5 us (1%)
    pallas_call x1, Pallas kernels, named_call(): pl.pallas_call(functools.partial(kernel, names), out_shape=[o[0] for o in...  196 us
    pallas_call x2, Pallas kernels, remote_call(): pl.pallas_call(kernel, out_shape=outs, in_specs=[hbm if i in in_hbm else...  63.5 us
    pallas_call x1, Pallas kernels, finish(): pl.pallas_call(finish_kernel, out_shape=[shape((2 * kept, half, hidden_wi...  13.8 us
    unnamed x44, local copies, waits for them, and re-layouts  6.41 us
  transfers between devices with their start and end apart: 2, of which 1 were waited for; matrix products, arithmetic and copies ran while one was open for 4% of the time, Pallas kernels for 14%

profile of v3, /device:TPU:0, one launch (start us, length us, event | category | flops | bytes accessed | tf_op | source)
XLA Modules:
  0.0 314.5 jit_solution(411859575321104804)
XLA Ops:
  0.7 1.2 constant_dynamic-slice_fusion.2
  1.9 3.0 collective-permute-start
  4.9 1.4 convert_bitcast_fusion
  6.3 0.7 compare_reduce_fusion
  7.0 1.1 copy.102
  8.1 0.2 copy.106
  8.8 0.1 convert_reduce_fusion
  8.9 0.8 copy.114.refs_5_
  9.8 0.6 pad_add_fusion.s
  10.5 0.2 fusion.4
  10.7 2.4 constant_dynamic-slice_fusion.1
  13.1 5.1 %collective-permute-done.refs_21_ = bf16[1,768,384]{2,1,0:T(8,128)(2,1)S(1)} collective-permute-done((bf16[1,768,384]{2,1,0:T(8,128)(2,1)S(1)}, bf16[1,768,384]{2,1,0:T(8,128)(2,1)S(1)}, u32[]{:S(2)}, u32[]{:S(2)}) %collective-permute-start) | collective-permute-done | bytes 589856 | tf_op jit(solution)/shard_map/ppermute | solution.py:1497
  18.2 0.6 broadcast_in_dim.54.count
  18.9 0.2 copy-done.11
  19.1 20.2 %shard_map.186 = (bf16[8,96,768]{2,1,0:T(8,128)(2,1)S(1)}, bf16[8,4,96,192]{3,2,1,0:T(8,128)(2,1)S(1)}, s32[8,8,128]{2,1,0:T(8,128)S(1)}, s32[8,1024]{1,0:T(8,128)S(1)}) custom-call(bf16[96,768]{1,0:T(8,128)(2,1)S(1)} %concatenate.3.wq, bf16[96,192]{1,0:T(8,128)(2,1)S(1)} %bitcast.51, s32[8,128]{1,0:T(8,128)S(1)} %broadcast_in_dim.54.count, ...), custom_call_target="tpu_custom_call" | custom-call | bytes 60000000 | tf_op jit(solution)/shard_map/pallas_call | solution.py:573
  39.3 0.3 convert_reduce_fusion.1
  39.6 0.6 reshape.124.refs_11_
  40.3 0.6 convolution_convert_fusion
  40.9 0.6 collective-permute-start.1
  41.5 0.9 copy.115.refs_13_
  42.4 0.3 fusion.16
  42.9 0.8 copy.113
  43.7 0.2 convolution_convert_fusion.1
  44.1 0.1 copy.122
  44.3 0.2 copy.112.router
  44.5 0.6 slice_reduce_fusion
  45.9 43.3 %shard_map.187 = (f32[256,768]{1,0:T(8,128)S(1)}, bf16[256,768]{1,0:T(8,128)(2,1)S(1)}, bf16[8,256,384]{2,1,0:T(8,128)(2,1)S(1)}, f32[8,32,256]{2,1,0:T(8,128)S(...) custom-call(bf16[256,192]{1,0:T(8,128)(2,1)S(1)} %copy.111.mixed.refs_15_, ...), custom_call_target="tpu_custom_call" | custom-call | bytes 78000000 | tf_op jit(solution)/shard_map/pallas_call | solution.py:573
  89.2 1.1 copy-done.2
  90.3 0.8 copy-done.5
  91.2 0.7 copy-done.6
  91.9 0.7 dynamic-slice_bitcast_fusion.1.refs_9_
  92.6 0.8 dynamic-slice_bitcast_fusion.refs_18_
  93.4 0.6 slice_bitcast_fusion.1.refs_8_
  94.0 0.6 broadcast_in_dim.60.refs_6_
  94.6 195.6 %shard_map.188 = (bf16[4,64,768]{2,1,0:T(8,128)(2,1)}, f32[4,8,128]{2,1,0:T(8,128)}, f32[4,64,768]{2,1,0:T(8,128)}, f32[96,896]{1,0:T(8,128)}, f32[2,768]{1,0:T(...) custom-call(s32[16,1024]{1,0:T(8,128)} %copy-done.8, ...), custom_call_target="tpu_custom_call" | custom-call | bytes 570000000 | tf_op jit(solution)/shard_map/pallas_call | solution.py:1312
  290.2 1.0 slice.54
  291.2 1.0 slice_bitcast_fusion
  292.2 0.8 slice.57
  293.0 0.1 copy.117
  293.1 0.9 copy.119
  294.0 0.7 copy.118
  294.7 0.7 copy.120
  295.4 0.8 constant_dynamic-slice_fusion
  296.2 0.5 slice_bitcast_fusion.2
  296.7 0.6 reduce_sum.59
  298.0 13.8 %shard_map.189 = (f32[8,384,768]{2,1,0:T(8,128)}, f32[8,768,384]{2,1,0:T(8,128)}) custom-call(s32[3]{0:T(128)} %pad_add_fusion.s, bf16[4,256,384]{2,1,0:T(8,128)(2,1)} %get-tuple-element.65.near, bf16[4,256,768]{2,1,0:T(8,128)(2,1)} %get-tuple-element.66.near_pre, bf16[4,256,384]{2,1,0:T(8,128)(2,1)} %get-tuple-element.67.far, ...), custom_call_target="tpu_custom_call" | custom-call | bytes 24000000 | tf_op jit(solution)/shard_map/pallas_call | solution.py:1476
  311.8 0.7 copy.125
  312.5 0.9 copy.126
  (52 shorter events, 1.0 us)
Async XLA Ops:
  0.6 7.6 %copy-start.15 = (bf16[96,32]{0,1:T(8,128)(2,1)S(1)}, bf16[96,32]{0,1:T(8,128)(2,1)}, u32[]{:S(2)}) copy-start(bf16[96,32]{0,1:T(8,128)(2,1)} %param.19) | copy-start | bytes 18436
  0.7 7.7 %copy-start.17 = (bf16[96]{0:T(256)(128)(2,1)S(1)}, bf16[96]{0:T(256)(128)(2,1)}, u32[]{:S(2)}) copy-start(bf16[96]{0:T(256)(128)(2,1)} %param.15) | copy-start | bytes 580
  0.7 7.8 %copy-start.18 = (bf16[96]{0:T(256)(128)(2,1)S(1)}, bf16[96]{0:T(256)(128)(2,1)}, u32[]{:S(2)}) copy-start(bf16[96]{0:T(256)(128)(2,1)} %param.18) | copy-start | bytes 580
  0.7 7.9 %copy-start.16 = (s32[4,256,2]{1,2,0:T(2,128)S(1)}, s32[4,256,2]{1,2,0:T(2,128)}, u32[]{:S(2)}) copy-start(s32[4,256,2]{1,2,0:T(2,128)} %param.13) | copy-start | bytes 24580
  0.7 7.9 %copy-start.13 = (bf16[3,64,96]{2,1,0:T(8,128)(2,1)S(1)}, bf16[3,64,96]{2,1,0:T(8,128)(2,1)}, u32[]{:S(2)}) copy-start(bf16[3,64,96]{2,1,0:T(8,128)(2,1)} %param.17) | copy-start | bytes 110596
  0.7 8.1 %copy-start = (bf16[1,256,768]{2,1,0:T(8,128)(2,1)S(1)}, bf16[1,256,768]{2,1,0:T(8,128)(2,1)}, u32[]{:S(2)}) copy-start(bf16[1,256,768]{2,1,0:T(8,128)(2,1)} %param.11) | copy-start | bytes 1179652
  1.9 16.3 %collective-permute-start = (bf16[1,768,384]{2,1,0:T(8,128)(2,1)S(1)}, bf16[1,768,384]{2,1,0:T(8,128)(2,1)S(1)}, u32[]{:S(2)}, u32[]{:S(2)}) collective-permute-start(bf16[1,768,384]{2,1,0:T(8,128)(2,1)S(1)} %constant_dynamic-slice_fusion.2), channel_id=1, source_target_pairs={{0,16},{16,0},{1,17},{17,1},{2,18},{18,2},{3,19},{19,3},{4,20},{20... | collective-permute-start | bytes 1769480 | tf_op jit(solution)/shard_map/ppermute | solution.py:1497
  18.2 0.8 copy-start.11
  39.3 1.6 copy-start.1
  40.9 53.1 %collective-permute-start.1 = (bf16[2,768,384]{2,1,0:T(8,128)(2,1)}, bf16[2,768,384]{2,1,0:T(8,128)(2,1)}, u32[]{:S(2)}, u32[]{:S(2)}) collective-permute-start(bf16[2,768,384]{2,1,0:T(8,128)(2,1)} %constant_dynamic-slice_fusion.1), channel_id=1, source_target_pairs={{0,16},{16,0},{1,17},{17,1},{2,18},{18,2},{3,19},{19,3},{4,20},{20... | collective-permute-start | bytes 3538952 | tf_op jit(solution)/shard_map/ppermute | solution.py:1497
  44.0 45.1 %copy-start.3 = (bf16[256,192]{1,0:T(8,128)(2,1)}, bf16[256,192]{1,0:T(8,128)(2,1)S(1)}, u32[]{:S(2)}) copy-start(bf16[256,192]{1,0:T(8,128)(2,1)S(1)} %copy.111.mixed.refs_15_) | copy-start | bytes 294916
  44.1 45.1 %copy-start.9 = (f32[1,768]{1,0:T(1,128)}, f32[1,768]{1,0:T(1,128)S(1)}, u32[]{:S(2)}) copy-start(f32[1,768]{1,0:T(1,128)S(1)} %reshape.123.gain.refs_7_) | copy-start | bytes 9220
  89.2 1.1 copy-start.2
  90.3 0.8 copy-start.5
  91.2 0.7 copy-start.6
  91.9 2.7 copy-start.4
  91.9 2.7 copy-start.7
  91.9 2.7 copy-start.8
  290.2 6.5 %copy-start.14 = (f32[4,8,128]{2,1,0:T(8,128)S(1)}, f32[4,8,128]{2,1,0:T(8,128)}, u32[]{:S(2)}) copy-start(f32[4,8,128]{2,1,0:T(8,128)} %get-tuple-element.61) | copy-start | bytes 49156
  297.9 13.8 %copy-start.12 = (bf16[4,64,768]{2,1,0:T(8,128)(2,1)S(1)}, bf16[4,64,768]{2,1,0:T(8,128)(2,1)}, u32[]{:S(2)}) copy-start(bf16[4,64,768]{2,1,0:T(8,128)(2,1)} %get-tuple-element.60) | copy-start | bytes 1179652
  298.0 14.6 %copy-start.10 = (f32[4,64,768]{2,1,0:T(8,128)S(1)}, f32[4,64,768]{2,1,0:T(8,128)}, u32[]{:S(2)}) copy-start(f32[4,64,768]{2,1,0:T(8,128)} %get-tuple-element.62) | copy-start | bytes 2359300

commit v4 on v3

--- a/solution.py
+++ b/solution.py
@@ -321,6 +321,7 @@
 
     def send(self, src, dst, device):
         k = len(self.copies)
+        assert k < self.send_sems.shape[0]
         copy = pltpu.make_async_remote_copy(
             src_ref=src,
             dst_ref=dst,
@@ -557,221 +558,8 @@
     return pl.CostEstimate(flops=0, bytes_accessed=microseconds * 3_000_000, transcendentals=0)
 
 
-def remote_call(
-    kernel,
-    outs,
-    ins,
-    scratch,
-    copies,
-    collective_id,
-    vmem_mib,
-    microseconds,
-    in_hbm=(),
-    out_hbm=(),
-):
-    vmem, hbm = pl.BlockSpec(memory_space=pltpu.VMEM), pl.BlockSpec(memory_space=pltpu.HBM)
-    return pl.pallas_call(
-        kernel,
-        out_shape=outs,
-        in_specs=[hbm if i in in_hbm else vmem for i in range(len(ins))],
-        out_specs=[hbm if i in out_hbm else vmem for i in range(len(outs))],
-        scratch_shapes=[
-            *scratch,
-            pltpu.SemaphoreType.DMA((copies,)),
-            pltpu.SemaphoreType.DMA((copies,)),
-        ],
-        compiler_params=pltpu.CompilerParams(
-            collective_id=collective_id,
-            has_side_effects=True,
-            vmem_limit_bytes=vmem_mib * 2**20,
-        ),
-        cost_estimate=spends(microseconds),
-    )(*ins)
-
-
 def shape(dims, dtype=LOW):
     return jax.ShapeDtypeStruct(dims, dtype)
-
-
-def weights_kernel(heads, wq, wo, count, route, oq, oo, counts, far_route, ss, rs):
-    place = Place(heads)
-    links = Links(ss, rs)
-    me = place.image(0, 0, 0)
-    place.greet(place.plane_peers + place.z_peers)
-    oq[me] = wq[...]
-    oo[me, place.z] = wo[...]
-    counts[me] = count[...]
-    half = wq.shape[1] // 2
-    mid = heads // 2
-    main = PlaneGather(
-        links,
-        place,
-        lambda i: oq.at[i, :, pl.ds(0, half)],
-        lambda i: oq.at[i, :, pl.ds(half, half)],
-        lambda i: oq.at[i],
-    )
-    side = PlaneGather(
-        links,
-        place,
-        lambda i: oo.at[i, pl.ds(0, mid)],
-        lambda i: oo.at[i, pl.ds(mid, heads - mid)],
-        lambda i: oo.at[i],
-    )
-    main.start()
-    along = all_heads(
-        links, place, lambda k, z: (oo.at[me, place.z], oo.at[me, place.z])
-    )
-    small = [links.send(counts.at[me], counts.at[me], d) for d in place.plane_peers]
-    small.append(links.send(route, far_route, place.x_peer))
-    main.forward()
-    for copy in along:
-        copy.wait_recv()
-    side.start()
-    main.share()
-    main.finish()
-    side.forward()
-    side.share()
-    side.finish()
-    for copy in small:
-        copy.wait_recv()
-    links.drain()
-
-
-def gather_weights_fast(heads, wq, wo, count, route):
-    outs = [
-        shape((8, *wq.shape)),
-        shape((8, heads, *wo.shape)),
-        shape((8, *count.shape), jnp.int32),
-        shape(route.shape, jnp.int32),
-    ]
-    copies = 2 * GATHER_COPIES + heads - 1 + 7 + 1
-    return remote_call(
-        functools.partial(weights_kernel, heads),
-        outs,
-        [wq, wo, count, route],
-        [],
-        copies,
-        1,
-        32,
-        20,
-    )
-
-
-def mix_kernel(
-    heads,
-    experts,
-    skip,
-    mixed,
-    wo,
-    tokens,
-    gain,
-    router,
-    near_route,
-    far_route,
-    down,
-    residual,
-    second,
-    group,
-    probs,
-    slots,
-    arrived,
-    everyone,
-    other_half,
-    ss,
-    rs,
-):
-    place = Place(heads)
-    links = Links(ss, rs)
-    me = place.image(0, 0, 0)
-    place.greet(place.plane_peers + place.z_peers)
-    everyone[place.z] = mixed[...]
-    along = all_heads(links, place, lambda k, z: (everyone.at[place.z], everyone.at[place.z]))
-    local_experts = slots.shape[0] // 2
-    ids = place.z * local_experts + lax.broadcasted_iota(jnp.int32, (local_experts, 1), 0)
-    first = place.f == 0
-    near, far = near_route[...], far_route[...]
-    both = [jnp.where(first, near, far), jnp.where(first, far, near)]
-    chosen = jnp.concatenate([(r[0:1] == ids) | (r[1:2] == ids) for r in both], 0)
-    count = chosen.astype(WIDE)
-    before = lax.broadcasted_iota(jnp.int32, (128, 128), 0)
-    before = (before < lax.broadcasted_iota(jnp.int32, (128, 128), 1)).astype(LOW)
-    running = jnp.zeros((2 * local_experts, 1), WIDE)
-    for b in range(slots.shape[1] // 128):
-        columns = slice(b * 128, (b + 1) * 128)
-        here = count[:, columns]
-        slot = dot(here.astype(LOW), before) + running
-        slots[:, columns] = jnp.where(chosen[:, columns], slot, -1.0).astype(jnp.int32)
-        running = running + jnp.sum(here, -1, keepdims=True)
-    for copy in along:
-        copy.wait_recv()
-    rows_all, width = tokens.shape
-    half = width // 2
-    total = jnp.zeros((rows_all, width), WIDE)
-    for z in range(heads):
-        weight = wo[:, z].reshape(width, wo.shape[3])
-        total = total + lax.dot_general(
-            everyone[z], weight, (((1,), (1,)), ((), ())), preferred_element_type=WIDE
-        )
-    residual[...] = total
-
-    def norm(rows):
-        values = tokens[rows, :].astype(WIDE) + residual[rows, :]
-        residual[rows, :] = values
-        normed, _ = normalize(values)
-        second[rows, :] = (normed * gain[...]).astype(LOW)
-
-    in_rows(rows_all, 64, norm)
-    low, high = second[:, :half], second[:, half:]
-    group[me] = jnp.where(first, low, high)
-    other_half[...] = jnp.where(first, high, low)
-    x1 = links.send(other_half, group.at[me], place.x_peer)
-    theirs = pl.ds((1 - place.f) * (local_experts // 2) + skip, arrived.shape[0])
-    bulk = links.send(down.at[theirs], arrived, place.x_peer)
-    y1 = links.send(group.at[me], group.at[me], place.y_peer)
-    shared = [links.send(group.at[me], group.at[me], place.core_peer)]
-    logits = lax.dot_general(
-        router[...], second[...], (((0,), (1,)), ((), ())), preferred_element_type=WIDE
-    )[:experts]
-    powers = jnp.exp(logits - jnp.max(logits, 0, keepdims=True))
-    probs[me] = powers / jnp.sum(powers, 0, keepdims=True)
-    small = [links.send(probs.at[me], probs.at[me], d) for d in place.plane_peers]
-    across, beside, corner = place.image(1, 0, 0), place.image(0, 1, 0), place.image(1, 1, 0)
-    x1.wait_recv()
-    y2 = links.send(group.at[across], group.at[across], place.y_peer)
-    shared.append(links.send(group.at[across], group.at[across], place.core_peer))
-    y1.wait_recv()
-    shared.append(links.send(group.at[beside], group.at[beside], place.core_peer))
-    y2.wait_recv()
-    shared.append(links.send(group.at[corner], group.at[corner], place.core_peer))
-    for copy in shared + small + [bulk]:
-        copy.wait_recv()
-    links.drain()
-
-
-def mix_heads(
-    heads, experts, skip, mixed, wo, tokens, gain, router, near_route, far_route, down
-):
-    rows, width = tokens.shape
-    late = down.shape[0] // 2 - skip
-    return remote_call(
-        functools.partial(mix_kernel, heads, experts, skip),
-        [
-            shape((rows, width), WIDE),
-            shape((rows, width)),
-            shape((8, rows, width // 2)),
-            shape((8, experts, rows), WIDE),
-            shape((2 * experts // heads, near_route.shape[1]), jnp.int32),
-            shape((late, *down.shape[1:])),
-        ],
-        [mixed, wo, tokens, gain, router, near_route, far_route, down],
-        [pltpu.VMEM((heads, *mixed.shape), LOW), pltpu.VMEM((rows, width // 2), LOW)],
-        heads - 1 + 7 + 8,
-        2,
-        48,
-        26,
-        in_hbm=(7,),
-        out_hbm=(5,),
-    )
 
 
 class ChunkSum:
@@ -901,7 +689,7 @@
             total = total + far[k, n].astype(WIDE)
         values = residual[mine, columns[k]] + total
         result[z, :, columns[k]] = values.astype(LOW)
-        error = (values - teacher[mine, columns[k]].astype(WIDE)) * valid[mine, :]
+        error = (values - teacher[mine, columns[k]].astype(WIDE)) * valid[mine, 0:1]
         grad = error * scale[0:1, 0:1]
         final_grad[:, columns[k]] = grad
         group[me, mine, columns[k]] = grad.astype(LOW)
@@ -930,7 +718,7 @@
             forward,
         ],
     )
-    loss[z] = sum(squares)
+    loss[z] = sum(squares) * r.loss_scale[0:1, 0:1]
     extra = all_heads(links, place, lambda k, to: (result.at[z], result.at[z]))
     extra += all_heads(links, place, lambda k, to: (loss.at[z], loss.at[z]))
     for gather in gathers:
@@ -952,6 +740,7 @@
         self.sems, self.count = sems, 0
 
     def start(self, src, dst):
+        assert self.count < self.sems.shape[0]
         copy = pltpu.make_async_copy(src, dst, self.sems.at[self.count])
         self.count += 1
         copy.start()
@@ -963,42 +752,208 @@
     return values * cdf, cdf + values * DENSITY * jnp.exp(-0.5 * values * values)
 
 
-def experts_part(place, links, loads, pieces, r):
-    slots, x, probs, up, down = r.slots, r.x, r.probs, r.up, r.down
+def front_part(place, links, r):
+    heads, f, z, me = place.heads, place.f, place.z, place.image(0, 0, 0)
+    oq, oo, counts, slots = r.qkv, r.wo_all, r.counts, r.slots
+    kept = r.w_far.shape[0]
+    theirs = (1 - f) * kept
+    oq[me] = r.shard[...]
+    oo[me, z] = r.wo_shard[...]
+    counts[me] = jnp.broadcast_to(jnp.sum(r.valid_row[...].astype(WIDE), -1, keepdims=True), (8, 128))
+    half, mid = oq.shape[2] // 2, heads // 2
+    main = PlaneGather(
+        links,
+        place,
+        lambda i: oq.at[i, :, pl.ds(0, half)],
+        lambda i: oq.at[i, :, pl.ds(half, half)],
+        lambda i: oq.at[i],
+    )
+    side = PlaneGather(
+        links,
+        place,
+        lambda i: oo.at[i, pl.ds(0, mid)],
+        lambda i: oo.at[i, pl.ds(mid, heads - mid)],
+        lambda i: oo.at[i],
+    )
+
+    def bulk(i):
+        return links.send(r.down.at[theirs + i], r.w_far.at[i], place.x_peer)
+
+    main.start()
+    along = all_heads(links, place, lambda k, to: (oo.at[me, z], oo.at[me, z]))
+    small = [links.send(counts.at[me], counts.at[me], d) for d in place.plane_peers]
+    small.append(links.send(r.near_route, r.far_route, place.x_peer))
+    main.forward()
+    for copy in along:
+        copy.wait_recv()
+    side.start()
+    down = [bulk(0)]
+    main.share()
+    main.finish()
+    width = r.tokens.shape[1]
+    experts = r.probs.shape[1]
+    narrow = oq[:, :, 0:128].reshape(width, 128).astype(WIDE)
+    turned = jnp.transpose(narrow)
+    r.router[...] = turned[:experts].astype(LOW)
+    r.gain_one[...] = turned[experts : experts + 1]
+    r.gain[...] = turned[experts + 1 : experts + 2]
+    rows_all = r.tokens.shape[0]
+
+    def first_norm(rows):
+        normed, _ = normalize(r.tokens[rows, :].astype(WIDE))
+        r.first_in[rows, :] = (normed * r.gain_one[...]).astype(LOW)
+
+    in_rows(rows_all, 64, first_norm)
+    qkv_width = r.projected.shape[1]
+    weight = oq[:, :, pl.ds(128, qkv_width)].reshape(width, qkv_width)
+    r.projected[...] = dot(r.first_in[...], weight).astype(LOW)
+    side.forward()
+    down.append(bulk(1))
+    head_count = r.log_total.shape[1]
+    size = qkv_width // head_count // 3
+    keys_ok = r.valid_row[...] > 0
+    mixed = []
+    for h in range(head_count):
+        at = 3 * h * size
+        query, key, value = (r.projected[:, at + n * size : at + (n + 1) * size] for n in range(3))
+        scores = jnp.where(keys_ok, dot(query, key, (1, 1)) * size ** (-0.5), MASKED)
+        peak = jnp.max(scores, -1, keepdims=True)
+        powers = jnp.exp(scores - peak)
+        total = jnp.sum(powers, -1, keepdims=True)
+        r.log_total[:, h : h + 1] = peak + jnp.log(total)
+        mixed.append(dot((powers / total).astype(LOW), value).astype(LOW))
+    r.mixed[...] = jnp.concatenate(mixed, 1)
+    everyone = r.all_mixed
+    everyone[z] = r.mixed[...]
+    along = all_heads(links, place, lambda k, to: (everyone.at[z], everyone.at[z]))
+    side.share()
+    for copy in small:
+        copy.wait_recv()
+    valid_total = sum(counts[i] for i in range(8))[0:1, 0:1]
+    r.scale[...] = jnp.broadcast_to(8 * rows_all / valid_total, (8, 128))
+    r.loss_scale[...] = jnp.broadcast_to(8 / (valid_total * width), (8, 128))
+    column = jnp.broadcast_to(r.valid_row[...].astype(WIDE), (8, rows_all))
+    r.valid[...] = jnp.transpose(column)
+    local_experts = 2 * kept
+    ids = z * local_experts + lax.broadcasted_iota(jnp.int32, (local_experts, 1), 0)
+    first = f == 0
+    near, far = r.near_route[...], r.far_route[...]
+    both = [jnp.where(first, near, far), jnp.where(first, far, near)]
+    chosen = []
+    for route in both:
+        hits = route[0:1] == ids
+        for c in range(1, r.choices):
+            hits = hits | (route[c : c + 1] == ids)
+        chosen.append(hits)
+    chosen = jnp.concatenate(chosen, 0)
+    count = chosen.astype(WIDE)
+    before = lax.broadcasted_iota(jnp.int32, (128, 128), 0)
+    before = (before < lax.broadcasted_iota(jnp.int32, (128, 128), 1)).astype(LOW)
+    running = jnp.zeros((2 * local_experts, 1), WIDE)
+    for b in range(slots.shape[1] // 128):
+        columns = slice(b * 128, (b + 1) * 128)
+        here = count[:, columns]
+        slot = dot(here.astype(LOW), before) + running
+        slots[:, columns] = jnp.where(chosen[:, columns], slot, -1.0).astype(jnp.int32)
+        running = running + jnp.sum(here, -1, keepdims=True)
+    for copy in along:
+        copy.wait_recv()
+    side.finish()
+    half = width // 2
+    total = jnp.zeros((rows_all, width), WIDE)
+    for n in range(heads):
+        weight = oo[:, n].reshape(width, oo.shape[3])
+        total = total + dot(everyone[n], weight, (1, 1))
+    r.residual[...] = total
+
+    def norm(rows):
+        values = r.tokens[rows, :].astype(WIDE) + r.residual[rows, :]
+        r.residual[rows, :] = values
+        normed, _ = normalize(values)
+        r.second_in[rows, :] = (normed * r.gain[...]).astype(LOW)
+
+    in_rows(rows_all, 64, norm)
+    low, high = r.second_in[:, :half], r.second_in[:, half:]
+
+    def part_of(df, dy, dc):
+        return r.x.at[
+            1 - f if df else f, 1 - place.y if dy else place.y, 1 - place.c if dc else place.c
+        ]
+
+    mine, across, beside, corner = (
+        part_of(0, 0, 0),
+        part_of(1, 0, 0),
+        part_of(0, 1, 0),
+        part_of(1, 1, 0),
+    )
+    mine[...] = jnp.where(first, low, high)
+    r.other_half[...] = jnp.where(first, high, low)
+    x1 = links.send(r.other_half, mine, place.x_peer)
+    y1 = links.send(mine, mine, place.y_peer)
+    shared = [links.send(mine, mine, place.core_peer)]
+    down.append(bulk(2))
+    logits = dot(r.router[...], r.second_in[...], (1, 1))
+    powers = jnp.exp(logits - jnp.max(logits, 0, keepdims=True))
+    probs = powers / jnp.sum(powers, 0, keepdims=True)
+    r.probs_own[...] = probs
+    r.probs[me] = probs
+    small = [links.send(r.probs.at[me], r.probs.at[me], d) for d in place.plane_peers]
+    x1.wait_recv()
+    y2 = links.send(across, across, place.y_peer)
+    shared.append(links.send(across, across, place.core_peer))
+    y1.wait_recv()
+    shared.append(links.send(beside, beside, place.core_peer))
+    y2.wait_recv()
+    shared.append(links.send(corner, corner, place.core_peer))
+    for copy in shared + small:
+        copy.wait_recv()
+    return [y1, y2, *shared], down
+
+
+FRONT_COPIES = 2 * GATHER_COPIES + 7 + 1 + 1 + 2 + 4 + 7
+
+
+def experts_part(place, links, loads, weights, down_far, r):
+    slots, probs = r.slots, r.probs
     pick_near, pick_far, gates, hidden = r.pick_near, r.pick_far, r.gates, r.hidden
     buffer_near, buffer_far, own, weighted = r.buffer_near, r.buffer_far, r.own, r.weighted
     away, arrived, w_up, w_near, w_far = r.away, r.arrived, r.w_up, r.w_near, r.w_far
     kept, pair, _ = own.shape
-    capacity, half = pair // 2, x.shape[2]
+    capacity, half = pair // 2, r.x.shape[4]
+    group_rows = slots.shape[1]
+    stores = []
+
+    def kept_rows(i, buffer, target):
+        stores.append(loads.start(buffer.at[i % 2], target.at[i]))
+
     local_experts = 2 * kept
     mine, theirs = place.f * kept, (1 - place.f) * kept
-    ups = {}
-    for far in (1, 0):
-        for i in range(kept):
-            source = (theirs if far else mine) + i
-            ups[far, i] = loads.start(up.at[source], w_up.at[far, i])
-    nears = [loads.start(down.at[mine + i], w_near.at[i]) for i in range(kept)]
-    fars, at = [], 0
-    for piece in pieces:
-        size = piece.shape[0]
-        fars.append(loads.start(piece, w_far.at[pl.ds(at, size)]))
-        at += size
-    place.greet(place.everyone())
+    ups, nears = weights
     sent = []
     for i in range(kept):
+        if i > 1:
+            stores[i - 2].wait()
         for g in range(2):
             rows = slice(i * capacity, (i + 1) * capacity)
             hot = one_hot(slots, g * local_experts + theirs + i, capacity).astype(LOW)
             pick_far[g, rows] = hot
-            buffer_far[i, g * capacity : (g + 1) * capacity] = dot(hot, x[g]).astype(LOW)
+            x = r.x[g].reshape(group_rows, half)
+            buffer_far[i % 2, g * capacity : (g + 1) * capacity] = dot(hot, x).astype(LOW)
         ups[1, i].wait()
-        away[i] = dot(buffer_far[i], w_up[1, i]).astype(LOW)
+        kept_rows(i, buffer_far, r.far_out)
+        away[i] = dot(buffer_far[i % 2], w_up[1, i]).astype(LOW)
         sent.append(links.send(away.at[i], arrived.at[i], place.x_peer))
-    late = [
-        links.send(down.at[theirs + i], w_far.at[i], place.x_peer) for i in range(at, kept)
+    down_far = [
+        *down_far,
+        *(
+            links.send(r.down.at[theirs + i], w_far.at[i], place.x_peer)
+            for i in range(len(down_far), kept)
+        ),
     ]
     for i in range(kept):
         expert = place.z * local_experts + mine + i
+        if i > 1:
+            stores[kept + i - 2].wait()
         for g in range(2):
             rows = slice(i * capacity, (i + 1) * capacity)
             into = slice(g * capacity, (g + 1) * capacity)
@@ -1007,15 +962,16 @@
             chances = jnp.concatenate(chances, 1)
             gates[i, into] = jnp.sum(jnp.where(hot, chances, 0.0), -1, keepdims=True)
             pick_near[g, rows] = hot.astype(LOW)
-            buffer_near[i, into] = dot(hot.astype(LOW), x[g]).astype(LOW)
+            x = r.x[g].reshape(group_rows, half)
+            buffer_near[i % 2, into] = dot(hot.astype(LOW), x).astype(LOW)
         ups[0, i].wait()
-        own[i] = dot(buffer_near[i], w_up[0, i])
-    for copy in nears + fars:
+        kept_rows(i, buffer_near, r.near_out)
+        own[i] = dot(buffer_near[i % 2], w_up[0, i])
+    for copy in nears:
         copy.wait()
     for i in range(kept):
         sent[i].wait_recv()
-        if i >= at:
-            late[i - at].wait_recv()
+        down_far[i].wait_recv()
         values, slopes = gelu_parts(own[i] + arrived[i].astype(WIDE))
         hidden[i] = values.astype(LOW)
         own[i] = slopes
@@ -1029,6 +985,7 @@
         total = dot(pick_near[g], weighted[g], (0, 0)).astype(LOW)
         r.part[g] = total.reshape(r.part.shape[1:])
     links.left(sent)
+    return stores[kept - 2 : kept] + stores[2 * kept - 2 :]
 
 
 def experts_back_part(place, links, loads, r):
@@ -1068,8 +1025,6 @@
     bulk = [links.send(send_held.at[early], r.down_far.at[early], place.x_peer)]
     stores = [
         loads.start(r.hidden, r.hidden_out),
-        loads.start(r.buffer_near, r.near_out),
-        loads.start(r.buffer_far, r.far_out),
         loads.start(pre_near, r.near_pre),
         loads.start(out_grad, r.grad_out),
     ]
@@ -1089,17 +1044,17 @@
     for g in range(2):
         near = dot(pick_near[g], rows_near[g], (0, 0))
         both = (near + dot(pick_far[g], rows_far[g], (0, 0))).astype(LOW)
-        r.back_part[g] = both.reshape(r.back_part.shape[1:])
+        r.x[g] = both.reshape(r.x.shape[1:])
     return stores, bulk
 
 
 def back_part(place, links, chunks, bulk, r):
     heads, f, y, z = place.heads, place.f, place.y, place.z
     t, me = 2 * y + place.c, place.image(0, 0, 0)
-    part, gate_part, probs, valid = r.back_part, r.gate_rows, r.probs_own, r.valid_row
+    part, gate_part, probs, valid = r.x, r.gate_rows, r.probs_own, r.valid_row
     residual, gain, router, final_grad, tokens = (r.residual, r.gain, r.router, r.final_grad, r.tokens)
     gain_one, second_in, projected, log_total, mixed = (r.gain_one, r.second_in, r.projected, r.log_total, r.mixed)
-    qkv, wo, tokens_grad, dense_out, gain_out = (r.qkv, r.wo, r.tokens_grad, r.dense_out, r.gain_out)
+    qkv, wo, tokens_grad, dense_out, gain_out = (r.qkv, r.wo_all, r.tokens_grad, r.dense_out, r.gain_out)
     core_in, y_in, far, pair, x_in = (r.core_in, r.y_in, r.far, r.pair, r.x_in)
     gate_in, gate_sum, gate_all, logit_rows, logit_grads = (r.gate_in, r.gate_sum, r.gate_all, r.logit_rows, r.logit_grads)
     attended, first_in, projected_grad, first_part, dense = (r.attended, r.first_in, r.projected_grad, r.first_part, r.dense)
@@ -1186,11 +1141,6 @@
     dense_width = dense.shape[2]
     dense[:, :, pl.ds(dense_width - 128, 128)] = router_grad.reshape(blocks, block, 128)
 
-    def first_norm(rows):
-        again, _ = normalize(tokens[rows, :].astype(WIDE))
-        first_in[rows, :] = (again * gain_one[...]).astype(LOW)
-
-    in_rows(rows_all, 64, first_norm)
     to_heads(chunks - 1)
     to_x(chunks - 2)
     to_x(chunks - 1)
@@ -1218,7 +1168,7 @@
     ):
         copy.wait_recv()
 
-    mixed_grad = dot(attended[...], wo[...].reshape(width, wo.shape[2])).astype(LOW)
+    mixed_grad = dot(attended[...], wo[:, z].reshape(width, wo.shape[3])).astype(LOW)
     head_count = log_total.shape[1]
     size = qkv_width // head_count // 3
     score_scale = size ** (-0.5)
@@ -1290,18 +1240,29 @@
         copy.wait_recv()
 
 
-def layer_kernel(heads, chunks, names, piece_names, *refs):
-    r = types.SimpleNamespace(**dict(zip(names, refs)))
+def layer_kernel(heads, chunks, choices, names, *refs):
+    r = types.SimpleNamespace(**dict(zip(names, refs)), choices=choices)
     place = Place(heads)
     links = Links(r.send_sems, r.recv_sems)
     loads = Loads(r.load_sems)
-    experts_part(place, links, loads, [getattr(r, n) for n in piece_names], r)
+    kept = r.w_far.shape[0]
+    mine, theirs = place.f * kept, (1 - place.f) * kept
+    ups = {}
+    for far in (1, 0):
+        for i in range(kept):
+            source = (theirs if far else mine) + i
+            ups[far, i] = loads.start(r.up.at[source], r.w_up.at[far, i])
+    nears = [loads.start(r.down.at[mine + i], r.w_near.at[i]) for i in range(kept)]
+    place.greet(place.everyone())
+    from_x, down_far = front_part(place, links, r)
+    held = experts_part(place, links, loads, (ups, nears), down_far, r)
     extra = combine_part(place, links, chunks, r)
+    links.left(from_x)
     stores, bulk = experts_back_part(place, links, loads, r)
     for copy in extra:
         copy.wait_recv()
     back_part(place, links, chunks, bulk, r)
-    for copy in stores:
+    for copy in held + stores:
         copy.wait()
     links.drain()
 
@@ -1330,20 +1291,17 @@
     return types.SimpleNamespace(**dict(zip(outs, made)))
 
 
-def layer(heads, capacity, head_count, pieces, vmem, hbm):
-    rows, width = vmem["residual"].shape
+def layer(heads, experts, capacity, choices, head_count, vmem, hbm):
+    rows, width = vmem["tokens"].shape
     own, half, chunks = rows // heads, width // 2, width // 256
     local_experts, _, hidden_width = hbm["up"].shape
     kept, pair, group_rows = local_experts // 2, 2 * capacity, 4 * rows
-    block = width // 8
-    qkv_width, mixed_width = vmem["projected"].shape[1], vmem["mixed"].shape[1]
+    block, mixed_width = vmem["wo_shard"].shape
+    qkv_width = 3 * mixed_width
     dense_width = qkv_width + mixed_width + 128
     cut = 128 * ((dense_width // 128 + 1) // 2)
-    late = kept - sum(piece.shape[0] for piece in pieces)
-    piece_names = [f"piece{n}" for n in range(len(pieces))]
     ins = {name: (array, False) for name, array in vmem.items()}
     ins.update({name: (array, True) for name, array in hbm.items()})
-    ins.update({name: (array, True) for name, array in zip(piece_names, pieces)})
     outs = {
         "result": (shape((heads, own, width)), False),
         "loss": (shape((heads, 8, 128), WIDE), False),
@@ -1361,8 +1319,8 @@
     low = {
         "pick_near": (2, kept * capacity, group_rows),
         "pick_far": (2, kept * capacity, group_rows),
-        "buffer_near": (kept, pair, half),
-        "buffer_far": (kept, pair, half),
+        "buffer_near": (2, pair, half),
+        "buffer_far": (2, pair, half),
         "hidden": (kept, pair, hidden_width),
         "weighted": (2, kept * capacity, width),
         "away": (kept, pair, hidden_width),
@@ -1381,13 +1339,21 @@
         "image_far": (chunks, heads - 1, own, 256),
         "out_grad": (kept, pair, width),
         "slot_rows": (pair, width),
-        "back_part": (2, 2, 2, rows, half),
+        "x": (2, 2, 2, rows, half),
+        "other_half": (rows, half),
+        "qkv": (8, *vmem["shard"].shape),
+        "wo_all": (8, heads, block, mixed_width),
+        "router": (experts, width),
+        "projected": (rows, qkv_width),
+        "mixed": (rows, mixed_width),
+        "all_mixed": (heads, rows, mixed_width),
+        "second_in": (rows, width),
         "core_in": (chunks, 2, 2, rows, 128),
         "y_in": (chunks, 2, rows, 128),
         "far": (chunks, heads - 1, 2, own, 128),
         "pair": (chunks, 2, own, 128),
         "x_in": (chunks, own, 128),
-        "logit_grads": vmem["probs_own"].shape,
+        "logit_grads": (experts, rows),
         "attended": (rows, width),
         "first_in": (rows, width),
         "projected_grad": (rows, qkv_width),
@@ -1403,6 +1369,16 @@
     }
     wide = {
         "gates": (kept, pair, 1),
+        "counts": (8, 8, 128),
+        "scale": (8, 128),
+        "loss_scale": (8, 128),
+        "valid": (rows, 8),
+        "gain_one": (1, width),
+        "gain": (1, width),
+        "log_total": (rows, head_count),
+        "residual": (rows, width),
+        "probs": (8, experts, rows),
+        "probs_own": (experts, rows),
         "own": (kept, pair, hidden_width),
         "final_grad": (own, width),
         "gate_rows": (2, kept, group_rows),
@@ -1416,19 +1392,21 @@
     }
     scratch = {name: pltpu.VMEM(dims, LOW) for name, dims in low.items()}
     scratch.update({name: pltpu.VMEM(dims, WIDE) for name, dims in wide.items()})
-    copies = kept + late + chunks * (5 + GATHER_COPIES + 2 * (heads - 1)) + 2 * (heads - 1)
+    whole = {"far_route": (8, group_rows), "slots": (2 * local_experts, group_rows)}
+    scratch.update({name: pltpu.VMEM(dims, jnp.int32) for name, dims in whole.items()})
+    copies = FRONT_COPIES + 2 * (heads - 1) + 2 * kept + chunks * (5 + GATHER_COPIES + 2 * (heads - 1)) + 2 * (heads - 1)
     copies += kept + 2 + chunks * (3 + heads - 1) + 3 + 2 * heads - 1 + heads - 1
     copies += SUM_COPIES + 3 * (heads - 1) + 7
     return named_call(
-        lambda names, *refs: layer_kernel(heads, chunks, names, piece_names, *refs),
+        functools.partial(layer_kernel, heads, chunks, choices),
         ins,
         outs,
         scratch,
         copies,
-        3 * kept + len(pieces) + 6,
-        3,
-        54,
-        190,
+        5 * kept + 6,
+        1,
+        59,
+        280,
     )
 
 
@@ -1520,16 +1498,8 @@
     expert_count = local_experts * heads
     group_rows = 4 * rows
     capacity = 2 * routes.shape[2] * group_rows // expert_count
-    total_tokens, total_images = 8 * rows, 8
-    score_scale = head_dim ** (-0.5)
-
     mine, theirs = f * kept, (1 - f) * kept
     half = width // 2
-    first_chunk, second_chunk = kept // 4, kept // 2
-    down_a = lax.dynamic_slice_in_dim(expert_down, theirs, first_chunk, 0)
-    down_a, qkv_weight = lax.optimization_barrier((down_a, qkv_weight))
-    down_a = swap(down_a)
-
     qkv_width = head_count * qkv_dim
     pad = -(128 + qkv_width) % 256
     wq = jnp.concatenate(
@@ -1544,95 +1514,20 @@
         1,
     )
     wo = out_weight.reshape(head_count * head_dim, block).T
-    count = jnp.full((8, 128), jnp.sum(valid_mask), jnp.int32)
     near_route = jnp.pad(routes.reshape(group_rows, -1).T, ((0, 8 - routes.shape[2]), (0, 0)))
-    count, down_a = lax.optimization_barrier((count, down_a))
-    gathered, wo_all, counts, far_route = gather_weights_fast(heads, wq, wo, count, near_route)
-    gathered, down_b = lax.optimization_barrier(
-        (gathered, lax.dynamic_slice_in_dim(expert_down, theirs + first_chunk, second_chunk, 0))
-    )
-    down_b = swap(down_b)
-    gathered_blocks = gathered
-    gathered = gathered.reshape(width, -1)
-    qkv_full = gathered[:, 128 : 128 + qkv_width]
-    lanes = jnp.arange(128)
-    router_wide = jnp.where(lanes < expert_count, gathered[:, :128], 0)
-    gain_a = gathered[:, expert_count].astype(WIDE)[None]
-    gain_b = gathered[:, expert_count + 1].astype(WIDE)[None]
-    valid_total = jnp.sum(counts[:, 0, 0]).astype(WIDE)
-
-    inputs = tokens[0].astype(WIDE)
-    normed_one, _ = normalize(inputs)
-    first_in = (normed_one * gain_a).astype(LOW)
-    projected = (
-        jnp.dot(first_in, qkv_full, preferred_element_type=WIDE)
-        .astype(LOW)
-        .reshape(rows, head_count, qkv_dim)
-    )
-    queries = projected[..., :head_dim]
-    key_rows = projected[..., head_dim : 2 * head_dim]
-    values = projected[..., 2 * head_dim :]
-    keys_ok = (valid_mask > 0)[0][None, None, :]
-
-    def scores_now():
-        raw = jnp.einsum("qhe,khe->hqk", queries, key_rows, preferred_element_type=WIDE)
-        return jnp.where(keys_ok, raw * score_scale, MASKED)
-
-    scores = scores_now()
-    peak_score = jnp.max(scores, -1, keepdims=True)
-    exp_scores = jnp.exp(scores - peak_score)
-    score_total = jnp.sum(exp_scores, -1, keepdims=True)
-    logarithm_total = peak_score + jnp.log(score_total)
-    attention = (exp_scores / score_total).astype(LOW)
-    mixed = (
-        jnp.einsum("hqk,khe->qhe", attention, values, preferred_element_type=WIDE)
-        .astype(LOW)
-        .reshape(rows, head_count * head_dim)
-    )
-    residual, second_in, group_in, probs_all, slots, down_c = mix_heads(
-        heads,
-        expert_count,
-        first_chunk + second_chunk,
-        mixed,
-        wo_all,
-        tokens[0],
-        gain_b,
-        router_wide,
-        near_route,
-        far_route,
-        expert_down,
-    )
-    group_in, down_b = lax.optimization_barrier((group_in, down_b))
-
-    rows_in = group_in.reshape(2, group_rows, half)
-    pieces = [down_a, down_b, down_c]
-    me = f * 4 + lax.axis_index(TENSOR)
-    valid_rows = valid_mask[0].astype(WIDE)[:, None]
     vmem = {
-        "slots": slots,
-        "x": rows_in,
-        "probs": probs_all,
-        "residual": residual,
+        "shard": wq,
+        "wo_shard": wo,
+        "near_route": near_route,
+        "tokens": tokens[0],
         "teacher": teacher[0],
-        "valid": valid_rows,
-        "scale": jnp.full((8, 128), total_tokens / valid_total, WIDE),
-        "gain": gain_b,
-        "router": router_wide[:, :expert_count].T,
-        "probs_own": lax.dynamic_index_in_dim(probs_all, me, 0, False),
-        "tokens": tokens[0],
-        "gain_one": gain_a,
-        "second_in": second_in,
-        "projected": projected.reshape(rows, qkv_width),
-        "log_total": logarithm_total.reshape(head_count, rows).T,
-        "mixed": mixed,
         "valid_row": valid_mask,
-        "qkv": gathered_blocks,
-        "wo": lax.dynamic_index_in_dim(wo_all, z, 1, False),
     }
     hbm = {"up": expert_up, "down": expert_down}
-    made = layer(heads, capacity, head_count, pieces, vmem, hbm)
+    made = layer(heads, expert_count, capacity, routes.shape[2], head_count, vmem, hbm)
+    me = f * 4 + lax.axis_index(TENSOR)
     result, tokens_grad, dense_out = made.result, made.tokens_grad, made.dense_out
-    loss_terms = (jnp.sum(made.loss) * (total_images / (valid_total * width)))[None]
+    loss_terms = jnp.sum(made.loss)[None]
     own_gains = lax.dynamic_slice_in_dim(made.gain_out, me * block, block, 1)
     scalars = jnp.stack([f, mine, theirs]).astype(jnp.int32)
     up_grad, down_grad = finish(

time: 315 us -> 299 us (0.949)
  Pallas kernels: 273 us -> 284 us
  local copies, waits for them, and re-layouts: 23.4 us -> 12.7 us
  waiting for transfers between devices: 5.1 us -> 0 us
  other arithmetic: 4.89 us -> 1.19 us
  starting transfers between devices: 3.64 us -> 0 us
    pallas_call x1, Pallas kernels: 196 us -> 270 us  [named_call(): pl.pallas_call(functools.partial(kernel, names), out_shape=[o[0] for o in...]
    pallas_call x2 -> x0, Pallas kernels: 63.5 us -> none  [remote_call(): pl.pallas_call(kernel, out_shape=outs, in_specs=[hbm if i in in_hbm else...]
    ppermute x2 -> x0, waiting for transfers between devices: 5.1 us -> none  [swap(): return lax.ppermute(values, FSDP, [(0, 1), (1, 0)])]
    ppermute x2 -> x0, starting transfers between devices: 3.64 us -> none  [swap(): return lax.ppermute(values, FSDP, [(0, 1), (1, 0)])]
    dynamic_slice x2 -> x0, local copies, waits for them, and re-layouts: 3.58 us -> none  [the longest x1 2.4 us: fast(): lax.dynamic_slice_in_dim(expert_down, theirs + first_chunk, second_chunk, 0)]
    unnamed x44 -> x14, local copies, waits for them, and re-layouts: 6.41 us -> 5.07 us
  transfers between devices with their start and end apart: 2 -> 0, of which waited for: 1 -> 0; matrix products, arithmetic and copies ran while one was open for 4% -> 0% of each run, Pallas kernels for 14% -> 0%
where the time goes in v4:
time: 299 us
  Pallas kernels  284 us (95%)
  local copies, waits for them, and re-layouts  12.7 us (4%)
    pallas_call x1, Pallas kernels, named_call(): pl.pallas_call(functools.partial(kernel, names), out_shape=[o[0] for o in...  270 us
    pallas_call x1, Pallas kernels, finish(): pl.pallas_call(finish_kernel, out_shape=[shape((2 * kept, half, hidden_wi...  13.8 us

profile of v4, /device:TPU:0, one launch (start us, length us, event | category | flops | bytes accessed | tf_op | source)
XLA Modules:
  0.0 298.6 jit_solution(8535624248831920066)
XLA Ops:
  0.6 1.1 copy.30
  1.7 0.2 copy.34
  1.9 0.8 copy.31
  2.7 0.8 copy.32
  3.5 0.8 copy.33
  4.2 0.8 concatenate.3.refs_0_
  5.0 1.5 copy.35
  6.5 1.3 pad.4.refs_2_
  7.9 270.2 %shard_map.186 = (bf16[4,64,768]{2,1,0:T(8,128)(2,1)}, f32[4,8,128]{2,1,0:T(8,128)}, f32[4,64,768]{2,1,0:T(8,128)}, f32[96,896]{1,0:T(8,128)}, f32[2,768]{1,0:T(...) custom-call(bf16[96,768]{1,0:T(8,128)(2,1)} %concatenate.3.refs_0_, ...), custom_call_target="tpu_custom_call" | custom-call | bytes 840000000 | tf_op jit(solution)/shard_map/pallas_call | solution.py:1273
  278.1 0.6 pad_add_fusion.s
  278.6 0.0 copy-start.1
  278.6 0.0 copy-start.3
  278.6 13.8 %shard_map.187 = (f32[8,384,768]{2,1,0:T(8,128)}, f32[8,768,384]{2,1,0:T(8,128)}) custom-call(s32[3]{0:T(128)} %pad_add_fusion.s, bf16[4,256,384]{2,1,0:T(8,128)(2,1)} %get-tuple-element.29.near, bf16[4,256,768]{2,1,0:T(8,128)(2,1)} %get-tuple-element.30.near_pre, bf16[4,256,384]{2,1,0:T(8,128)(2,1)} %get-tuple-element.31.far, ...), custom_call_target="tpu_custom_call" | custom-call | bytes 24000000 | tf_op jit(solution)/shard_map/pallas_call | solution.py:1454
  292.4 0.0 copy-start.2
  292.4 0.0 copy-start
  292.5 0.8 constant_dynamic-slice_fusion
  293.3 0.5 slice_bitcast_fusion.1
  293.8 0.0 copy-done.1
  293.8 0.1 copy.37
  293.9 0.9 copy.39
  294.8 0.1 slice_bitcast_fusion
  294.9 0.7 copy.38
  295.7 0.7 copy.40
  296.3 0.0 copy-done.3
  296.3 0.6 reduce_sum.9
  297.0 0.0 copy-done.2
  297.0 0.7 copy.43
  297.7 0.0 copy-done
  297.7 0.9 copy.44
  (4 shorter events, 0.0 us)
Async XLA Ops:
  278.6 15.1 %copy-start.1 = (f32[96,896]{1,0:T(8,128)S(1)}, f32[96,896]{1,0:T(8,128)}, u32[]{:S(2)}) copy-start(f32[96,896]{1,0:T(8,128)} %get-tuple-element.28) | copy-start | bytes 1032196
  278.6 17.7 %copy-start.3 = (f32[4,8,128]{2,1,0:T(8,128)S(1)}, f32[4,8,128]{2,1,0:T(8,128)}, u32[]{:S(2)}) copy-start(f32[4,8,128]{2,1,0:T(8,128)} %get-tuple-element.25) | copy-start | bytes 49156
  292.4 4.5 %copy-start.2 = (bf16[4,64,768]{2,1,0:T(8,128)(2,1)S(1)}, bf16[4,64,768]{2,1,0:T(8,128)(2,1)}, u32[]{:S(2)}) copy-start(bf16[4,64,768]{2,1,0:T(8,128)(2,1)} %get-tuple-element.24) | copy-start | bytes 1179652
  292.4 5.3 %copy-start = (f32[4,64,768]{2,1,0:T(8,128)S(1)}, f32[4,64,768]{2,1,0:T(8,128)}, u32[]{:S(2)}) copy-start(f32[4,64,768]{2,1,0:T(8,128)} %get-tuple-element.26) | copy-start | bytes 2359300

commit v5 on v4

--- a/solution.py
+++ b/solution.py
@@ -668,6 +668,9 @@
     ]
 
     def to_heads(k):
+        if k == chunks - 1:
+            r.hidden_copies.append(send_hidden(place, links, r, 1))
+
         def keep(rows, part_of, values):
             image_sum[k, rows, pl.ds(part_of * half, half)] = values.astype(LOW)
 
@@ -757,8 +760,17 @@
     oq, oo, counts, slots = r.qkv, r.wo_all, r.counts, r.slots
     kept = r.w_far.shape[0]
     theirs = (1 - f) * kept
-    oq[me] = r.shard[...]
-    oo[me, z] = r.wo_shard[...]
+    rows = [r.router_in[...], r.gain_one_in[...], r.gain_two_in[...]]
+    rows = [row.astype(WIDE) for row in rows]
+    block = oq.shape[1]
+    rows.append(jnp.zeros((128 - sum(row.shape[0] for row in rows), block), WIDE))
+    oq[me, :, 0:128] = jnp.transpose(jnp.concatenate(rows, 0)).astype(LOW)
+    qkv = jnp.concatenate([r.qkv_in[h] for h in range(r.qkv_in.shape[0])], 1)
+    oq[me, :, pl.ds(128, qkv.shape[1])] = qkv
+    rest = oq.shape[2] - 128 - qkv.shape[1]
+    if rest:
+        oq[me, :, pl.ds(128 + qkv.shape[1], rest)] = jnp.zeros((block, rest), LOW)
+    oo[me, z] = jnp.transpose(r.out_in[...].astype(WIDE)).astype(LOW)
     counts[me] = jnp.broadcast_to(jnp.sum(r.valid_row[...].astype(WIDE), -1, keepdims=True), (8, 128))
     half, mid = oq.shape[2] // 2, heads // 2
     main = PlaneGather(
@@ -841,10 +853,11 @@
     both = [jnp.where(first, near, far), jnp.where(first, far, near)]
     chosen = []
     for route in both:
-        hits = route[0:1] == ids
-        for c in range(1, r.choices):
-            hits = hits | (route[c : c + 1] == ids)
-        chosen.append(hits)
+        hits = []
+        for c in range(route.shape[1]):
+            row = jnp.concatenate([route[k, c : c + 1] for k in range(4)], 1)
+            hits.append(row == ids)
+        chosen.append(functools.reduce(jnp.logical_or, hits))
     chosen = jnp.concatenate(chosen, 0)
     count = chosen.astype(WIDE)
     before = lax.broadcasted_iota(jnp.int32, (128, 128), 0)
@@ -911,6 +924,10 @@
 
 
 FRONT_COPIES = 2 * GATHER_COPIES + 7 + 1 + 1 + 2 + 4 + 7
+
+
+def send_hidden(place, links, r, i):
+    return links.send(r.hidden.at[i], r.far_hidden.at[i], place.x_peer)
 
 
 def experts_part(place, links, loads, weights, down_far, r):
@@ -974,6 +991,8 @@
         down_far[i].wait_recv()
         values, slopes = gelu_parts(own[i] + arrived[i].astype(WIDE))
         hidden[i] = values.astype(LOW)
+        if i == 0:
+            r.hidden_copies.append(send_hidden(place, links, r, 0))
         own[i] = slopes
         for weight, f in ((w_near, place.f), (w_far, 1 - place.f)):
             out = (dot(hidden[i], weight[i]) * gates[i]).astype(LOW)
@@ -988,19 +1007,23 @@
     return stores[kept - 2 : kept] + stores[2 * kept - 2 :]
 
 
-def experts_back_part(place, links, loads, r):
+def experts_back_part(place, links, loads, chunks, r):
     pick_near, pick_far, hidden, slope, gates = r.pick_near, r.pick_far, r.hidden, r.own, r.gates
     w_up, w_near, w_far, group = r.w_up, r.w_near, r.w_far, r.group
     pre_near, pre_far, out_grad = r.away, r.arrived, r.out_grad
     side = r.weighted.shape[2] // 2
     rows_near = r.weighted.at[:, :, pl.ds(0, side)]
     rows_far = r.weighted.at[:, :, pl.ds(side, side)]
-    send_held = r.w_far
-    kept, pair, width = out_grad.shape
-    capacity, half = pair // 2, width // 2
+    kept, pair, half = out_grad.shape
+    capacity, width = pair // 2, 2 * half
     first = pl.ds(pl.multiple_of(place.f * half, half), half)
     second = pl.ds(pl.multiple_of((1 - place.f) * half, half), half)
-    sent = []
+    sent = {}
+
+    def send(g, i):
+        piece = pl.ds(g * capacity, capacity)
+        sent[g, i] = links.send(pre_near.at[i, piece], pre_far.at[i, piece], place.x_peer)
+
     for i in range(kept):
         rows = slice(i * capacity, (i + 1) * capacity)
         for g in range(2):
@@ -1011,142 +1034,204 @@
         raw = dot(r.slot_rows[:, first], w_near[i], (1, 1))
         raw = raw + dot(r.slot_rows[:, second], w_far[i], (1, 1))
         pre_near[i] = (raw * gates[i] * slope[i]).astype(LOW)
-        sent.append(links.send(pre_near.at[i], pre_far.at[i], place.x_peer))
-        out_grad[i] = (r.slot_rows[...].astype(WIDE) * gates[i]).astype(LOW)
+        send(0, i)
+        out_grad[i] = (r.slot_rows[:, first].astype(WIDE) * gates[i]).astype(LOW)
         gate_grad = jnp.sum(raw * hidden[i].astype(WIDE), -1, keepdims=True)
         for g in range(2):
             terms = gate_grad[g * capacity : (g + 1) * capacity]
             terms = terms * pick_near[g, rows].astype(WIDE)
             r.gate_rows[g, i : i + 1] = jnp.sum(terms, 0, keepdims=True)
-    bulk = []
     for i in range(kept):
-        send_held[i] = dot(hidden[i], out_grad[i, :, second], (0, 0)).astype(LOW)
-    early = pl.ds(0, kept // 2)
-    bulk = [links.send(send_held.at[early], r.down_far.at[early], place.x_peer)]
+        send(1, i)
+    t = 2 * place.y + place.c
+    r.gate_in[t] = r.gate_rows[...]
+    shared = [
+        links.send(r.gate_rows, r.gate_in.at[t], d) for d in place.tensor_peers()
+    ]
     stores = [
-        loads.start(r.hidden, r.hidden_out),
+        loads.start(r.hidden, r.near_hidden),
         loads.start(pre_near, r.near_pre),
-        loads.start(out_grad, r.grad_out),
+        loads.start(out_grad, r.near_grad),
     ]
 
-    def through_up(far, i, pre, rows_out):
-        back = dot(pre[i], w_up[far, i], (1, 1)).astype(LOW)
+    for i in range(kept):
+        back = dot(pre_near[i], w_up[0, i], (1, 1)).astype(LOW)
         rows = slice(i * capacity, (i + 1) * capacity)
         for g in range(2):
-            rows_out[g, rows] = back[g * capacity : (g + 1) * capacity]
-
+            rows_near[g, rows] = back[g * capacity : (g + 1) * capacity]
+    for copy in shared:
+        copy.wait_recv()
+    spread = share_gates(place, links, r)
+    experts = place.z * 2 * kept + (1 - place.f) * kept
     for i in range(kept):
-        through_up(0, i, pre_near, rows_near)
-    for i in range(kept):
-        sent[i].wait_recv()
-        through_up(1, i, pre_far, rows_far)
-    stores.append(loads.start(pre_far, r.far_pre))
+        rows = slice(i * capacity, (i + 1) * capacity)
+        for g in range(2):
+            hot = pick_far[g, rows]
+            chances = [r.probs[4 * g + k, pl.ds(experts + i, 1), :] for k in range(4)]
+            chances = jnp.concatenate(chances, 1)
+            gate = jnp.sum(hot.astype(WIDE) * chances, -1, keepdims=True)
+            rows_in = group[4 * g : 4 * g + 4, :, first].reshape(pick_far.shape[2], half)
+            into = slice(g * capacity, (g + 1) * capacity)
+            r.far_held[i, into] = (dot(hot, rows_in) * gate).astype(LOW)
+    stores.append(loads.start(r.far_held, r.far_grad))
+    for i in range(2, kept):
+        r.hidden_copies.append(send_hidden(place, links, r, i))
+    sums = RowSum(links, place, r)
+    sums.spread = spread
+    steps = {0: sums.to_y, 1: sums.to_heads, kept - 1: sums.total}
     for g in range(2):
+        into = slice(g * capacity, (g + 1) * capacity)
+        for i in range(kept):
+            sent[g, i].wait_recv()
+            back = dot(pre_far[i, into], w_up[1, i], (1, 1)).astype(LOW)
+            rows_far[g, i * capacity : (i + 1) * capacity] = back
+            if g and i in steps:
+                for k in range(chunks):
+                    steps[i](0, k)
         near = dot(pick_near[g], rows_near[g], (0, 0))
         both = (near + dot(pick_far[g], rows_far[g], (0, 0))).astype(LOW)
         r.x[g] = both.reshape(r.x.shape[1:])
-    return stores, bulk
-
-
-def back_part(place, links, chunks, bulk, r):
+        for k in range(chunks):
+            sums.start(g, k)
+    stores.append(loads.start(pre_far, r.far_pre))
+    return stores, sums
+
+
+def share_gates(place, links, r):
+    t = 2 * place.y + place.c
+    r.gate_sum[...] = sum(r.gate_in[k] for k in range(4))
+    rows_all = r.probs_own.shape[1]
+    rows_of = pl.ds(pl.multiple_of(t * rows_all, rows_all), rows_all)
+    r.gate_all[place.z, place.f] = r.gate_sum[place.f, :, rows_of]
+    return [
+        links.send(r.gate_sum.at[d[FSDP], :, rows_of], r.gate_all.at[place.z, place.f], d)
+        for d in place.owners()
+    ]
+
+
+def router_back(r):
+    experts, rows_all = r.probs_own.shape
+    width = r.residual.shape[1]
+    chances = r.probs_own[...]
+    prob_grad = r.gate_all[...].reshape(experts, rows_all)
+    logit_grad = chances * (prob_grad - jnp.sum(chances * prob_grad, 0, keepdims=True))
+    r.logit_grads[...] = logit_grad.astype(LOW)
+    r.logit_rows[...] = dot(r.logit_grads[...], r.router[...], (0, 0))
+    router_grad = dot(r.second_in[...], r.logit_grads[...], (0, 1))
+    spare = jnp.zeros((width, 128 - experts), WIDE)
+    router_grad = jnp.concatenate([router_grad, spare], 1).astype(LOW)
+    blocks, block, dense_width = r.dense.shape
+    r.dense[:, :, pl.ds(dense_width - 128, 128)] = router_grad.reshape(blocks, block, 128)
+
+
+class RowSum:
+    def __init__(self, links, place, r):
+        self.links, self.place, self.r = links, place, r
+        self.into, self.beside, self.along, self.cross = {}, {}, {}, {}
+        self.rows = r.x.shape[3]
+        self.own = self.rows // place.heads
+
+    def start(self, g, k):
+        source = self.r.x.at[g, :, 1 - self.place.c, :, pl.ds(k * 128, 128)]
+        self.into[g, k] = self.links.send(
+            source, self.r.core_in.at[k, g], self.place.core_peer
+        )
+
+    def to_y(self, g, k):
+        self.into[g, k].wait_recv()
+        rc, c, y = self.r.core_in.at[k, g], self.place.c, self.place.y
+
+        def add(rows):
+            here = self.r.x[g, :, c, rows, pl.ds(k * 128, 128)].astype(WIDE)
+            rc[:, rows, :] = (rc[:, rows, :].astype(WIDE) + here).astype(LOW)
+
+        in_rows(self.rows, 64, add)
+        self.beside[g, k] = self.links.send(
+            rc.at[1 - y], self.r.y_in.at[k, g], self.place.y_peer
+        )
+
+    def to_heads(self, g, k):
+        self.beside[g, k].wait_recv()
+        y_in, core_in = self.r.y_in.at[k, g], self.r.core_in.at[k, g, self.place.y]
+
+        def add(rows):
+            both = y_in[rows, :].astype(WIDE) + core_in[rows, :].astype(WIDE)
+            y_in[rows, :] = both.astype(LOW)
+
+        in_rows(self.rows, 64, add)
+        own = self.own
+        self.along[g, k] = all_heads(
+            self.links,
+            self.place,
+            lambda n, to: (
+                y_in.at[pl.ds(pl.multiple_of(to * own, own), own)],
+                self.r.far.at[k, n, g],
+            ),
+        )
+
+    def total(self, g, k):
+        for copy in self.along[g, k]:
+            copy.wait_recv()
+        z, own = self.place.z, self.own
+        total = self.r.y_in[k, g, pl.ds(pl.multiple_of(z * own, own), own), :].astype(WIDE)
+        for n in range(self.place.heads - 1):
+            total = total + self.r.far[k, n, g].astype(WIDE)
+        self.r.pair[k, g] = total.astype(LOW)
+
+    def to_x(self, k):
+        self.cross[k] = self.links.send(
+            self.r.pair.at[k, 1 - self.place.f], self.r.x_in.at[k], self.place.x_peer
+        )
+
+
+def back_part(place, links, chunks, sums, r):
     heads, f, y, z = place.heads, place.f, place.y, place.z
-    t, me = 2 * y + place.c, place.image(0, 0, 0)
-    part, gate_part, probs, valid = r.x, r.gate_rows, r.probs_own, r.valid_row
-    residual, gain, router, final_grad, tokens = (r.residual, r.gain, r.router, r.final_grad, r.tokens)
-    gain_one, second_in, projected, log_total, mixed = (r.gain_one, r.second_in, r.projected, r.log_total, r.mixed)
-    qkv, wo, tokens_grad, dense_out, gain_out = (r.qkv, r.wo_all, r.tokens_grad, r.dense_out, r.gain_out)
-    core_in, y_in, far, pair, x_in = (r.core_in, r.y_in, r.far, r.pair, r.x_in)
-    gate_in, gate_sum, gate_all, logit_rows, logit_grads = (r.gate_in, r.gate_sum, r.gate_all, r.logit_rows, r.logit_grads)
-    attended, first_in, projected_grad, first_part, dense = (r.attended, r.first_in, r.projected_grad, r.first_part, r.dense)
-    dense_core, xa, ya, yb, xb = (r.dense_core, r.xa, r.ya, r.yb, r.xb)
-    first_far, rounded, gain_part, gain_plane, gain_heads = (r.first_far, r.rounded, r.gain_part, r.gain_plane, r.gain_heads)
-    tensor_peers, owners = place.tensor_peers(), place.owners()
+    me, valid = place.image(0, 0, 0), r.valid_row
+    residual, gain, final_grad, tokens = r.residual, r.gain, r.final_grad, r.tokens
+    gain_one, projected, log_total, mixed = r.gain_one, r.projected, r.log_total, r.mixed
+    qkv, wo, tokens_grad, dense_out, gain_out = (
+        r.qkv,
+        r.wo_all,
+        r.tokens_grad,
+        r.dense_out,
+        r.gain_out,
+    )
+    pair, x_in, logit_rows, attended, first_in = (
+        r.pair,
+        r.x_in,
+        r.logit_rows,
+        r.attended,
+        r.first_in,
+    )
+    projected_grad, first_part, dense, dense_core = (
+        r.projected_grad,
+        r.first_part,
+        r.dense,
+        r.dense_core,
+    )
+    xa, ya, yb, xb, first_far, rounded = r.xa, r.ya, r.yb, r.xb, r.first_far, r.rounded
+    gain_part, gain_plane, gain_heads = r.gain_part, r.gain_plane, r.gain_heads
     rows_all, width = residual.shape
     half = width // 2
     own = rows_all // heads
-    into, beside, along, cross = {}, {}, {}, {}
-    for k in range(chunks):
-        source = part.at[:, :, 1 - place.c, :, pl.ds(k * 128, 128)]
-        into[k] = links.send(source, core_in.at[k], place.core_peer)
-    gate_in[t] = gate_part[...]
-    shared = [links.send(gate_part, gate_in.at[t], d) for d in tensor_peers]
     mine = pl.ds(pl.multiple_of(z * own, own), own)
-
-    def to_y(k):
-        into[k].wait_recv()
-        rc = core_in.at[k]
-
-        def add(rows):
-            here = part[:, :, place.c, rows, pl.ds(k * 128, 128)].astype(WIDE)
-            rc[:, :, rows, :] = (rc[:, :, rows, :].astype(WIDE) + here).astype(LOW)
-
-        in_rows(rows_all, 32, add)
-        beside[k] = links.send(rc.at[:, 1 - y], y_in.at[k], place.y_peer)
-
-    def to_heads(k):
-        beside[k].wait_recv()
-
-        def add(rows):
-            both = y_in[k, :, rows, :].astype(WIDE) + core_in[k, :, y, rows, :].astype(WIDE)
-            y_in[k, :, rows, :] = both.astype(LOW)
-
-        in_rows(rows_all, 64, add)
-        along[k] = all_heads(
-            links,
-            place,
-            lambda n, to: (
-                y_in.at[k, :, pl.ds(pl.multiple_of(to * own, own), own)],
-                far.at[k, n],
-            ),
-        )
-
-    def to_x(k):
-        for copy in along[k]:
-            copy.wait_recv()
-        total = y_in[k, :, mine, :].astype(WIDE)
-        for n in range(heads - 1):
-            total = total + far[k, n].astype(WIDE)
-        pair[k] = total.astype(LOW)
-        cross[k] = links.send(pair.at[k, 1 - f], x_in.at[k], place.x_peer)
-
-    to_y(0)
-    for copy in shared:
-        copy.wait_recv()
-    gate_sum[...] = sum(gate_in[k] for k in range(4))
-    kept = gate_sum.shape[1]
-    rows_of = pl.ds(pl.multiple_of(t * rows_all, rows_all), rows_all)
-    gate_all[z, f] = gate_sum[f, :, rows_of]
-    spread = [
-        links.send(gate_sum.at[d[FSDP], :, rows_of], gate_all.at[z, f], d) for d in owners
-    ]
-    to_y(1)
-    to_heads(0)
-    for k in range(2, chunks):
-        to_y(k)
-        to_heads(k - 1)
-        to_x(k - 2)
-    for copy in spread:
-        copy.wait_recv()
-    chances = probs[...]
-    prob_grad = gate_all[...].reshape(2 * heads * kept, rows_all)
-    logit_grad = chances * (prob_grad - jnp.sum(chances * prob_grad, 0, keepdims=True))
-    logit_grads[...] = logit_grad.astype(LOW)
-    logit_rows[...] = dot(logit_grads[...], router[...], (0, 0))
+    blocks, block, dense_width = dense.shape
+    qkv_width = projected.shape[1]
+    for step in range(chunks + 2):
+        if step == 2:
+            for copy in sums.spread:
+                copy.wait_recv()
+            router_back(r)
+        for k in range(chunks):
+            if step == k:
+                sums.to_y(1, k)
+            if step == k + 1:
+                sums.to_heads(1, k)
+            if step == k + 2:
+                sums.total(1, k)
+                sums.to_x(k)
     normed, spread_two = normalize(residual[mine, :])
-    router_grad = dot(second_in[...], logit_grads[...], (0, 1))
-    spare = jnp.zeros((width, 128 - router_grad.shape[1]), WIDE)
-    router_grad = jnp.concatenate([router_grad, spare], 1).astype(LOW)
-    blocks, block = dense.shape[:2]
-    qkv_width = projected.shape[1]
-    dense_width = dense.shape[2]
-    dense[:, :, pl.ds(dense_width - 128, 128)] = router_grad.reshape(blocks, block, 128)
-
-    to_heads(chunks - 1)
-    to_x(chunks - 2)
-    to_x(chunks - 1)
-    early = r.w_far.shape[0] // 2
-    late = pl.ds(early, r.w_far.shape[0] - early)
-    bulk.append(links.send(r.w_far.at[late], r.down_far.at[late], place.x_peer))
+    cross = sums.cross
     near = jnp.concatenate([pair[k, f].astype(WIDE) for k in range(chunks)], 1)
     for k in range(chunks):
         cross[k].wait_recv()
@@ -1190,7 +1275,11 @@
     weight = qkv[:, :, pl.ds(128, qkv_width)].reshape(width, qkv_width)
     back = dot(projected_grad[...], weight, (1, 1))
     first_part[...] = back.astype(LOW).reshape(heads, own, width)
-    along = all_heads(links, place, lambda n, to: (first_part.at[to], first_far.at[n]))
+    cuts = [pl.ds(q * own // 2, own // 2) for q in range(2)]
+    along = [
+        all_heads(links, place, lambda n, to: (first_part.at[to, q], first_far.at[n, q]))
+        for q in cuts
+    ]
     dense_now = jnp.concatenate(
         [
             dot(first_in[...], projected_grad[...], (0, 0)).astype(LOW),
@@ -1210,20 +1299,24 @@
         copy.wait_recv()
     gain_heads[z] = sum(gain_plane[i] for i in range(8))
     gains = all_heads(links, place, lambda n, to: (gain_heads.at[z], gain_heads.at[z]))
-    normed, spread_one = normalize(tokens[mine, :].astype(WIDE))
-    for copy in along:
-        copy.wait_recv()
-    first_grad = first_part[z].astype(WIDE)
-    for n in range(heads - 1):
-        first_grad = first_grad + first_far[n].astype(WIDE)
-    weighted = first_grad * gain_one[...]
-    inner = (
-        weighted
-        - jnp.mean(weighted, -1, keepdims=True)
-        - normed * jnp.mean(weighted * normed, -1, keepdims=True)
-    )
-    rounded[z] = (total_grad + inner * spread_one).astype(LOW)
-    along = all_heads(links, place, lambda n, to: (rounded.at[z], rounded.at[z]))
+    ends = []
+    for n_cut, q in enumerate(cuts):
+        at = pl.ds(pl.multiple_of(z * own + n_cut * own // 2, own // 2), own // 2)
+        normed, spread_one = normalize(tokens[at, :].astype(WIDE))
+        for copy in along[n_cut]:
+            copy.wait_recv()
+        first_grad = first_part[z, q].astype(WIDE)
+        for n in range(heads - 1):
+            first_grad = first_grad + first_far[n, q].astype(WIDE)
+        weighted = first_grad * gain_one[...]
+        inner = (
+            weighted
+            - jnp.mean(weighted, -1, keepdims=True)
+            - normed * jnp.mean(weighted * normed, -1, keepdims=True)
+        )
+        here = total_grad[n_cut * own // 2 : (n_cut + 1) * own // 2]
+        rounded[z, q] = (here + inner * spread_one).astype(LOW)
+        ends += all_heads(links, place, lambda n, to: (rounded.at[z, q], rounded.at[z, q]))
 
     def keep(rows, columns, values):
         dense_out[rows, columns] = values
@@ -1232,21 +1325,22 @@
     for copy in gains:
         copy.wait_recv()
     gain_out[...] = sum(gain_heads[i] for i in range(heads))
-    for copy in along:
+    for copy in ends:
         copy.wait_recv()
     for i in range(heads):
         tokens_grad[i] = rounded[i].astype(WIDE)
-    for copy in bulk:
+    for copy in r.hidden_copies:
         copy.wait_recv()
 
 
-def layer_kernel(heads, chunks, choices, names, *refs):
-    r = types.SimpleNamespace(**dict(zip(names, refs)), choices=choices)
+def layer_kernel(heads, chunks, small, names, *refs):
+    r = types.SimpleNamespace(**dict(zip(names, refs)), hidden_copies=[])
     place = Place(heads)
     links = Links(r.send_sems, r.recv_sems)
     loads = Loads(r.load_sems)
     kept = r.w_far.shape[0]
     mine, theirs = place.f * kept, (1 - place.f) * kept
+    first = [loads.start(getattr(r, name + "_hbm"), getattr(r, name)) for name in small]
     ups = {}
     for far in (1, 0):
         for i in range(kept):
@@ -1254,14 +1348,16 @@
             ups[far, i] = loads.start(r.up.at[source], r.w_up.at[far, i])
     nears = [loads.start(r.down.at[mine + i], r.w_near.at[i]) for i in range(kept)]
     place.greet(place.everyone())
+    for copy in first:
+        copy.wait()
     from_x, down_far = front_part(place, links, r)
     held = experts_part(place, links, loads, (ups, nears), down_far, r)
     extra = combine_part(place, links, chunks, r)
     links.left(from_x)
-    stores, bulk = experts_back_part(place, links, loads, r)
+    stores, sums = experts_back_part(place, links, loads, chunks, r)
     for copy in extra:
         copy.wait_recv()
-    back_part(place, links, chunks, bulk, r)
+    back_part(place, links, chunks, sums, r)
     for copy in held + stores:
         copy.wait()
     links.drain()
@@ -1291,156 +1387,168 @@
     return types.SimpleNamespace(**dict(zip(outs, made)))
 
 
-def layer(heads, experts, capacity, choices, head_count, vmem, hbm):
-    rows, width = vmem["tokens"].shape
+def layer(heads, experts, capacity, small, hbm):
+    rows, width = small["tokens"].shape
     own, half, chunks = rows // heads, width // 2, width // 256
     local_experts, _, hidden_width = hbm["up"].shape
     kept, pair, group_rows = local_experts // 2, 2 * capacity, 4 * rows
-    block, mixed_width = vmem["wo_shard"].shape
+    mixed_width, block = small["out_in"].shape
+    head_count = small["qkv_in"].shape[0]
     qkv_width = 3 * mixed_width
+    gathered_width = 128 + qkv_width + -(128 + qkv_width) % 256
     dense_width = qkv_width + mixed_width + 128
     cut = 128 * ((dense_width // 128 + 1) // 2)
-    ins = {name: (array, False) for name, array in vmem.items()}
-    ins.update({name: (array, True) for name, array in hbm.items()})
-    outs = {
-        "result": (shape((heads, own, width)), False),
-        "loss": (shape((heads, 8, 128), WIDE), False),
-        "tokens_grad": (shape((heads, own, width), WIDE), False),
-        "dense_out": (shape((block, dense_width), WIDE), False),
-        "gain_out": (shape((2, width), WIDE), False),
-        "down_far": (shape((kept, hidden_width, half)), True),
-        "hidden_out": (shape((kept, pair, hidden_width)), True),
-        "near_out": (shape((kept, pair, half)), True),
-        "far_out": (shape((kept, pair, half)), True),
-        "near_pre": (shape((kept, pair, hidden_width)), True),
-        "far_pre": (shape((kept, pair, hidden_width)), True),
-        "grad_out": (shape((kept, pair, width)), True),
-    }
-    low = {
-        "pick_near": (2, kept * capacity, group_rows),
-        "pick_far": (2, kept * capacity, group_rows),
-        "buffer_near": (2, pair, half),
-        "buffer_far": (2, pair, half),
-        "hidden": (kept, pair, hidden_width),
-        "weighted": (2, kept * capacity, width),
-        "away": (kept, pair, hidden_width),
-        "arrived": (kept, pair, hidden_width),
-        "w_up": (2, kept, half, hidden_width),
-        "w_near": (kept, hidden_width, half),
-        "w_far": (kept, hidden_width, half),
-        "part": (2, 2, 2, rows, width),
-        "group": (8, rows, width),
-        "sum_core": (chunks, 2, 2, rows, 256),
-        "sum_xa": (chunks, 2, rows, 128),
-        "sum_ya": (chunks, rows, 128),
-        "sum_yb": (chunks, 2, rows, 128),
-        "sum_xb": (chunks, rows, 128),
-        "image_sum": (chunks, rows, 256),
-        "image_far": (chunks, heads - 1, own, 256),
-        "out_grad": (kept, pair, width),
-        "slot_rows": (pair, width),
-        "x": (2, 2, 2, rows, half),
-        "other_half": (rows, half),
-        "qkv": (8, *vmem["shard"].shape),
-        "wo_all": (8, heads, block, mixed_width),
-        "router": (experts, width),
-        "projected": (rows, qkv_width),
-        "mixed": (rows, mixed_width),
-        "all_mixed": (heads, rows, mixed_width),
-        "second_in": (rows, width),
-        "core_in": (chunks, 2, 2, rows, 128),
-        "y_in": (chunks, 2, rows, 128),
-        "far": (chunks, heads - 1, 2, own, 128),
-        "pair": (chunks, 2, own, 128),
-        "x_in": (chunks, own, 128),
-        "logit_grads": (experts, rows),
-        "attended": (rows, width),
-        "first_in": (rows, width),
-        "projected_grad": (rows, qkv_width),
-        "first_part": (heads, own, width),
-        "dense": (8, block, dense_width),
-        "dense_core": (4, block, dense_width),
-        "xa": (2, block, cut),
-        "ya": (block, cut),
-        "yb": (2, block, dense_width - cut),
-        "xb": (block, dense_width - cut),
-        "first_far": (heads - 1, own, width),
-        "rounded": (heads, own, width),
-    }
-    wide = {
-        "gates": (kept, pair, 1),
-        "counts": (8, 8, 128),
-        "scale": (8, 128),
-        "loss_scale": (8, 128),
-        "valid": (rows, 8),
-        "gain_one": (1, width),
-        "gain": (1, width),
-        "log_total": (rows, head_count),
-        "residual": (rows, width),
-        "probs": (8, experts, rows),
-        "probs_own": (experts, rows),
-        "own": (kept, pair, hidden_width),
-        "final_grad": (own, width),
-        "gate_rows": (2, kept, group_rows),
-        "gate_in": (4, 2, kept, group_rows),
-        "gate_sum": (2, kept, group_rows),
-        "gate_all": (heads, 2, kept, rows),
-        "logit_rows": (rows, width),
-        "gain_part": (2, width),
-        "gain_plane": (8, 2, width),
-        "gain_heads": (heads, 2, width),
-    }
+    ins = {name: (array, True) for name, array in hbm.items()}
+    ins.update({name + "_hbm": (array, True) for name, array in small.items()})
+    outs = dict(
+        result=(shape((heads, own, width)), False),
+        loss=(shape((heads, 8, 128), WIDE), False),
+        tokens_grad=(shape((heads, own, width), WIDE), False),
+        dense_out=(shape((block, dense_width), WIDE), False),
+        gain_out=(shape((2, width), WIDE), False),
+        near_out=(shape((kept, pair, half)), True),
+        near_pre=(shape((kept, pair, hidden_width)), True),
+        near_hidden=(shape((kept, pair, hidden_width)), True),
+        near_grad=(shape((kept, pair, half)), True),
+        far_out=(shape((kept, pair, half)), True),
+        far_pre=(shape((kept, pair, hidden_width)), True),
+        far_hidden=(shape((kept, pair, hidden_width)), True),
+        far_grad=(shape((kept, pair, half)), True),
+    )
+    low = dict(
+        pick_near=(2, kept * capacity, group_rows),
+        pick_far=(2, kept * capacity, group_rows),
+        buffer_near=(2, pair, half),
+        buffer_far=(2, pair, half),
+        hidden=(kept, pair, hidden_width),
+        weighted=(2, kept * capacity, width),
+        away=(kept, pair, hidden_width),
+        arrived=(kept, pair, hidden_width),
+        w_up=(2, kept, half, hidden_width),
+        w_near=(kept, hidden_width, half),
+        w_far=(kept, hidden_width, half),
+        part=(2, 2, 2, rows, width),
+        group=(8, rows, width),
+        sum_core=(chunks, 2, 2, rows, 256),
+        sum_xa=(chunks, 2, rows, 128),
+        sum_ya=(chunks, rows, 128),
+        sum_yb=(chunks, 2, rows, 128),
+        sum_xb=(chunks, rows, 128),
+        image_sum=(chunks, rows, 256),
+        image_far=(chunks, heads - 1, own, 256),
+        out_grad=(kept, pair, half),
+        far_held=(kept, pair, half),
+        slot_rows=(pair, width),
+        x=(2, 2, 2, rows, half),
+        other_half=(rows, half),
+        qkv=(8, block, gathered_width),
+        wo_all=(8, heads, block, mixed_width),
+        router=(experts, width),
+        projected=(rows, qkv_width),
+        mixed=(rows, mixed_width),
+        all_mixed=(heads, rows, mixed_width),
+        second_in=(rows, width),
+        core_in=(chunks, 2, 2, rows, 128),
+        y_in=(chunks, 2, rows, 128),
+        far=(chunks, heads - 1, 2, own, 128),
+        pair=(chunks, 2, own, 128),
+        x_in=(chunks, own, 128),
+        logit_grads=(experts, rows),
+        attended=(rows, width),
+        first_in=(rows, width),
+        projected_grad=(rows, qkv_width),
+        first_part=(heads, own, width),
+        dense=(8, block, dense_width),
+        dense_core=(4, block, dense_width),
+        xa=(2, block, cut),
+        ya=(block, cut),
+        yb=(2, block, dense_width - cut),
+        xb=(block, dense_width - cut),
+        first_far=(heads - 1, own, width),
+        rounded=(heads, own, width),
+    )
+    wide = dict(
+        gates=(kept, pair, 1),
+        counts=(8, 8, 128),
+        scale=(8, 128),
+        loss_scale=(8, 128),
+        valid=(rows, 8),
+        gain_one=(1, width),
+        gain=(1, width),
+        log_total=(rows, head_count),
+        residual=(rows, width),
+        probs=(8, experts, rows),
+        probs_own=(experts, rows),
+        own=(kept, pair, hidden_width),
+        final_grad=(own, width),
+        gate_rows=(2, kept, group_rows),
+        gate_in=(4, 2, kept, group_rows),
+        gate_sum=(2, kept, group_rows),
+        gate_all=(heads, 2, kept, rows),
+        logit_rows=(rows, width),
+        gain_part=(2, width),
+        gain_plane=(8, 2, width),
+        gain_heads=(heads, 2, width),
+    )
     scratch = {name: pltpu.VMEM(dims, LOW) for name, dims in low.items()}
     scratch.update({name: pltpu.VMEM(dims, WIDE) for name, dims in wide.items()})
-    whole = {"far_route": (8, group_rows), "slots": (2 * local_experts, group_rows)}
+    whole = dict(
+        far_route=small["near_route"].shape,
+        slots=(2 * local_experts, group_rows),
+    )
+    scratch.update({name: pltpu.VMEM(a.shape, a.dtype) for name, a in small.items()})
     scratch.update({name: pltpu.VMEM(dims, jnp.int32) for name, dims in whole.items()})
     copies = FRONT_COPIES + 2 * (heads - 1) + 2 * kept + chunks * (5 + GATHER_COPIES + 2 * (heads - 1)) + 2 * (heads - 1)
-    copies += kept + 2 + chunks * (3 + heads - 1) + 3 + 2 * heads - 1 + heads - 1
-    copies += SUM_COPIES + 3 * (heads - 1) + 7
+    copies += 2 * kept + kept + 2 * chunks * (2 + heads - 1) + chunks + 3 + 2 * heads - 1
+    copies += heads - 1 + SUM_COPIES + 5 * (heads - 1) + 7
     return named_call(
-        functools.partial(layer_kernel, heads, chunks, choices),
+        functools.partial(layer_kernel, heads, chunks, tuple(small)),
         ins,
         outs,
         scratch,
         copies,
-        5 * kept + 6,
+        5 * kept + 6 + len(small),
         1,
         59,
         280,
     )
 
 
-def finish_kernel(s, near, near_pre, far, far_pre, hidden, out_grad, *refs):
-    pieces, (up, down) = refs[:-2], refs[-2:]
+def finish_kernel(s, *refs):
+    sides, rest = (refs[:4], refs[4:8]), refs[8:]
+    result_in, tokens_in, dense, gains, loss_in = rest[:5]
+    up, down, result, tokens_grad, qkv_grad, out_grad, router_grad, gain_grads, loss = rest[5:]
     i = pl.program_id(0)
-    kept, half = pl.num_programs(0) // 2, down.shape[2]
-    j = i - s[1]
-    held = (j >= 0) & (j < kept)
-
-    @pl.when(held)
+    kept = pl.num_programs(0) // 2
+    for side, (rows, pre, hidden, grad) in enumerate(sides):
+        j = i - s[side]
+
+        @pl.when((j >= 0) & (j < kept))
+        def _(rows=rows, pre=pre, hidden=hidden, grad=grad):
+            up[0] = dot(rows[0], pre[0], (0, 0))
+            down[0] = dot(hidden[0], grad[0], (0, 0))
+
+    @pl.when(i == 0)
     def _():
-        up[0] = dot(near[0], near_pre[0], (0, 0))
-        columns = pl.ds(pl.multiple_of(s[0] * half, half), half)
-        down[0] = dot(hidden[0], out_grad[0, :, columns], (0, 0))
-
-    @pl.when(jnp.logical_not(held))
-    def _():
-        up[0] = dot(far[0], far_pre[0], (0, 0))
-
-    at = 0
-    for piece in pieces:
-        for k in range(piece.shape[0]):
-
-            @pl.when(i - s[2] == at + k)
-            def _(piece=piece, k=k):
-                down[0] = piece[k].astype(WIDE)
-
-        at += piece.shape[0]
-
-
-def finish(scalars, near, near_pre, far, far_pre, hidden, out_grad, arrived):
-    kept, _, half = near.shape
-    hidden_width = near_pre.shape[2]
+        result[...] = result_in[...].reshape(result.shape)
+        tokens_grad[...] = tokens_in[...].reshape(tokens_grad.shape)
+        head_count, block, size = qkv_grad.shape
+        for h in range(head_count):
+            qkv_grad[h] = dense[:, h * size : (h + 1) * size]
+        at = head_count * size
+        mixed_width = out_grad.shape[0]
+        out_grad[...] = jnp.transpose(dense[:, at : at + mixed_width])
+        last = jnp.transpose(dense[:, at + mixed_width : at + mixed_width + 128])
+        router_grad[...] = last[: router_grad.shape[0]]
+        gain_grads[...] = sum(
+            jnp.where(s[2] == b, gains[:, b * block : (b + 1) * block], 0.0) for b in range(8)
+        )
+        loss[...] = jnp.sum(jnp.sum(loss_in[...], 0), keepdims=True)
+
+
+def finish(scalars, near, far, small, shapes):
+    kept, _, half = near[0].shape
+    hidden_width = near[1].shape[2]
 
     def of(array, which):
         return pl.BlockSpec(
@@ -1448,31 +1556,30 @@
         )
 
     def all_of(array):
-        return pl.BlockSpec(array.shape, lambda i, s: (0, 0, 0))
-
-    ins = [(near, 1), (near_pre, 1), (far, 2), (far_pre, 2), (hidden, 1), (out_grad, 1)]
+        return pl.BlockSpec(array.shape, lambda i, s, n=len(array.shape): (0,) * n)
+
     return pl.pallas_call(
         finish_kernel,
         out_shape=[
             shape((2 * kept, half, hidden_width), WIDE),
             shape((2 * kept, hidden_width, half), WIDE),
+            *shapes,
         ],
         grid_spec=pltpu.PrefetchScalarGridSpec(
             num_scalar_prefetch=1,
             grid=(2 * kept,),
-            in_specs=[of(*a) for a in ins] + [all_of(piece) for piece in arrived],
+            in_specs=[of(array, 0) for array in near]
+            + [of(array, 1) for array in far]
+            + [all_of(array) for array in small],
             out_specs=[
                 pl.BlockSpec((1, half, hidden_width), lambda i, s: (i, 0, 0)),
                 pl.BlockSpec((1, hidden_width, half), lambda i, s: (i, 0, 0)),
+                *[all_of(array) for array in shapes],
             ],
         ),
         compiler_params=pltpu.CompilerParams(vmem_limit_bytes=60 * 2**20),
         cost_estimate=spends(8),
-    )(scalars, *[a[0] for a in ins], *arrived)
-
-
-def swap(values):
-    return lax.ppermute(values, FSDP, [(0, 1), (1, 0)])
+    )(scalars, *near, *far, *small)
 
 
 def fast(
@@ -1489,67 +1596,51 @@
     expert_down,
 ):
     heads = lax.axis_size(HEADS)
-    f, z = lax.axis_index(FSDP), lax.axis_index(HEADS)
+    f, t = lax.axis_index(FSDP), lax.axis_index(TENSOR)
     _, rows, width = tokens.shape
     block, head_count, qkv_dim = qkv_weight.shape
-    head_dim = qkv_dim // 3
+    mixed_width = out_weight.shape[0] * out_weight.shape[1]
     local_experts = expert_up.shape[0]
     kept = local_experts // 2
     expert_count = local_experts * heads
-    group_rows = 4 * rows
-    capacity = 2 * routes.shape[2] * group_rows // expert_count
-    mine, theirs = f * kept, (1 - f) * kept
-    half = width // 2
-    qkv_width = head_count * qkv_dim
-    pad = -(128 + qkv_width) % 256
-    wq = jnp.concatenate(
+    capacity = 2 * routes.shape[2] * 4 * rows // expert_count
+    small = dict(
+        router_in=router_weight.T,
+        gain_one_in=gain_one[None],
+        gain_two_in=gain_two[None],
+        qkv_in=jnp.swapaxes(qkv_weight, 0, 1),
+        out_in=out_weight.reshape(mixed_width, block),
+        near_route=jnp.swapaxes(routes, 1, 2),
+        tokens=tokens[0],
+        teacher=teacher[0],
+        valid_row=valid_mask,
+    )
+    made = layer(heads, expert_count, capacity, small, dict(up=expert_up, down=expert_down))
+    scalars = jnp.stack([f * kept, (1 - f) * kept, f * 4 + t]).astype(jnp.int32)
+    up_grad, down_grad, result, tokens_grad, qkv_grad, out_grad, router_grad, gains, loss = finish(
+        scalars,
+        [made.near_out, made.near_pre, made.near_hidden, made.near_grad],
+        [made.far_out, made.far_pre, made.far_hidden, made.far_grad],
+        [made.result, made.tokens_grad, made.dense_out, made.gain_out, made.loss],
         [
-            router_weight,
-            gain_one[:, None],
-            gain_two[:, None],
-            jnp.zeros((block, 128 - expert_count - 2), LOW),
-            qkv_weight.reshape(block, qkv_width),
-            jnp.zeros((block, pad), LOW),
+            shape((rows, width)),
+            shape((rows, width), WIDE),
+            shape((head_count, block, qkv_dim), WIDE),
+            shape((mixed_width, block), WIDE),
+            shape((expert_count, block), WIDE),
+            shape((2, block), WIDE),
+            shape((1, 1), WIDE),
         ],
-        1,
-    )
-    wo = out_weight.reshape(head_count * head_dim, block).T
-    near_route = jnp.pad(routes.reshape(group_rows, -1).T, ((0, 8 - routes.shape[2]), (0, 0)))
-    vmem = {
-        "shard": wq,
-        "wo_shard": wo,
-        "near_route": near_route,
-        "tokens": tokens[0],
-        "teacher": teacher[0],
-        "valid_row": valid_mask,
-    }
-    hbm = {"up": expert_up, "down": expert_down}
-    made = layer(heads, expert_count, capacity, routes.shape[2], head_count, vmem, hbm)
-    me = f * 4 + lax.axis_index(TENSOR)
-    result, tokens_grad, dense_out = made.result, made.tokens_grad, made.dense_out
-    loss_terms = jnp.sum(made.loss)[None]
-    own_gains = lax.dynamic_slice_in_dim(made.gain_out, me * block, block, 1)
-    scalars = jnp.stack([f, mine, theirs]).astype(jnp.int32)
-    up_grad, down_grad = finish(
-        scalars,
-        made.near_out,
-        made.near_pre,
-        made.far_out,
-        made.far_pre,
-        made.hidden_out,
-        made.grad_out,
-        [made.down_far],
-    )
-    out_width = head_count * head_dim
+    )
     return (
-        result.reshape(1, rows, width),
-        loss_terms,
-        tokens_grad.reshape(1, rows, width),
-        own_gains[0],
-        dense_out[:, :qkv_width].reshape(block, head_count, qkv_dim),
-        dense_out[:, qkv_width : qkv_width + out_width].T.reshape(head_count, head_dim, block),
-        own_gains[1],
-        dense_out[:, qkv_width + out_width :][:, :expert_count],
+        result[None],
+        loss.reshape(1),
+        tokens_grad[None],
+        gains[0],
+        jnp.swapaxes(qkv_grad, 0, 1),
+        out_grad.reshape(head_count, -1, block),
+        gains[1],
+        router_grad.T,
         up_grad,
         down_grad,
     )

time: 299 us -> 271 us (0.906)
  Pallas kernels: 284 us -> 268 us
  local copies, waits for them, and re-layouts: 12.7 us -> 1.26 us
    pallas_call x1, Pallas kernels: 270 us -> 253 us  [named_call(): pl.pallas_call(functools.partial(kernel, names), out_shape=[o[0] for o in...]
    unnamed x14 -> x0, local copies, waits for them, and re-layouts: 5.07 us -> none
where the time goes in v5:
time: 271 us
  Pallas kernels  268 us (99%)
    pallas_call x1, Pallas kernels, named_call(): pl.pallas_call(functools.partial(kernel, names), out_shape=[o[0] for o in...  253 us
    pallas_call x1, Pallas kernels, finish(): pl.pallas_call(finish_kernel, out_shape=[shape((2 * kept, half, hidden_wi...  15.6 us

profile of v5, /device:TPU:0, one launch (start us, length us, event | category | flops | bytes accessed | tf_op | source)
XLA Modules:
  0.0 270.8 jit_solution(13503565606591652188)
XLA Ops:
  0.6 0.6 pad_add_fusion.s
  1.3 252.6 %shard_map.186 = (bf16[4,64,768]{2,1,0:T(8,128)(2,1)}, f32[4,8,128]{2,1,0:T(8,128)}, f32[4,64,768]{2,1,0:T(8,128)}, f32[96,896]{1,0:T(8,128)}, f32[2,768]{1,0:T(...) custom-call(bf16[8,384,768]{2,1,0:T(8,128)(2,1)} %refs_0_.1, ...), custom_call_target="tpu_custom_call" | custom-call | bytes 840000000 | tf_op jit(solution)/shard_map/pallas_call | solution.py:1369
  253.9 15.6 %shard_map.187 = (f32[8,384,768]{2,1,0:T(8,128)}, f32[8,768,384]{2,1,0:T(8,128)}, bf16[256,768]{1,0:T(8,128)(2,1)}, f32[256,768]{1,0:T(8,128)}, f32[3,96,192]{2,...) custom-call(s32[3]{0:T(128)} %pad_add_fusion.s, ...), custom_call_target="tpu_custom_call" | custom-call | bytes 24000000 | tf_op jit(solution)/shard_map/pallas_call | solution.py:1561
  269.5 1.3 slice_bitcast_fusion

commit v6 on v5

--- a/solution.py
+++ b/solution.py
@@ -668,9 +668,6 @@
     ]
 
     def to_heads(k):
-        if k == chunks - 1:
-            r.hidden_copies.append(send_hidden(place, links, r, 1))
-
         def keep(rows, part_of, values):
             image_sum[k, rows, pl.ds(part_of * half, half)] = values.astype(LOW)
 
@@ -1074,8 +1071,7 @@
             into = slice(g * capacity, (g + 1) * capacity)
             r.far_held[i, into] = (dot(hot, rows_in) * gate).astype(LOW)
     stores.append(loads.start(r.far_held, r.far_grad))
-    for i in range(2, kept):
-        r.hidden_copies.append(send_hidden(place, links, r, i))
+    r.hidden_copies.append(send_hidden(place, links, r, 1))
     sums = RowSum(links, place, r)
     sums.spread = spread
     steps = {0: sums.to_y, 1: sums.to_heads, kept - 1: sums.total}
@@ -1230,6 +1226,8 @@
             if step == k + 2:
                 sums.total(1, k)
                 sums.to_x(k)
+    for i in range(2, r.hidden.shape[0]):
+        r.hidden_copies.append(send_hidden(place, links, r, i))
     normed, spread_two = normalize(residual[mine, :])
     cross = sums.cross
     near = jnp.concatenate([pair[k, f].astype(WIDE) for k in range(chunks)], 1)

time: 271 us -> 270 us (level)
  no operation moved by 1% of the time
where the time goes in v6:
time: 270 us; the launch traced here: 269 us
  Pallas kernels  266 us (99%)
    pallas_call x1, Pallas kernels, named_call(): pl.pallas_call(functools.partial(kernel, names), out_shape=[o[0] for o in...  251 us
    pallas_call x1, Pallas kernels, finish(): pl.pallas_call(finish_kernel, out_shape=[shape((2 * kept, half, hidden_wi...  15.6 us

profile of v6, /device:TPU:0, one launch (start us, length us, event | category | flops | bytes accessed | tf_op | source)
XLA Modules:
  0.0 268.8 jit_solution(15850492387293545937)
XLA Ops:
  0.6 0.6 pad_add_fusion.s
  1.3 250.7 %shard_map.186 = (bf16[4,64,768]{2,1,0:T(8,128)(2,1)}, f32[4,8,128]{2,1,0:T(8,128)}, f32[4,64,768]{2,1,0:T(8,128)}, f32[96,896]{1,0:T(8,128)}, f32[2,768]{1,0:T(...) custom-call(bf16[8,384,768]{2,1,0:T(8,128)(2,1)} %refs_0_.1, ...), custom_call_target="tpu_custom_call" | custom-call | bytes 840000000 | tf_op jit(solution)/shard_map/pallas_call | solution.py:1367
  252.0 15.6 %shard_map.187 = (f32[8,384,768]{2,1,0:T(8,128)}, f32[8,768,384]{2,1,0:T(8,128)}, bf16[256,768]{1,0:T(8,128)(2,1)}, f32[256,768]{1,0:T(8,128)}, f32[3,96,192]{2,...) custom-call(s32[3]{0:T(128)} %pad_add_fusion.s, ...), custom_call_target="tpu_custom_call" | custom-call | bytes 24000000 | tf_op jit(solution)/shard_map/pallas_call | solution.py:1559
  267.6 1.3 slice_bitcast_fusion

commit v7 on v6

--- a/solution.py
+++ b/solution.py
@@ -793,10 +793,10 @@
     small = [links.send(counts.at[me], counts.at[me], d) for d in place.plane_peers]
     small.append(links.send(r.near_route, r.far_route, place.x_peer))
     main.forward()
+    down = [bulk(0)]
     for copy in along:
         copy.wait_recv()
     side.start()
-    down = [bulk(0)]
     main.share()
     main.finish()
     width = r.tokens.shape[1]

time: 270 us -> 268 us (level)
  no operation moved by 1% of the time
where the time goes in v7:
time: 268 us
  Pallas kernels  265 us (99%)
    pallas_call x1, Pallas kernels, named_call(): pl.pallas_call(functools.partial(kernel, names), out_shape=[o[0] for o in...  250 us
    pallas_call x1, Pallas kernels, finish(): pl.pallas_call(finish_kernel, out_shape=[shape((2 * kept, half, hidden_wi...  15.6 us

profile of v7, /device:TPU:0, one launch (start us, length us, event | category | flops | bytes accessed | tf_op | source)
XLA Modules:
  0.0 267.9 jit_solution(2674416042172363541)
XLA Ops:
  0.6 0.6 pad_add_fusion.s
  1.3 249.7 %shard_map.186 = (bf16[4,64,768]{2,1,0:T(8,128)(2,1)}, f32[4,8,128]{2,1,0:T(8,128)}, f32[4,64,768]{2,1,0:T(8,128)}, f32[96,896]{1,0:T(8,128)}, f32[2,768]{1,0:T(...) custom-call(bf16[8,384,768]{2,1,0:T(8,128)(2,1)} %refs_0_.1, ...), custom_call_target="tpu_custom_call" | custom-call | bytes 840000000 | tf_op jit(solution)/shard_map/pallas_call | solution.py:1367
  251.0 15.6 %shard_map.187 = (f32[8,384,768]{2,1,0:T(8,128)}, f32[8,768,384]{2,1,0:T(8,128)}, bf16[256,768]{1,0:T(8,128)(2,1)}, f32[256,768]{1,0:T(8,128)}, f32[3,96,192]{2,...) custom-call(s32[3]{0:T(128)} %pad_add_fusion.s, ...), custom_call_target="tpu_custom_call" | custom-call | bytes 24000000 | tf_op jit(solution)/shard_map/pallas_call | solution.py:1559
  266.6 1.3 slice_bitcast_fusion
